TPU v7x, 128 devices: a whole 4x4x4 slice. The times are simulated.
128 devices in a mesh: band: 32 (over x, z_lo, y), pw: 4 (over z_hi, core).
Axes of the slice: x: 4, y: 4, z: 4 (z_hi: 2, z_lo: 2; z = z_hi * 2 + z_lo), core: 2. Of those that a mesh axis runs over, the one named last changes fastest.
Arguments:
- cond_pairs: bfloat16 [256, 256, 5120], P('band', None, 'pw'), may hold values from -6 to 6
- vectors: bfloat16 [8, 24, 256], P(None, None, 'band'), may hold values from -0.375 to 0.375
- screened: bfloat16 [5120, 5120], P('pw', 'band'), may hold values from -0.078125 to 0.078125
- val_pairs: bfloat16 [256, 24, 5120], P('band', None, 'pw'), may hold values from -0.015625 to 0.015625
Outputs:
- sigma: float32 [8, 256, 256], P(None, 'pw', 'band')
All inputs are finite; a program needn't handle non-finite values.
Results may differ from a plain program's by a relative error of at most 0.004.
Values may be sent and summed in bfloat16 or wider, within the bound.
No kernel may reach another device: no remote copies, remote signals or barrier semaphores. Data moves between devices by JAX's collectives and lax.ppermute only.
A program may use at most 192 MiB of HBM per device.

v0:
```python
import jax
import jax.numpy as jnp
from jax import lax
from jax.sharding import PartitionSpec as P


def make_adder(block, piece):
    return jnp.einsum("kcg,hg->kch", block, piece, preferred_element_type=jnp.float32)


def shards(cond_pairs, vectors, screened, val_pairs):
    whole_x = lax.all_gather(vectors, "band", axis=2, tiled=True)
    nvec, vblock, ncond = whole_x.shape
    rows = whole_x.reshape(nvec * vblock, ncond)
    mixed = jnp.einsum("kd,cdg->kcg", rows, cond_pairs, preferred_element_type=jnp.float32).astype(
        jnp.bfloat16
    )
    full_b = lax.all_gather(mixed, "pw", axis=2, tiled=True)
    count = full_b.shape[0]
    local_c = full_b.shape[1]
    slab = screened.shape[0]
    half = count // 2
    right_part = make_adder(full_b[:half], lax.all_gather(screened, "band", axis=1, tiled=True))
    left_part = make_adder(full_b[half:], lax.all_gather(screened, "band", axis=1, tiled=True))
    applied = jnp.concatenate([right_part, left_part], axis=0)
    applied = applied.astype(jnp.bfloat16).reshape(nvec, vblock, local_c, slab)
    partial_sigma = jnp.einsum(
        "uwg,kwcg->kuc",
        lax.all_gather(val_pairs, "band", axis=0, tiled=True),
        applied,
        preferred_element_type=jnp.float32,
    )
    return lax.psum_scatter(partial_sigma, "pw", scatter_dimension=1, tiled=True)


def solution(mesh):
    return jax.shard_map(
        shards,
        mesh=mesh,
        in_specs=(
            P("band", None, "pw"),
            P(None, None, "band"),
            P("pw", "band"),
            P("band", None, "pw"),
        ),
        out_specs=P(None, "pw", "band"),
        check_vma=False,
    )
```

profile of v0, /device:TPU:1, one launch (start us, length us, event | category | flops | bytes accessed | tf_op | source)
XLA Modules:
  0.0 610.8 jit_solution(9499502527356614570)
XLA Ops:
  6.5 0.0 copy-start.1
  6.5 0.0 all-gather.4.cloned.1.call-start
  6.5 72.0 %all_gather.13 = bf16[8,24,256]{1,2,0:T(8,128)(2,1)S(1)} all-gather(bf16[8,24,8]{1,2,0:T(8,128)(2,1)} %param.5), channel_id=1, replica_groups=mesh['band'=32,'pw'=4] {'band'}, dimensions={2}, use_global_device_ids=true | all-gather | bytes 101376 | tf_op jit(solution)/shard_map/all_gather | solution.py:12
  78.6 0.2 copy.9
  78.8 5.7 convolution_convert_fusion
  84.4 0.0 all-gather.4.cloned.1.call-update
  84.5 0.0 all-gather.6.cloned.1.call-start
  84.5 0.7 all-gather.6.cloned.1.call-update
  85.2 0.0 all-gather.8.cloned.1.call-start
  85.3 0.0 copy-done.1
  85.3 0.9 copy.12
  86.1 0.0 all-gather.8.cloned.1.call-update
  86.2 0.0 reduce-scatter.4.cloned.1.call-start
  86.2 113.6 %all-gather.4.cloned.1.call-done = bf16[192,8,5120]{2,0,1:T(8,128)(2,1)} async-done(((bf16[192,8,1280]{2,0,1:T(8,128)(2,1)}), bf16[192,8,5120]{2,0,1:T(8,128)(2,1)}) %all-gather.4.cloned.1.call-update) | async-done | bytes 15728656 | tf_op jit(solution)/shard_map/all_gather | solution.py:18
  199.8 10.9 %fusion.21 = (bf16[96,8,5120]{2,0,1:T(8,128)(2,1)}, bf16[96,8,5120]{2,0,1:T(8,128)(2,1)}) fusion(bf16[192,8,5120]{2,0,1:T(8,128)(2,1)} %all-gather.4.cloned.1.call-done), kind=kLoop, calls=%fused_computation.13 | loop fusion | bytes 31457280 | tf_op jit(solution)/shard_map/slice | solution.py:23
  210.7 152.4 %all-gather.6.cloned.1.call-done = bf16[1280,5120]{0,1:T(8,128)(2,1)} async-done(((bf16[1280,160]{0,1:T(8,128)(2,1)}), bf16[1280,5120]{0,1:T(8,128)(2,1)}) %all-gather.6.cloned.1.call-update) | async-done | bytes 13107216 | tf_op jit(solution)/shard_map/all_gather | solution.py:23
  363.1 0.0 copy-start
  363.1 18.9 %fusion.13 = bf16[96,8,1280]{2,1,0:T(8,128)(2,1)S(1)} fusion(bf16[1280,5120]{0,1:T(8,128)(2,1)} %all-gather.6.cloned.1.call-done, bf16[96,8,5120]{2,0,1:T(8,128)(2,1)} %get-tuple-element.6), kind=kOutput, calls=%fused_computation.11 | convolution fusion | flops 10067312640 | bytes 22937600 | tf_op jit(solution)/shard_map/kcg,hg->kch/dot_general | solution.py:8
  382.0 0.0 copy-done
  382.0 16.0 %fusion.8 = bf16[96,8,1280]{2,1,0:T(8,128)(2,1)S(1)} fusion(bf16[1280,5120]{0,1:T(8,128)(2,1)} %all-gather.6.cloned.1.call-done, bf16[96,8,5120]{2,0,1:T(8,128)(2,1)S(1)} %copy-done), kind=kOutput, calls=%fused_computation.10 | convolution fusion | flops 10067312640 | bytes 22937600 | tf_op jit(solution)/shard_map/kcg,hg->kch/dot_general | solution.py:8
  398.0 2.2 pad_maximum_fusion
  400.3 151.4 %all-gather.8.cloned.1.call-done = bf16[256,24,1280]{2,0,1:T(8,128)(2,1)} async-done(((bf16[8,24,1280]{2,0,1:T(8,128)(2,1)}), bf16[256,24,1280]{2,0,1:T(8,128)(2,1)}) %all-gather.8.cloned.1.call-update) | async-done | bytes 15728656 | tf_op jit(solution)/shard_map/all_gather | solution.py:29
  551.7 11.5 %fusion.18 = f32[8,256,8]{1,2,0:T(8,128)S(1)} fusion(bf16[8,24,8,1280]{3,2,1,0:T(8,128)(2,1)} %bitcast.29, bf16[256,24,1280]{2,0,1:T(8,128)(2,1)} %all-gather.8.cloned.1.call-done), kind=kOutput, calls=%fused_computation.12 | convolution fusion | flops 1006632960 | bytes 19726336 | tf_op jit(solution)/shard_map/uwg,kwcg->kuc/dot_general | solution.py:27
  563.1 0.4 copy.14
  563.6 1.0 reshape.11
  564.5 0.0 reduce-scatter.4.cloned.1.call-update
  564.5 38.1 %reduce-scatter.4.cloned.1.call-done = f32[64,64]{1,0:T(8,128)} async-done(((f32[256,64]{1,0:T(8,128)}), f32[64,64]{1,0:T(8,128)}) %reduce-scatter.4.cloned.1.call-update) | async-done | bytes 16400
  602.6 0.9 reshape.12
  603.5 0.8 copy.15
Async XLA Ops:
  6.5 78.7 %copy-start.1 = (bf16[8,24,1280]{2,1,0:T(8,128)(2,1)S(1)}, bf16[8,24,1280]{2,1,0:T(8,128)(2,1)}, u32[]{:S(2)}) copy-start(bf16[8,24,1280]{2,1,0:T(8,128)(2,1)} %param.7) | copy-start | bytes 1474564
  6.5 193.2 %all-gather.4.cloned.1.call-start = ((), (), s32[]{:S(2)}) async-start(), calls=%async_computation.1 | async-start | bytes 19660800 | tf_op jit(solution)/shard_map/all_gather | solution.py:18
  84.5 278.6 %all-gather.6.cloned.1.call-start = ((), (), s32[]{:S(2)}) async-start(), calls=%async_computation.2 | async-start | bytes 13516800 | tf_op jit(solution)/shard_map/all_gather | solution.py:23
  85.2 466.4 %all-gather.8.cloned.1.call-start = ((), (), s32[]{:S(2)}) async-start(), calls=%async_computation.3 | async-start | bytes 16220160 | tf_op jit(solution)/shard_map/all_gather | solution.py:29
  86.2 516.4 %reduce-scatter.4.cloned.1.call-start = ((), (), s32[]{:S(2)}) async-start(), calls=%async_computation.4 | async-start | bytes 163840
  363.1 19.0 %copy-start = (bf16[96,8,5120]{2,0,1:T(8,128)(2,1)S(1)}, bf16[96,8,5120]{2,0,1:T(8,128)(2,1)}, u32[]{:S(2)}) copy-start(bf16[96,8,5120]{2,0,1:T(8,128)(2,1)} %get-tuple-element.5) | copy-start | bytes 23592964
Sparse Core Ops, SparseCore 0:
  84.6 115.1 all-gather.3
  201.4 161.5 all-gather.5
  364.7 186.8 all-gather.7
  564.7 37.8 reduce-scatter.3
where the time goes:
time: 611 us
  waiting for transfers between devices  456 us (75%)
  blocking collectives  72 us (12%)
  matrix products  52.1 us (9%)
  local copies, waits for them, and re-layouts  15 us (2%)
  between operations  13.2 us (2%)
    all_gather x1, waiting for transfers between devices, shards(): lax.all_gather(screened, 'band', axis=1, tiled=True)  152 us
    all_gather x1, waiting for transfers between devices, shards(): lax.all_gather(val_pairs, 'band', axis=0, tiled=True)  151 us
    all_gather x1, waiting for transfers between devices, shards(): full_b = lax.all_gather(mixed, 'pw', axis=2, tiled=True)  114 us
    all_gather x1, blocking collectives, shards(): whole_x = lax.all_gather(vectors, 'band', axis=2, tiled=True)  72 us
    unnamed x5, waiting for transfers between devices  38.8 us
    dot_general x2, matrix products, make_adder(): jnp.einsum('kcg,hg->kch', block, piece, preferred_element_type=jnp.float32)  35 us
  transfers between devices with their start and end apart: 4, of which 4 were waited for; matrix products, arithmetic and copies ran while one was open for 8% of the time, Pallas kernels for 0%

commit v1 on v0

v1 whole, which is shorter than its diff:
```python
import jax
import jax.numpy as jnp
from jax import lax
from jax.experimental import pallas as pl
from jax.experimental.pallas import tpu as pltpu
from jax.sharding import Mesh, PartitionSpec as P

F32, BF16 = jnp.float32, jnp.bfloat16
ANY = pl.BlockSpec(memory_space=pl.ANY)
SMEM = pl.BlockSpec(memory_space=pltpu.SMEM)
VMEM = pl.BlockSpec(memory_space=pltpu.VMEM)
VMEM_LIMIT = 56 * 1024 * 1024

NX, NY = 4, 4
NT = (((1,), (1,)), ((), ()))


def shift_from(a, axis, s):
    return lax.ppermute(a, axis, [(i, (i - s) % 4) for i in range(4)])


def shift_to(a, axis, s):
    return lax.ppermute(a, axis, [(i, (i + s) % 4) for i in range(4)])


def swap(a, axis):
    return lax.ppermute(a, axis, [(0, 1), (1, 0)])


def gather_zl_y(first, second):
    pair = jnp.stack([first, swap(first, "zl")])
    line = jnp.stack([second] + [shift_from(second, "y", s) for s in (1, 2, 3)])
    pairs = [pair] + [shift_from(pair, "y", s) for s in (1, 2, 3)]
    return pairs, [line, swap(line, "zl")]


def mixed_kernel(where, x_ref, b_ref, *refs):
    outs, xs, rows = refs[:4], refs[4], refs[5]

    @pl.when(pl.program_id(0) == 0)
    def _():
        x, zl, y = where[0], where[1], where[2]
        for at in range(32):
            z_of, x_of, y_of = at // 16, (at // 4) % 4, at % 4
            to = ((x + x_of) % 4) * 8 + (zl + z_of) % 2 * 4 + (y + y_of) % 4
            rows[pl.ds(pl.multiple_of(to * 8, 8), 8), :] = x_ref[at * 8 : at * 8 + 8, :]
        turned = rows[:, :].T
        rows2 = refs[6]
        rows2[...] = turned
        for j in range(4):
            q = (x + j) % 4
            xs[j * 48 : j * 48 + 48, :] = rows2[pl.ds(pl.multiple_of(q * 48, 48), 48), :].astype(BF16)

    lhs = xs[...]
    for pair in range(4):
        two = [jnp.dot(lhs, b_ref[2 * pair + i], preferred_element_type=F32) for i in range(2)]
        for j in range(4):
            for w in range(6):
                at = (j * 6 + w) * 8
                both = jnp.concatenate([t[at : at + 8] for t in two], axis=0)
                outs[j][w, 16 * pair : 16 * pair + 16, :] = both.astype(BF16)


def mix(where, x_all, cond):
    g = cond.shape[2]
    step = 256
    return pl.pallas_call(
        mixed_kernel,
        grid=(g // step,),
        in_specs=[
            SMEM,
            pl.BlockSpec((256, 192), lambda i: (0, 0)),
            pl.BlockSpec((8, 256, step), lambda i: (0, 0, i)),
        ],
        out_specs=[pl.BlockSpec((6, 64, step), lambda i: (0, 0, i))] * 4,
        out_shape=[jax.ShapeDtypeStruct((6, 64, g), BF16)] * 4,
        scratch_shapes=[pltpu.VMEM((192, 256), BF16), pltpu.VMEM((256, 192), F32), pltpu.VMEM((192, 256), F32)],
        compiler_params=pltpu.CompilerParams(vmem_limit_bytes=VMEM_LIMIT),
        cost_estimate=pl.CostEstimate(flops=2 * 192 * 256 * 8 * g, bytes_accessed=9200000, transcendentals=0),
        name="mix",
    )(where, x_all, cond)


def z_kernel(where, *refs):
    m, wa, wb = refs[0:4], refs[4:8], refs[8:10]
    send, keep, ms, ws, m_sem, w_sem = refs[10:]
    zl, y, zh, core = where[1], where[2], where[3], where[4]
    copies = []
    for t in range(4):
        owner = 1 - core if t < 2 else core
        q = 2 * owner + (zh + t % 2) % 2
        for r in range(4):
            copies.append(
                pltpu.make_async_copy(
                    m[r].at[pl.ds(pl.multiple_of(q * 48, 48), 48)], ms.at[t, pl.ds(48 * r, 48)], m_sem.at[t * 4 + r]
                )
            )
    for z_of in range(2):
        for y_of in range(4):
            to = ((zl + z_of) % 2 * 4 + (y + y_of) % 4) * 160
            at = z_of * 4 + y_of
            copies.append(
                pltpu.make_async_copy(
                    wa[y_of].at[z_of], ws.at[pl.ds(pl.multiple_of(to, 160), 80)], w_sem.at[at]
                )
            )
            copies.append(
                pltpu.make_async_copy(
                    wb[z_of].at[y_of], ws.at[pl.ds(pl.multiple_of(to + 80, 80), 80)], w_sem.at[8 + at]
                )
            )
    for c in copies:
        c.start()
    for c in copies:
        c.wait()

    for half, out in enumerate((send, keep)):

        @pl.loop(0, 2)
        def _(a, half=half, out=out):
            lhs = ms[2 * half + a]
            for n in range(5):
                cols = slice(256 * n, 256 * n + 256)
                res = lax.dot_general(lhs, ws[cols, :], NT, preferred_element_type=F32)
                for w in range(6):
                    for r in range(4):
                        at = (r * 6 + w) * 8
                        out[a, (w * 4 + r) * 8 : (w * 4 + r) * 8 + 8, cols] = res[at : at + 8]


def make_z(where, m, wa, wb):
    g = m[0].shape[1]
    shape = jax.ShapeDtypeStruct((2, 192, g), F32)
    return pl.pallas_call(
        z_kernel,
        in_specs=[SMEM] + [ANY] * 10,
        out_specs=[VMEM, VMEM],
        out_shape=[shape, shape],
        scratch_shapes=[
            pltpu.VMEM((4, 192, g), BF16),
            pltpu.VMEM((g, g), BF16),
            pltpu.SemaphoreType.DMA((16,)),
            pltpu.SemaphoreType.DMA((16,)),
        ],
        compiler_params=pltpu.CompilerParams(vmem_limit_bytes=VMEM_LIMIT),
        cost_estimate=pl.CostEstimate(flops=2 * 768 * g * g, bytes_accessed=9000000, transcendentals=0),
        name="make_z",
    )(where, *m, *wa, *wb)


def last_kernel(where, *refs):
    za, zb, mx = refs[0:4], refs[4:6], refs[6:10]
    out, zs, xs, total, sem = refs[10:]
    zl, y = where[1], where[2]
    copies = []
    for z_of in range(2):
        for y_of in range(4):
            at = z_of * 4 + y_of
            copies.append(pltpu.make_async_copy(za[y_of].at[z_of], zs.at[pl.ds(0, 3), at], sem.at[at]))
            copies.append(pltpu.make_async_copy(zb[z_of].at[y_of], zs.at[pl.ds(3, 3), at], sem.at[8 + at]))
    for j in range(4):
        copies.append(pltpu.make_async_copy(mx[j], xs.at[:, j], sem.at[16 + j]))
    for c in copies:
        c.start()
    for c in copies:
        c.wait()
    sums = jnp.zeros((256, 256), F32)
    for w in range(6):
        lhs = zs[w].reshape(256, zs.shape[3])
        rhs = xs[w].reshape(256, xs.shape[3])
        sums = sums + lax.dot_general(lhs, rhs, NT, preferred_element_type=F32)
    for z_of in range(2):
        for y_of in range(4):
            to = ((zl + z_of) % 2 * 4 + (y + y_of) % 4) * 8
            for r in range(4):
                at = ((z_of * 4 + y_of) * 4 + r) * 8
                total[pl.ds(pl.multiple_of(r * 64 + to, 8), 8), :] = sums[at : at + 8]
    turned = total[...].T
    for j in range(4):
        out[j] = turned[64 * j : 64 * j + 64]


def last(where, za, zb, mixed):
    g = mixed[0].shape[2]
    return pl.pallas_call(
        last_kernel,
        in_specs=[SMEM] + [ANY] * 10,
        out_specs=VMEM,
        out_shape=jax.ShapeDtypeStruct((4, 64, 256), F32),
        scratch_shapes=[
            pltpu.VMEM((6, 8, 32, g), BF16),
            pltpu.VMEM((6, 4, 64, g), BF16),
            pltpu.VMEM((256, 256), F32),
            pltpu.SemaphoreType.DMA((20,)),
        ],
        compiler_params=pltpu.CompilerParams(vmem_limit_bytes=VMEM_LIMIT),
        cost_estimate=pl.CostEstimate(flops=2 * 256 * 256 * 6 * g, bytes_accessed=8000000, transcendentals=0),
        name="last",
    )(where, *za, *zb, *mixed)


def shards(cond_pairs, vectors, screened, val_pairs):
    g = cond_pairs.shape[2]
    axes = ("x", "zl", "y", "zh", "core")
    where = jnp.stack([lax.axis_index(a) for a in axes]).astype(jnp.int32)

    own = jnp.transpose(vectors, (2, 1, 0)).reshape(8, 192).astype(F32)
    by_y = jnp.concatenate([own] + [shift_from(own, "y", s) for s in (1, 2, 3)])
    by_x = jnp.concatenate([by_y] + [shift_from(by_y, "x", s) for s in (1, 2, 3)])
    x_all = jnp.concatenate([by_x, swap(by_x, "zl")])

    w_t = screened.T
    wa, wb = gather_zl_y(w_t[:80], w_t[80:])
    m_own = jnp.transpose(val_pairs, (1, 0, 2)).reshape(192, g)
    m = [m_own] + [shift_from(m_own, "x", s) for s in (1, 2, 3)]

    mixed = mix(where, x_all, cond_pairs)
    mixed = [mixed[0]] + [shift_to(mixed[j], "x", j) for j in (1, 2, 3)]

    send, keep = make_z(where, m, wa, wb)
    part = (keep + swap(send, "core")).astype(BF16)
    got = []
    for a in range(2):
        perm = [
            (x * 4 + zh * 2 + c, (2 * c + (zh ^ a)) * 4 + x) for x in range(4) for zh in range(2) for c in range(2)
        ]
        got.append(lax.ppermute(part[a], ("x", "zh", "core"), perm))
    z = (got[0].astype(F32) + got[1].astype(F32)).astype(BF16).reshape(2, 3, 32, g)
    za, zb = gather_zl_y(z[0], z[1])

    sums = last(where, za, zb, mixed)
    over_x = sums[0]
    for j in (1, 2, 3):
        over_x = over_x + shift_from(sums[j], "x", j)
    total = over_x[:, :64]
    for r in (1, 2, 3):
        total = total + shift_to(over_x[:, 64 * r : 64 * r + 64], ("zh", "core"), r)
    return jnp.transpose(total.reshape(8, 8, 64), (1, 2, 0))


def solution(mesh):
    fine = Mesh(mesh.devices.reshape(4, 2, 4, 2, 2), ("x", "zl", "y", "zh", "core"))
    band, pw = ("x", "zl", "y"), ("zh", "core")
    return jax.shard_map(
        shards,
        mesh=fine,
        in_specs=(P(band, None, pw), P(None, None, band), P(pw, band), P(band, None, pw)),
        out_specs=P(None, pw, band),
        check_vma=False,
    )
```

time: 611 us -> 197 us (0.32)
  waiting for transfers between devices: 456 us -> 94.6 us
  blocking collectives: 72 us -> 0 us
  starting transfers between devices: 0.12 us -> 67.2 us
  matrix products: 52.1 us -> 0 us
  Pallas kernels: 0 us -> 23.2 us
  between operations: 13.2 us -> 0.41 us
  local copies, waits for them, and re-layouts: 15 us -> 7.54 us
    all_gather x3 -> x0, waiting for transfers between devices: 417 us -> none  [the longest x1 152 us: shards(): lax.all_gather(screened, 'band', axis=1, tiled=True)]
    ppermute x0 -> x38, waiting for transfers between devices: none -> 94.6 us  [the longest x24 40.7 us: shift_from(): return lax.ppermute(a, axis, [(i, (i - s) % 4) for i in range(4)])]
    all_gather x1 -> x0, blocking collectives: 72 us -> none  [shards(): whole_x = lax.all_gather(vectors, 'band', axis=2, tiled=True)]
    ppermute x0 -> x38, starting transfers between devices: none -> 67.2 us  [the longest x24 28.1 us: shift_from(): return lax.ppermute(a, axis, [(i, (i - s) % 4) for i in range(4)])]
    dot_general x4 -> x0, matrix products: 52.1 us -> none  [the longest x2 35 us: make_adder(): jnp.einsum('kcg,hg->kch', block, piece, preferred_element_type=jnp.float32)]
    unnamed x5 -> x0, waiting for transfers between devices: 38.8 us -> none
    pallas_call x0 -> x3, Pallas kernels: none -> 23.2 us  [the longest x1 9.68 us: make_z(): pl.pallas_call(z_kernel, in_specs=[SMEM] + [ANY] * 10, out_specs=[VMEM, V...]
    slice x1 -> x2, local copies, waits for them, and re-layouts: 10.9 us -> 0.11 us  [the longest x1 0.08 us: shards(): total = total + shift_to(over_x[:, 64 * r:64 * r + 64], ('zh', 'core'), r)]
  transfers between devices with their start and end apart: 4 -> 38, of which waited for: 4 -> 14; matrix products, arithmetic and copies ran while one was open for 8% -> 2% of each run, Pallas kernels for 0% -> 4%
where the time goes in v1:
time: 197 us; the launch traced here: 196 us
  waiting for transfers between devices  94.6 us (48%)
  starting transfers between devices  67.2 us (34%)
  Pallas kernels  23.2 us (12%)
  local copies, waits for them, and re-layouts  7.54 us (4%)
  other arithmetic  3.02 us (2%)
    ppermute x24, waiting for transfers between devices, shift_from(): return lax.ppermute(a, axis, [(i, (i - s) % 4) for i in range(4)])  40.7 us
    ppermute x6, waiting for transfers between devices, swap(): return lax.ppermute(a, axis, [(0, 1), (1, 0)])  40.7 us
    ppermute x24, starting transfers between devices, shift_from(): return lax.ppermute(a, axis, [(i, (i - s) % 4) for i in range(4)])  28.1 us
    ppermute x6, starting transfers between devices, swap(): return lax.ppermute(a, axis, [(0, 1), (1, 0)])  16.5 us
    ppermute x6, waiting for transfers between devices, shift_to(): return lax.ppermute(a, axis, [(i, (i + s) % 4) for i in range(4)])  13.1 us
    ppermute x2, starting transfers between devices, shards(): got.append(lax.ppermute(part[a], ('x', 'zh', 'core'), perm))  11.7 us
    ppermute x6, starting transfers between devices, shift_to(): return lax.ppermute(a, axis, [(i, (i + s) % 4) for i in range(4)])  11 us
    pallas_call x1, Pallas kernels, make_z(): pl.pallas_call(z_kernel, in_specs=[SMEM] + [ANY] * 10, out_specs=[VMEM, V...  9.68 us
  transfers between devices with their start and end apart: 38, of which 14 were waited for; matrix products, arithmetic and copies ran while one was open for 2% of the time, Pallas kernels for 4%

profile of v1, /device:TPU:1, one launch (start us, length us, event | category | flops | bytes accessed | tf_op | source)
XLA Modules:
  0.0 195.9 jit_solution(1209495658968342011)
XLA Ops:
  0.0 1.1 slice_bitcast_fusion.6
  1.1 2.2 %collective-permute-start.9 = (bf16[80,1280]{1,0:T(8,128)(2,1)S(1)}, bf16[80,1280]{1,0:T(8,128)(2,1)S(1)}, u32[]{:S(2)}, u32[]{:S(2)}) collective-permute-start(bf16[80,1280]{1,0:T(8,128)(2,1)S(1)} %get-tuple-element.23), channel_id=1, source_target_pairs={{0,4},{4,8},{8,12},{12,0},{1,5},{5,9},{9,13},{13,1},{2,6},{6,10},{... | collective-permute-start | bytes 614408 | tf_op jit(solution)/shard_map/ppermute | solution.py:19
  3.3 2.6 %collective-permute-start.8 = (bf16[80,1280]{1,0:T(8,128)(2,1)S(1)}, bf16[80,1280]{1,0:T(8,128)(2,1)S(1)}, u32[]{:S(2)}, u32[]{:S(2)}) collective-permute-start(bf16[80,1280]{1,0:T(8,128)(2,1)S(1)} %get-tuple-element.23), channel_id=1, source_target_pairs={{0,8},{4,12},{8,0},{12,4},{1,9},{5,13},{9,1},{13,5},{2,10},{6,14},... | collective-permute-start | bytes 614408 | tf_op jit(solution)/shard_map/ppermute | solution.py:19
  5.9 1.1 collective-permute-start.7
  7.0 1.1 copy.13
  8.1 2.5 %collective-permute-start = (bf16[192,1280]{1,0:T(8,128)(2,1)S(1)}, bf16[192,1280]{1,0:T(8,128)(2,1)S(1)}, u32[]{:S(2)}, u32[]{:S(2)}) collective-permute-start(bf16[192,1280]{1,0:T(8,128)(2,1)S(1)} %bitcast.58), channel_id=1, source_target_pairs={{0,96},{32,0},{64,32},{96,64},{1,97},{33,1},{65,33},{97,65},{2,98}... | collective-permute-start | bytes 1474568 | tf_op jit(solution)/shard_map/ppermute | solution.py:19
  11.2 1.6 collective-permute-start.3
  12.8 2.0 %collective-permute-done.8 = bf16[80,1280]{1,0:T(8,128)(2,1)S(1)} collective-permute-done((bf16[80,1280]{1,0:T(8,128)(2,1)S(1)}, bf16[80,1280]{1,0:T(8,128)(2,1)S(1)}, u32[]{:S(2)}, u32[]{:S(2)}) %collective-permute-start.8) | collective-permute-done | bytes 204832 | tf_op jit(solution)/shard_map/ppermute | solution.py:19
  14.9 1.7 collective-permute-start.10
  16.6 1.2 collective-permute-start.2
  17.9 2.9 %collective-permute-start.4 = (bf16[2,80,1280]{2,1,0:T(8,128)(2,1)S(1)}, bf16[2,80,1280]{2,1,0:T(8,128)(2,1)}, u32[]{:S(2)}, u32[]{:S(2)}) collective-permute-start(bf16[2,80,1280]{2,1,0:T(8,128)(2,1)S(1)} %pad_maximum_fusion.3.refs_4_), channel_id=1, source_target_pairs={{0,12},{4,0},{8,4},{12,8},{1,13},{5,1},{9,5},{13,9},{2,14},{6,2},{... | collective-permute-start | bytes 1228808 | tf_op jit(solution)/shard_map/ppermute | solution.py:19
  21.0 2.1 %collective-permute-done.1.refs_2_ = bf16[192,1280]{1,0:T(8,128)(2,1)S(1)} collective-permute-done((bf16[192,1280]{1,0:T(8,128)(2,1)S(1)}, bf16[192,1280]{1,0:T(8,128)(2,1)S(1)}, u32[]{:S(2)}, u32[]{:S(2)}) %collective-permute-start.1) | collective-permute-done | bytes 491552 | tf_op jit(solution)/shard_map/ppermute | solution.py:19
  23.1 0.8 copy-done.16
  24.9 11.0 %collective-permute-done.2.refs_3_ = bf16[192,1280]{1,0:T(8,128)(2,1)} collective-permute-done((bf16[192,1280]{1,0:T(8,128)(2,1)S(1)}, bf16[192,1280]{1,0:T(8,128)(2,1)}, u32[]{:S(2)}, u32[]{:S(2)}) %collective-permute-start.2) | collective-permute-done | bytes 491552 | tf_op jit(solution)/shard_map/ppermute | solution.py:19
  36.0 0.9 copy-done.14
  36.9 9.7 %make_z.1 = (f32[2,192,1280]{2,1,0:T(8,128)}, f32[2,192,1280]{2,1,0:T(8,128)}) custom-call(s32[5]{0:T(128)} %stack.65.where, bf16[192,1280]{1,0:T(8,128)(2,1)} %bitcast.61, bf16[192,1280]{1,0:T(8,128)(2,1)} %copy-done.15, bf16[192,1280]{1,0:T(8,128)(2,1)} %copy-done.16, bf16[192,1280]{1,0:T(8,128)(2,1)} %collective-permute-done.2.refs_3_, ...), custom_call_target="tpu_custom_call" | custom-call | flops 2516582400 | bytes 9000000 | tf_op jit(solution)/shard_map/make_z/pallas_call | solution.py:134
  46.6 10.7 %collective-permute-start.11 = (f32[2,192,1280]{2,1,0:T(8,128)}, f32[2,192,1280]{2,1,0:T(8,128)S(1)}, u32[]{:S(2)}, u32[]{:S(2)}) collective-permute-start(f32[2,192,1280]{2,1,0:T(8,128)} %get-tuple-element.12), channel_id=1, source_target_pairs={{0,1},{1,0},{2,3},{3,2},{4,5},{5,4},{6,7},{7,6},{8,9},{9,8},{10,11... | collective-permute-start | bytes 5898248 | tf_op jit(solution)/shard_map/ppermute | solution.py:27
  58.1 0.9 collective-permute-start.24
  59.1 1.0 collective-permute-done.22
  60.1 1.8 collective-permute-done.23
  61.9 0.8 collective-permute-done.24
  62.8 3.8 %collective-permute-start.25 = (f32[32,192]{1,0:T(8,128)S(1)}, f32[32,192]{1,0:T(8,128)S(1)}, u32[]{:S(2)}, u32[]{:S(2)}) collective-permute-start(f32[32,192]{1,0:T(8,128)S(1)} %get-tuple-element.39), channel_id=1, source_target_pairs={{0,96},{32,0},{64,32},{96,64},{1,97},{33,1},{65,33},{97,65},{2,98}... | collective-permute-start | bytes 73736 | tf_op jit(solution)/shard_map/ppermute | solution.py:19
  67.2 1.7 add_convert_fusion
  69.0 4.2 %collective-permute-start.13 = (bf16[192,1280]{1,0:T(8,128)(2,1)S(1)}, bf16[192,1280]{1,0:T(8,128)(2,1)S(1)}, u32[]{:S(2)}, u32[]{:S(2)}) collective-permute-start(bf16[192,1280]{1,0:T(8,128)(2,1)S(1)} %get-tuple-element.18), channel_id=1, source_target_pairs={{0,32},{1,96},{2,0},{3,64},{32,33},{33,97},{34,1},{35,65},{64,34},... | collective-permute-start | bytes 1474568 | tf_op jit(solution)/shard_map/ppermute | solution.py:227
  73.2 7.5 %collective-permute-start.12 = (bf16[192,1280]{1,0:T(8,128)(2,1)S(1)}, bf16[192,1280]{1,0:T(8,128)(2,1)S(1)}, u32[]{:S(2)}, u32[]{:S(2)}) collective-permute-start(bf16[192,1280]{1,0:T(8,128)(2,1)S(1)} %get-tuple-element.17), channel_id=1, source_target_pairs={{0,0},{1,64},{2,32},{3,96},{32,1},{33,65},{34,33},{35,97},{64,2},{... | collective-permute-start | bytes 1474568 | tf_op jit(solution)/shard_map/ppermute | solution.py:227
  80.8 0.8 collective-permute-start.28
  81.6 13.5 %collective-permute-done.28 = f32[128,192]{1,0:T(8,128)S(1)} collective-permute-done((f32[128,192]{1,0:T(8,128)S(1)}, f32[128,192]{1,0:T(8,128)S(1)}, u32[]{:S(2)}, u32[]{:S(2)}) %collective-permute-start.28) | collective-permute-done | bytes 98336 | tf_op jit(solution)/shard_map/ppermute | solution.py:27
  95.9 2.3 %collective-permute-start.19 = (bf16[3,32,1280]{2,1,0:T(8,128)(2,1)S(1)}, bf16[3,32,1280]{2,1,0:T(8,128)(2,1)S(1)}, u32[]{:S(2)}, u32[]{:S(2)}) collective-permute-start(bf16[3,32,1280]{2,1,0:T(8,128)(2,1)S(1)} %bitcast.52), channel_id=1, source_target_pairs={{0,8},{4,12},{8,0},{12,4},{1,9},{5,13},{9,1},{13,5},{2,10},{6,14},... | collective-permute-start | bytes 737288 | tf_op jit(solution)/shard_map/ppermute | solution.py:19
  98.4 7.2 %mix.1 = (bf16[6,64,1280]{2,1,0:T(8,128)(2,1)}, bf16[6,64,1280]{2,1,0:T(8,128)(2,1)}, bf16[6,64,1280]{2,1,0:T(8,128)(2,1)}, bf16[6,64,1280]{2,1,0:T(8,128)(2,1)}) custom-call(s32[5]{0:T(128)} %stack.65.where, f32[256,192]{1,0:T(8,128)} %copy-done.12, bf16[8,256,1280]{2,1,0:T(8,128)(2,1)} %b_ref.1), custom_call_target="tpu_custom_call" | custom-call | flops 1006632960 | bytes 9200000 | tf_op jit(solution)/shard_map/mix/pallas_call | solution.py:67
  105.8 2.5 %collective-permute-start.31 = (bf16[6,64,1280]{2,1,0:T(8,128)(2,1)}, bf16[6,64,1280]{2,1,0:T(8,128)(2,1)S(1)}, u32[]{:S(2)}, u32[]{:S(2)}) collective-permute-start(bf16[6,64,1280]{2,1,0:T(8,128)(2,1)} %get-tuple-element.16), channel_id=1, source_target_pairs={{0,96},{32,0},{64,32},{96,64},{1,97},{33,1},{65,33},{97,65},{2,98}... | collective-permute-start | bytes 2949128 | tf_op jit(solution)/shard_map/ppermute | solution.py:23
  108.7 1.2 collective-permute-start.14
  109.9 27.2 %collective-permute-done.14 = bf16[3,32,1280]{2,1,0:T(8,128)(2,1)S(1)} collective-permute-done((bf16[3,32,1280]{2,1,0:T(8,128)(2,1)S(1)}, bf16[3,32,1280]{2,1,0:T(8,128)(2,1)S(1)}, u32[]{:S(2)}, u32[]{:S(2)}) %collective-permute-start.14) | collective-permute-done | bytes 245792 | tf_op jit(solution)/shard_map/ppermute | solution.py:27
  137.2 0.7 collective-permute-start.15
  137.9 12.1 %collective-permute-done.29.refs_7_ = bf16[6,64,1280]{2,1,0:T(8,128)(2,1)S(1)} collective-permute-done((bf16[6,64,1280]{2,1,0:T(8,128)(2,1)}, bf16[6,64,1280]{2,1,0:T(8,128)(2,1)S(1)}, u32[]{:S(2)}, u32[]{:S(2)}) %collective-permute-start.29) | collective-permute-done | bytes 983072 | tf_op jit(solution)/shard_map/ppermute | solution.py:23
  150.0 2.0 %collective-permute-start.16 = (bf16[2,3,32,1280]{3,2,1,0:T(8,128)(2,1)S(1)}, bf16[2,3,32,1280]{3,2,1,0:T(8,128)(2,1)S(1)}, u32[]{:S(2)}, u32[]{:S(2)}) collective-permute-start(bf16[2,3,32,1280]{3,2,1,0:T(8,128)(2,1)S(1)} %pad_maximum_fusion.2.refs_0_), channel_id=1, source_target_pairs={{0,8},{4,12},{8,0},{12,4},{1,9},{5,13},{9,1},{13,5},{2,10},{6,14},... | collective-permute-start | bytes 1474568 | tf_op jit(solution)/shard_map/ppermute | solution.py:19
  152.0 11.7 %collective-permute-done.16.refs_2_ = bf16[2,3,32,1280]{3,2,1,0:T(8,128)(2,1)S(1)} collective-permute-done((bf16[2,3,32,1280]{3,2,1,0:T(8,128)(2,1)S(1)}, bf16[2,3,32,1280]{3,2,1,0:T(8,128)(2,1)S(1)}, u32[]{:S(2)}, u32[]{:S(2)}) %collective-permute-start.16) | collective-permute-done | bytes 491552 | tf_op jit(solution)/shard_map/ppermute | solution.py:19
  163.7 5.9 %collective-permute-done.17.refs_3_ = bf16[2,3,32,1280]{3,2,1,0:T(8,128)(2,1)S(1)} collective-permute-done((bf16[2,3,32,1280]{3,2,1,0:T(8,128)(2,1)S(1)}, bf16[2,3,32,1280]{3,2,1,0:T(8,128)(2,1)S(1)}, u32[]{:S(2)}, u32[]{:S(2)}) %collective-permute-start.17) | collective-permute-done | bytes 491552 | tf_op jit(solution)/shard_map/ppermute | solution.py:19
  169.7 0.8 copy-done.10
  170.8 6.3 %last.1 = f32[4,64,256]{2,1,0:T(8,128)} custom-call(s32[5]{0:T(128)} %stack.65.where, bf16[2,3,32,1280]{3,2,1,0:T(8,128)(2,1)} %copy-done.1, bf16[2,3,32,1280]{3,2,1,0:T(8,128)(2,1)} %copy-done.8, bf16[2,3,32,1280]{3,2,1,0:T(8,128)(2,1)} %copy-done.9, bf16[2,3,32,1280]{3,2,1,0:T(8,128)(2,1)} %copy-done.10, bf16[4,3,32,1280]{3,2,1,0:T(8,128)(2,1)} %copy-done, ...), custom_call_target="tpu_custom_call" | custom-call | flops 1006632960 | bytes 8000000 | tf_op jit(solution)/shard_map/last/pallas_call | solution.py:185
  177.1 0.9 slice_bitcast_fusion.4
  178.2 2.6 %collective-permute-start.32 = (f32[64,256]{1,0:T(8,128)S(1)}, f32[64,256]{1,0:T(8,128)S(1)}, u32[]{:S(2)}, u32[]{:S(2)}) collective-permute-start(f32[64,256]{1,0:T(8,128)S(1)} %get-tuple-element.25), channel_id=1, source_target_pairs={{0,96},{32,0},{64,32},{96,64},{1,97},{33,1},{65,33},{97,65},{2,98}... | collective-permute-start | bytes 196616 | tf_op jit(solution)/shard_map/ppermute | solution.py:19
  180.8 3.8 %collective-permute-done.34 = f32[64,256]{1,0:T(8,128)S(1)} collective-permute-done((f32[64,256]{1,0:T(8,128)S(1)}, f32[64,256]{1,0:T(8,128)S(1)}, u32[]{:S(2)}, u32[]{:S(2)}) %collective-permute-start.34) | collective-permute-done | bytes 65568 | tf_op jit(solution)/shard_map/ppermute | solution.py:19
  185.0 0.9 fusion.2
  186.0 0.9 collective-permute-start.37
  186.8 5.3 %collective-permute-start.36 = (f32[64,64]{1,0:T(8,128)S(1)}, f32[64,64]{1,0:T(8,128)S(1)}, u32[]{:S(2)}, u32[]{:S(2)}) collective-permute-start(f32[64,64]{1,0:T(8,128)S(1)} %get-tuple-element.30), channel_id=1, source_target_pairs={{0,2},{1,3},{2,0},{3,1},{4,6},{5,7},{6,4},{7,5},{8,10},{9,11},{10,... | collective-permute-start | bytes 49160 | tf_op jit(solution)/shard_map/ppermute | solution.py:23
  192.2 2.1 %collective-permute-start.35 = (f32[64,64]{1,0:T(8,128)S(1)}, f32[64,64]{1,0:T(8,128)S(1)}, u32[]{:S(2)}, u32[]{:S(2)}) collective-permute-start(f32[64,64]{1,0:T(8,128)S(1)} %get-tuple-element.28), channel_id=1, source_target_pairs={{0,1},{1,2},{2,3},{3,0},{4,5},{5,6},{6,7},{7,4},{8,9},{9,10},{10,1... | collective-permute-start | bytes 49160 | tf_op jit(solution)/shard_map/ppermute | solution.py:23
  194.3 1.0 collective-permute-done.35
  195.3 0.6 copy.14
  (92 shorter events, 6.1 us)
Async XLA Ops:
  1.1 10.1 %collective-permute-start.9 = (bf16[80,1280]{1,0:T(8,128)(2,1)S(1)}, bf16[80,1280]{1,0:T(8,128)(2,1)S(1)}, u32[]{:S(2)}, u32[]{:S(2)}) collective-permute-start(bf16[80,1280]{1,0:T(8,128)(2,1)S(1)} %get-tuple-element.23), channel_id=1, source_target_pairs={{0,4},{4,8},{8,12},{12,0},{1,5},{5,9},{9,13},{13,1},{2,6},{6,10},{... | collective-permute-start | bytes 614408 | tf_op jit(solution)/shard_map/ppermute | solution.py:19
  3.3 11.5 %collective-permute-start.8 = (bf16[80,1280]{1,0:T(8,128)(2,1)S(1)}, bf16[80,1280]{1,0:T(8,128)(2,1)S(1)}, u32[]{:S(2)}, u32[]{:S(2)}) collective-permute-start(bf16[80,1280]{1,0:T(8,128)(2,1)S(1)} %get-tuple-element.23), channel_id=1, source_target_pairs={{0,8},{4,12},{8,0},{12,4},{1,9},{5,13},{9,1},{13,5},{2,10},{6,14},... | collective-permute-start | bytes 614408 | tf_op jit(solution)/shard_map/ppermute | solution.py:19
  5.9 8.9 %collective-permute-start.7 = (bf16[80,1280]{1,0:T(8,128)(2,1)S(1)}, bf16[80,1280]{1,0:T(8,128)(2,1)S(1)}, u32[]{:S(2)}, u32[]{:S(2)}) collective-permute-start(bf16[80,1280]{1,0:T(8,128)(2,1)S(1)} %get-tuple-element.23), channel_id=1, source_target_pairs={{0,12},{4,0},{8,4},{12,8},{1,13},{5,1},{9,5},{13,9},{2,14},{6,2},{... | collective-permute-start | bytes 614408 | tf_op jit(solution)/shard_map/ppermute | solution.py:19
  8.1 27.9 %copy-start.7 = (bf16[24,8,1280]{2,1,0:T(8,128)(2,1)}, bf16[24,8,1280]{2,1,0:T(8,128)(2,1)S(1)}, u32[]{:S(2)}) copy-start(bf16[24,8,1280]{2,1,0:T(8,128)(2,1)S(1)} %copy.13) | copy-start | bytes 1474564
  8.1 12.6 %collective-permute-start = (bf16[192,1280]{1,0:T(8,128)(2,1)S(1)}, bf16[192,1280]{1,0:T(8,128)(2,1)S(1)}, u32[]{:S(2)}, u32[]{:S(2)}) collective-permute-start(bf16[192,1280]{1,0:T(8,128)(2,1)S(1)} %bitcast.58), channel_id=1, source_target_pairs={{0,96},{32,0},{64,32},{96,64},{1,97},{33,1},{65,33},{97,65},{2,98}... | collective-permute-start | bytes 1474568 | tf_op jit(solution)/shard_map/ppermute | solution.py:19
  10.6 12.5 %collective-permute-start.1 = (bf16[192,1280]{1,0:T(8,128)(2,1)S(1)}, bf16[192,1280]{1,0:T(8,128)(2,1)S(1)}, u32[]{:S(2)}, u32[]{:S(2)}) collective-permute-start(bf16[192,1280]{1,0:T(8,128)(2,1)S(1)} %bitcast.59), channel_id=1, source_target_pairs={{0,64},{32,96},{64,0},{96,32},{1,65},{33,97},{65,1},{97,33},{2,66}... | collective-permute-start | bytes 1474568 | tf_op jit(solution)/shard_map/ppermute | solution.py:19
  11.2 6.7 %collective-permute-start.3 = (bf16[80,1280]{1,0:T(8,128)(2,1)S(1)}, bf16[80,1280]{1,0:T(8,128)(2,1)S(1)}, u32[]{:S(2)}, u32[]{:S(2)}) collective-permute-start(bf16[80,1280]{1,0:T(8,128)(2,1)S(1)} %get-tuple-element.24), channel_id=1, source_target_pairs={{0,16},{16,0},{1,17},{17,1},{2,18},{18,2},{3,19},{19,3},{4,20},{20... | collective-permute-start | bytes 614408 | tf_op jit(solution)/shard_map/ppermute | solution.py:27
  14.9 21.1 %copy-start.6 = (bf16[4,80,1280]{2,1,0:T(8,128)(2,1)}, bf16[4,80,1280]{2,1,0:T(8,128)(2,1)S(1)}, u32[]{:S(2)}) copy-start(bf16[4,80,1280]{2,1,0:T(8,128)(2,1)S(1)} %pad_maximum_fusion.1.refs_8_) | copy-start | bytes 2457604
  14.9 21.1 %collective-permute-start.10 = (bf16[4,80,1280]{2,1,0:T(8,128)(2,1)S(1)}, bf16[4,80,1280]{2,1,0:T(8,128)(2,1)S(1)}, u32[]{:S(2)}, u32[]{:S(2)}) collective-permute-start(bf16[4,80,1280]{2,1,0:T(8,128)(2,1)S(1)} %pad_maximum_fusion.1.refs_8_), channel_id=1, source_target_pairs={{0,16},{16,0},{1,17},{17,1},{2,18},{18,2},{3,19},{19,3},{4,20},{20... | collective-permute-start | bytes 2457608 | tf_op jit(solution)/shard_map/ppermute | solution.py:27
  16.6 19.3 %collective-permute-start.2 = (bf16[192,1280]{1,0:T(8,128)(2,1)S(1)}, bf16[192,1280]{1,0:T(8,128)(2,1)}, u32[]{:S(2)}, u32[]{:S(2)}) collective-permute-start(bf16[192,1280]{1,0:T(8,128)(2,1)S(1)} %bitcast.60), channel_id=1, source_target_pairs={{0,32},{32,64},{64,96},{96,0},{1,33},{33,65},{65,97},{97,1},{2,34}... | collective-permute-start | bytes 1474568 | tf_op jit(solution)/shard_map/ppermute | solution.py:19
  17.9 18.1 %copy-start.11 = (bf16[2,80,1280]{2,1,0:T(8,128)(2,1)}, bf16[2,80,1280]{2,1,0:T(8,128)(2,1)S(1)}, u32[]{:S(2)}) copy-start(bf16[2,80,1280]{2,1,0:T(8,128)(2,1)S(1)} %pad_maximum_fusion.3.refs_4_) | copy-start | bytes 1228804
  17.9 18.1 %collective-permute-start.4 = (bf16[2,80,1280]{2,1,0:T(8,128)(2,1)S(1)}, bf16[2,80,1280]{2,1,0:T(8,128)(2,1)}, u32[]{:S(2)}, u32[]{:S(2)}) collective-permute-start(bf16[2,80,1280]{2,1,0:T(8,128)(2,1)S(1)} %pad_maximum_fusion.3.refs_4_), channel_id=1, source_target_pairs={{0,12},{4,0},{8,4},{12,8},{1,13},{5,1},{9,5},{13,9},{2,14},{6,2},{... | collective-permute-start | bytes 1228808 | tf_op jit(solution)/shard_map/ppermute | solution.py:19
  20.7 15.2 %collective-permute-start.5 = (bf16[2,80,1280]{2,1,0:T(8,128)(2,1)S(1)}, bf16[2,80,1280]{2,1,0:T(8,128)(2,1)}, u32[]{:S(2)}, u32[]{:S(2)}) collective-permute-start(bf16[2,80,1280]{2,1,0:T(8,128)(2,1)S(1)} %pad_maximum_fusion.3.refs_4_), channel_id=1, source_target_pairs={{0,8},{4,12},{8,0},{12,4},{1,9},{5,13},{9,1},{13,5},{2,10},{6,14},... | collective-permute-start | bytes 1228808 | tf_op jit(solution)/shard_map/ppermute | solution.py:19
  23.9 12.0 %collective-permute-start.6 = (bf16[2,80,1280]{2,1,0:T(8,128)(2,1)S(1)}, bf16[2,80,1280]{2,1,0:T(8,128)(2,1)}, u32[]{:S(2)}, u32[]{:S(2)}) collective-permute-start(bf16[2,80,1280]{2,1,0:T(8,128)(2,1)S(1)} %pad_maximum_fusion.3.refs_4_), channel_id=1, source_target_pairs={{0,4},{4,8},{8,12},{12,0},{1,5},{5,9},{9,13},{13,1},{2,6},{6,10},{... | collective-permute-start | bytes 1228808 | tf_op jit(solution)/shard_map/ppermute | solution.py:19
  24.9 32.4 %copy-start.13 = (bf16[8,24,8]{1,2,0:T(8,128)(2,1)S(1)}, bf16[8,24,8]{1,2,0:T(8,128)(2,1)}, u32[]{:S(2)}) copy-start(bf16[8,24,8]{1,2,0:T(8,128)(2,1)} %param.5) | copy-start | bytes 9220
  46.6 20.6 %collective-permute-start.11 = (f32[2,192,1280]{2,1,0:T(8,128)}, f32[2,192,1280]{2,1,0:T(8,128)S(1)}, u32[]{:S(2)}, u32[]{:S(2)}) collective-permute-start(f32[2,192,1280]{2,1,0:T(8,128)} %get-tuple-element.12), channel_id=1, source_target_pairs={{0,1},{1,0},{2,3},{3,2},{4,5},{5,4},{6,7},{7,6},{8,9},{9,8},{10,11... | collective-permute-start | bytes 5898248 | tf_op jit(solution)/shard_map/ppermute | solution.py:27
  57.5 2.6 %collective-permute-start.22 = (f32[8,192]{1,0:T(8,128)S(1)}, f32[8,192]{1,0:T(8,128)S(1)}, u32[]{:S(2)}, u32[]{:S(2)}) collective-permute-start(f32[8,192]{1,0:T(8,128)S(1)} %reshape.16), channel_id=1, source_target_pairs={{0,12},{4,0},{8,4},{12,8},{1,13},{5,1},{9,5},{13,9},{2,14},{6,2},{... | collective-permute-start | bytes 18440 | tf_op jit(solution)/shard_map/ppermute | solution.py:19
  57.9 4.0 %collective-permute-start.23 = (f32[8,192]{1,0:T(8,128)S(1)}, f32[8,192]{1,0:T(8,128)S(1)}, u32[]{:S(2)}, u32[]{:S(2)}) collective-permute-start(f32[8,192]{1,0:T(8,128)S(1)} %reshape.16), channel_id=1, source_target_pairs={{0,8},{4,12},{8,0},{12,4},{1,9},{5,13},{9,1},{13,5},{2,10},{6,14},... | collective-permute-start | bytes 18440 | tf_op jit(solution)/shard_map/ppermute | solution.py:19
  58.1 4.7 %collective-permute-start.24 = (f32[8,192]{1,0:T(8,128)S(1)}, f32[8,192]{1,0:T(8,128)S(1)}, u32[]{:S(2)}, u32[]{:S(2)}) collective-permute-start(f32[8,192]{1,0:T(8,128)S(1)} %reshape.16), channel_id=1, source_target_pairs={{0,4},{4,8},{8,12},{12,0},{1,5},{5,9},{9,13},{13,1},{2,6},{6,10},{... | collective-permute-start | bytes 18440 | tf_op jit(solution)/shard_map/ppermute | solution.py:19
  62.8 17.9 %collective-permute-start.25 = (f32[32,192]{1,0:T(8,128)S(1)}, f32[32,192]{1,0:T(8,128)S(1)}, u32[]{:S(2)}, u32[]{:S(2)}) collective-permute-start(f32[32,192]{1,0:T(8,128)S(1)} %get-tuple-element.39), channel_id=1, source_target_pairs={{0,96},{32,0},{64,32},{96,64},{1,97},{33,1},{65,33},{97,65},{2,98}... | collective-permute-start | bytes 73736 | tf_op jit(solution)/shard_map/ppermute | solution.py:19
  66.6 14.2 %collective-permute-start.26 = (f32[32,192]{1,0:T(8,128)S(1)}, f32[32,192]{1,0:T(8,128)S(1)}, u32[]{:S(2)}, u32[]{:S(2)}) collective-permute-start(f32[32,192]{1,0:T(8,128)S(1)} %get-tuple-element.39), channel_id=1, source_target_pairs={{0,64},{32,96},{64,0},{96,32},{1,65},{33,97},{65,1},{97,33},{2,66}... | collective-permute-start | bytes 73736 | tf_op jit(solution)/shard_map/ppermute | solution.py:19
  66.6 14.2 %collective-permute-start.27 = (f32[32,192]{1,0:T(8,128)S(1)}, f32[32,192]{1,0:T(8,128)S(1)}, u32[]{:S(2)}, u32[]{:S(2)}) collective-permute-start(f32[32,192]{1,0:T(8,128)S(1)} %get-tuple-element.39), channel_id=1, source_target_pairs={{0,32},{32,64},{64,96},{96,0},{1,33},{33,65},{65,97},{97,1},{2,34}... | collective-permute-start | bytes 73736 | tf_op jit(solution)/shard_map/ppermute | solution.py:19
  69.0 26.2 %collective-permute-start.13 = (bf16[192,1280]{1,0:T(8,128)(2,1)S(1)}, bf16[192,1280]{1,0:T(8,128)(2,1)S(1)}, u32[]{:S(2)}, u32[]{:S(2)}) collective-permute-start(bf16[192,1280]{1,0:T(8,128)(2,1)S(1)} %get-tuple-element.18), channel_id=1, source_target_pairs={{0,32},{1,96},{2,0},{3,64},{32,33},{33,97},{34,1},{35,65},{64,34},... | collective-permute-start | bytes 1474568 | tf_op jit(solution)/shard_map/ppermute | solution.py:227
  73.2 22.0 %collective-permute-start.12 = (bf16[192,1280]{1,0:T(8,128)(2,1)S(1)}, bf16[192,1280]{1,0:T(8,128)(2,1)S(1)}, u32[]{:S(2)}, u32[]{:S(2)}) collective-permute-start(bf16[192,1280]{1,0:T(8,128)(2,1)S(1)} %get-tuple-element.17), channel_id=1, source_target_pairs={{0,0},{1,64},{2,32},{3,96},{32,1},{33,65},{34,33},{35,97},{64,2},{... | collective-permute-start | bytes 1474568 | tf_op jit(solution)/shard_map/ppermute | solution.py:227
  80.8 14.3 %collective-permute-start.28 = (f32[128,192]{1,0:T(8,128)S(1)}, f32[128,192]{1,0:T(8,128)S(1)}, u32[]{:S(2)}, u32[]{:S(2)}) collective-permute-start(f32[128,192]{1,0:T(8,128)S(1)} %get-tuple-element.31), channel_id=1, source_target_pairs={{0,16},{16,0},{1,17},{17,1},{2,18},{18,2},{3,19},{19,3},{4,20},{20... | collective-permute-start | bytes 294920 | tf_op jit(solution)/shard_map/ppermute | solution.py:27
  95.3 10.5 %collective-permute-start.20 = (bf16[3,32,1280]{2,1,0:T(8,128)(2,1)S(1)}, bf16[3,32,1280]{2,1,0:T(8,128)(2,1)S(1)}, u32[]{:S(2)}, u32[]{:S(2)}) collective-permute-start(bf16[3,32,1280]{2,1,0:T(8,128)(2,1)S(1)} %bitcast.51), channel_id=1, source_target_pairs={{0,4},{4,8},{8,12},{12,0},{1,5},{5,9},{9,13},{13,1},{2,6},{6,10},{... | collective-permute-start | bytes 737288 | tf_op jit(solution)/shard_map/ppermute | solution.py:19
  95.9 12.3 %collective-permute-start.19 = (bf16[3,32,1280]{2,1,0:T(8,128)(2,1)S(1)}, bf16[3,32,1280]{2,1,0:T(8,128)(2,1)S(1)}, u32[]{:S(2)}, u32[]{:S(2)}) collective-permute-start(bf16[3,32,1280]{2,1,0:T(8,128)(2,1)S(1)} %bitcast.52), channel_id=1, source_target_pairs={{0,8},{4,12},{8,0},{12,4},{1,9},{5,13},{9,1},{13,5},{2,10},{6,14},... | collective-permute-start | bytes 737288 | tf_op jit(solution)/shard_map/ppermute | solution.py:19
  98.2 10.1 %collective-permute-start.18 = (bf16[3,32,1280]{2,1,0:T(8,128)(2,1)S(1)}, bf16[3,32,1280]{2,1,0:T(8,128)(2,1)S(1)}, u32[]{:S(2)}, u32[]{:S(2)}) collective-permute-start(bf16[3,32,1280]{2,1,0:T(8,128)(2,1)S(1)} %bitcast.53), channel_id=1, source_target_pairs={{0,12},{4,0},{8,4},{12,8},{1,13},{5,1},{9,5},{13,9},{2,14},{6,2},{... | collective-permute-start | bytes 737288 | tf_op jit(solution)/shard_map/ppermute | solution.py:19
  105.6 44.4 %collective-permute-start.29 = (bf16[6,64,1280]{2,1,0:T(8,128)(2,1)}, bf16[6,64,1280]{2,1,0:T(8,128)(2,1)S(1)}, u32[]{:S(2)}, u32[]{:S(2)}) collective-permute-start(bf16[6,64,1280]{2,1,0:T(8,128)(2,1)} %get-tuple-element.14), channel_id=1, source_target_pairs={{0,32},{32,64},{64,96},{96,0},{1,33},{33,65},{65,97},{97,1},{2,34}... | collective-permute-start | bytes 2949128 | tf_op jit(solution)/shard_map/ppermute | solution.py:23
  105.6 46.4 %collective-permute-start.30 = (bf16[6,64,1280]{2,1,0:T(8,128)(2,1)}, bf16[6,64,1280]{2,1,0:T(8,128)(2,1)S(1)}, u32[]{:S(2)}, u32[]{:S(2)}) collective-permute-start(bf16[6,64,1280]{2,1,0:T(8,128)(2,1)} %get-tuple-element.15), channel_id=1, source_target_pairs={{0,64},{32,96},{64,0},{96,32},{1,65},{33,97},{65,1},{97,33},{2,66}... | collective-permute-start | bytes 2949128 | tf_op jit(solution)/shard_map/ppermute | solution.py:23
  105.8 46.2 %collective-permute-start.31 = (bf16[6,64,1280]{2,1,0:T(8,128)(2,1)}, bf16[6,64,1280]{2,1,0:T(8,128)(2,1)S(1)}, u32[]{:S(2)}, u32[]{:S(2)}) collective-permute-start(bf16[6,64,1280]{2,1,0:T(8,128)(2,1)} %get-tuple-element.16), channel_id=1, source_target_pairs={{0,96},{32,0},{64,32},{96,64},{1,97},{33,1},{65,33},{97,65},{2,98}... | collective-permute-start | bytes 2949128 | tf_op jit(solution)/shard_map/ppermute | solution.py:23
  108.4 61.3 %copy-start = (bf16[4,3,32,1280]{3,2,1,0:T(8,128)(2,1)}, bf16[4,3,32,1280]{3,2,1,0:T(8,128)(2,1)S(1)}, u32[]{:S(2)}) copy-start(bf16[4,3,32,1280]{3,2,1,0:T(8,128)(2,1)S(1)} %pad_maximum_fusion.refs_4_) | copy-start | bytes 2949124
  108.4 61.3 %collective-permute-start.21 = (bf16[4,3,32,1280]{3,2,1,0:T(8,128)(2,1)S(1)}, bf16[4,3,32,1280]{3,2,1,0:T(8,128)(2,1)S(1)}, u32[]{:S(2)}, u32[]{:S(2)}) collective-permute-start(bf16[4,3,32,1280]{3,2,1,0:T(8,128)(2,1)S(1)} %pad_maximum_fusion.refs_4_), channel_id=1, source_target_pairs={{0,16},{16,0},{1,17},{17,1},{2,18},{18,2},{3,19},{19,3},{4,20},{20... | collective-permute-start | bytes 2949128 | tf_op jit(solution)/shard_map/ppermute | solution.py:27
  108.7 28.4 %collective-permute-start.14 = (bf16[3,32,1280]{2,1,0:T(8,128)(2,1)S(1)}, bf16[3,32,1280]{2,1,0:T(8,128)(2,1)S(1)}, u32[]{:S(2)}, u32[]{:S(2)}) collective-permute-start(bf16[3,32,1280]{2,1,0:T(8,128)(2,1)S(1)} %bitcast.55), channel_id=1, source_target_pairs={{0,16},{16,0},{1,17},{17,1},{2,18},{18,2},{3,19},{19,3},{4,20},{20... | collective-permute-start | bytes 737288 | tf_op jit(solution)/shard_map/ppermute | solution.py:27
  137.2 32.5 %copy-start.1 = (bf16[2,3,32,1280]{3,2,1,0:T(8,128)(2,1)}, bf16[2,3,32,1280]{3,2,1,0:T(8,128)(2,1)S(1)}, u32[]{:S(2)}) copy-start(bf16[2,3,32,1280]{3,2,1,0:T(8,128)(2,1)S(1)} %pad_maximum_fusion.2.refs_0_) | copy-start | bytes 1474564
  137.2 14.8 %collective-permute-start.15 = (bf16[2,3,32,1280]{3,2,1,0:T(8,128)(2,1)S(1)}, bf16[2,3,32,1280]{3,2,1,0:T(8,128)(2,1)S(1)}, u32[]{:S(2)}, u32[]{:S(2)}) collective-permute-start(bf16[2,3,32,1280]{3,2,1,0:T(8,128)(2,1)S(1)} %pad_maximum_fusion.2.refs_0_), channel_id=1, source_target_pairs={{0,12},{4,0},{8,4},{12,8},{1,13},{5,1},{9,5},{13,9},{2,14},{6,2},{... | collective-permute-start | bytes 1474568 | tf_op jit(solution)/shard_map/ppermute | solution.py:19
  150.0 19.7 %copy-start.2 = (bf16[6,64,1280]{2,1,0:T(8,128)(2,1)}, bf16[6,64,1280]{2,1,0:T(8,128)(2,1)S(1)}, u32[]{:S(2)}) copy-start(bf16[6,64,1280]{2,1,0:T(8,128)(2,1)S(1)} %collective-permute-done.29.refs_7_) | copy-start | bytes 2949124
  150.0 13.8 %collective-permute-start.16 = (bf16[2,3,32,1280]{3,2,1,0:T(8,128)(2,1)S(1)}, bf16[2,3,32,1280]{3,2,1,0:T(8,128)(2,1)S(1)}, u32[]{:S(2)}, u32[]{:S(2)}) collective-permute-start(bf16[2,3,32,1280]{3,2,1,0:T(8,128)(2,1)S(1)} %pad_maximum_fusion.2.refs_0_), channel_id=1, source_target_pairs={{0,8},{4,12},{8,0},{12,4},{1,9},{5,13},{9,1},{13,5},{2,10},{6,14},... | collective-permute-start | bytes 1474568 | tf_op jit(solution)/shard_map/ppermute | solution.py:19
  152.0 17.7 %copy-start.3 = (bf16[6,64,1280]{2,1,0:T(8,128)(2,1)}, bf16[6,64,1280]{2,1,0:T(8,128)(2,1)S(1)}, u32[]{:S(2)}) copy-start(bf16[6,64,1280]{2,1,0:T(8,128)(2,1)S(1)} %collective-permute-done.30.refs_8_) | copy-start | bytes 2949124
  152.0 17.7 %collective-permute-start.17 = (bf16[2,3,32,1280]{3,2,1,0:T(8,128)(2,1)S(1)}, bf16[2,3,32,1280]{3,2,1,0:T(8,128)(2,1)S(1)}, u32[]{:S(2)}, u32[]{:S(2)}) collective-permute-start(bf16[2,3,32,1280]{3,2,1,0:T(8,128)(2,1)S(1)} %pad_maximum_fusion.2.refs_0_), channel_id=1, source_target_pairs={{0,4},{4,8},{8,12},{12,0},{1,5},{5,9},{9,13},{13,1},{2,6},{6,10},{... | collective-permute-start | bytes 1474568 | tf_op jit(solution)/shard_map/ppermute | solution.py:19
  152.0 17.7 %copy-start.4 = (bf16[6,64,1280]{2,1,0:T(8,128)(2,1)}, bf16[6,64,1280]{2,1,0:T(8,128)(2,1)S(1)}, u32[]{:S(2)}) copy-start(bf16[6,64,1280]{2,1,0:T(8,128)(2,1)S(1)} %collective-permute-done.31.refs_9_) | copy-start | bytes 2949124
  152.0 17.7 %copy-start.8 = (bf16[2,3,32,1280]{3,2,1,0:T(8,128)(2,1)}, bf16[2,3,32,1280]{3,2,1,0:T(8,128)(2,1)S(1)}, u32[]{:S(2)}) copy-start(bf16[2,3,32,1280]{3,2,1,0:T(8,128)(2,1)S(1)} %collective-permute-done.15.refs_1_) | copy-start | bytes 1474564
  178.0 6.6 %collective-permute-start.34 = (f32[64,256]{1,0:T(8,128)S(1)}, f32[64,256]{1,0:T(8,128)S(1)}, u32[]{:S(2)}, u32[]{:S(2)}) collective-permute-start(f32[64,256]{1,0:T(8,128)S(1)} %get-tuple-element.26), channel_id=1, source_target_pairs={{0,32},{32,64},{64,96},{96,0},{1,33},{33,65},{65,97},{97,1},{2,34}... | collective-permute-start | bytes 196616 | tf_op jit(solution)/shard_map/ppermute | solution.py:19
  178.1 6.5 %collective-permute-start.33 = (f32[64,256]{1,0:T(8,128)S(1)}, f32[64,256]{1,0:T(8,128)S(1)}, u32[]{:S(2)}, u32[]{:S(2)}) collective-permute-start(f32[64,256]{1,0:T(8,128)S(1)} %get-tuple-element.27), channel_id=1, source_target_pairs={{0,64},{32,96},{64,0},{96,32},{1,65},{33,97},{65,1},{97,33},{2,66}... | collective-permute-start | bytes 196616 | tf_op jit(solution)/shard_map/ppermute | solution.py:19
  178.2 6.8 %collective-permute-start.32 = (f32[64,256]{1,0:T(8,128)S(1)}, f32[64,256]{1,0:T(8,128)S(1)}, u32[]{:S(2)}, u32[]{:S(2)}) collective-permute-start(f32[64,256]{1,0:T(8,128)S(1)} %get-tuple-element.25), channel_id=1, source_target_pairs={{0,96},{32,0},{64,32},{96,64},{1,97},{33,1},{65,33},{97,65},{2,98}... | collective-permute-start | bytes 196616 | tf_op jit(solution)/shard_map/ppermute | solution.py:19
  186.0 8.3 %collective-permute-start.37 = (f32[64,64]{1,0:T(8,128)S(1)}, f32[64,64]{1,0:T(8,128)S(1)}, u32[]{:S(2)}, u32[]{:S(2)}) collective-permute-start(f32[64,64]{1,0:T(8,128)S(1)} %get-tuple-element.29), channel_id=1, source_target_pairs={{0,3},{1,0},{2,1},{3,2},{4,7},{5,4},{6,5},{7,6},{8,11},{9,8},{10,9... | collective-permute-start | bytes 49160 | tf_op jit(solution)/shard_map/ppermute | solution.py:23
  186.8 7.4 %collective-permute-start.36 = (f32[64,64]{1,0:T(8,128)S(1)}, f32[64,64]{1,0:T(8,128)S(1)}, u32[]{:S(2)}, u32[]{:S(2)}) collective-permute-start(f32[64,64]{1,0:T(8,128)S(1)} %get-tuple-element.30), channel_id=1, source_target_pairs={{0,2},{1,3},{2,0},{3,1},{4,6},{5,7},{6,4},{7,5},{8,10},{9,11},{10,... | collective-permute-start | bytes 49160 | tf_op jit(solution)/shard_map/ppermute | solution.py:23
  192.2 3.1 %collective-permute-start.35 = (f32[64,64]{1,0:T(8,128)S(1)}, f32[64,64]{1,0:T(8,128)S(1)}, u32[]{:S(2)}, u32[]{:S(2)}) collective-permute-start(f32[64,64]{1,0:T(8,128)S(1)} %get-tuple-element.28), channel_id=1, source_target_pairs={{0,1},{1,2},{2,3},{3,0},{4,5},{5,6},{6,7},{7,4},{8,9},{9,10},{10,1... | collective-permute-start | bytes 49160 | tf_op jit(solution)/shard_map/ppermute | solution.py:23
  (7 other events, 28.2 us)

commit v2 on v1

v2 whole, which is shorter than its diff:
```python
import jax
import jax.numpy as jnp
from jax import lax
from jax.experimental import pallas as pl
from jax.experimental.pallas import tpu as pltpu
from jax.sharding import Mesh, PartitionSpec as P

F32, BF16 = jnp.float32, jnp.bfloat16
ANY = pl.BlockSpec(memory_space=pl.ANY)
SMEM = pl.BlockSpec(memory_space=pltpu.SMEM)
VMEM = pl.BlockSpec(memory_space=pltpu.VMEM)
VMEM_LIMIT = 56 * 1024 * 1024

NX, NY = 4, 4
NT = (((1,), (1,)), ((), ()))


def shift_from(a, axis, s):
    return lax.ppermute(a, axis, [(i, (i - s) % 4) for i in range(4)])


def shift_to(a, axis, s):
    return lax.ppermute(a, axis, [(i, (i + s) % 4) for i in range(4)])


def swap(a, axis):
    return lax.ppermute(a, axis, [(0, 1), (1, 0)])


def start_gather(own):
    return swap(own, "zl"), shift_from(own, "y", 1), shift_from(own, "y", 3), shift_from(own, "y", 2)


def end_gather(own, other, one, three, two):
    other_two = swap(two, "zl")
    other_one, other_three = shift_from(other, "y", 1), shift_from(other, "y", 3)
    return [own, one, two, three, other, other_one, other_two, other_three]


def mixed_kernel(where, x_ref, b_ref, *refs):
    outs, xs, rows = refs[:4], refs[4], refs[5]

    @pl.when(pl.program_id(0) == 0)
    def _():
        x = where[0]
        rows[...] = x_ref[...].T
        for j in range(4):
            q = (x + j) % 4
            xs[j * 48 : j * 48 + 48, :] = rows[pl.ds(pl.multiple_of(q * 48, 48), 48), :].astype(BF16)

    lhs = xs[...]
    for pair in range(4):
        two = [jnp.dot(lhs, b_ref[2 * pair + i], preferred_element_type=F32) for i in range(2)]
        for j in range(4):
            for w in range(6):
                at = (j * 6 + w) * 8
                both = jnp.concatenate([t[at : at + 8] for t in two], axis=0)
                outs[j][w, 16 * pair : 16 * pair + 16, :] = both.astype(BF16)


def mix(where, x_all, cond):
    g = cond.shape[2]
    step = 256
    return pl.pallas_call(
        mixed_kernel,
        grid=(g // step,),
        in_specs=[
            SMEM,
            pl.BlockSpec((256, 192), lambda i: (0, 0)),
            pl.BlockSpec((8, 256, step), lambda i: (0, 0, i)),
        ],
        out_specs=[pl.BlockSpec((6, 64, step), lambda i: (0, 0, i))] * 4,
        out_shape=[jax.ShapeDtypeStruct((6, 64, g), BF16)] * 4,
        scratch_shapes=[pltpu.VMEM((192, 256), BF16), pltpu.VMEM((192, 256), F32)],
        compiler_params=pltpu.CompilerParams(vmem_limit_bytes=VMEM_LIMIT),
        cost_estimate=pl.CostEstimate(flops=2 * 192 * 256 * 8 * g, bytes_accessed=9200000, transcendentals=0),
        name="mix",
    )(where, x_all, cond)


def z_kernel(where, m, *refs):
    w = refs[0:8]
    send, keep, ms, ws, m_sem, w_sem = refs[8:]
    zl, y, zh, core = where[1], where[2], where[3], where[4]
    copies = []
    for t in range(4):
        owner = 1 - core if t < 2 else core
        q = 2 * owner + (zh + t % 2) % 2
        for r in range(4):
            to = ms.at[t // 2, pl.ds((t % 2 * 4 + r) * 48, 48)]
            at = pl.ds(pl.multiple_of(192 * r + q * 48, 48), 48)
            copies.append(pltpu.make_async_copy(m.at[at], to, m_sem.at[t * 4 + r]))
    for at in range(8):
        to = ((zl + at // 4) % 2 * 4 + (y + at % 4) % 4) * 160
        copies.append(pltpu.make_async_copy(w[at], ws.at[pl.ds(pl.multiple_of(to, 160), 160)], w_sem.at[at]))
    for c in copies:
        c.start()
    for c in copies:
        c.wait()

    for half, out in enumerate((send, keep)):

        @pl.loop(0, 5)
        def _(n, half=half, out=out):
            cols = pl.ds(pl.multiple_of(256 * n, 256), 256)
            res = lax.dot_general(ms[half], ws[cols, :], NT, preferred_element_type=F32)
            for a in range(2):
                for w in range(6):
                    for r in range(4):
                        at = ((a * 4 + r) * 6 + w) * 8
                        out[a, (w * 4 + r) * 8 : (w * 4 + r) * 8 + 8, cols] = res[at : at + 8]


def make_z(where, m, w):
    g = m.shape[1]
    shape = jax.ShapeDtypeStruct((2, 192, g), F32)
    return pl.pallas_call(
        z_kernel,
        in_specs=[SMEM] + [ANY] * 9,
        out_specs=[VMEM, VMEM],
        out_shape=[shape, shape],
        scratch_shapes=[
            pltpu.VMEM((2, 384, g), BF16),
            pltpu.VMEM((g, g), BF16),
            pltpu.SemaphoreType.DMA((16,)),
            pltpu.SemaphoreType.DMA((8,)),
        ],
        compiler_params=pltpu.CompilerParams(vmem_limit_bytes=VMEM_LIMIT),
        cost_estimate=pl.CostEstimate(flops=2 * 768 * g * g, bytes_accessed=9000000, transcendentals=0),
        name="make_z",
    )(where, m, *w)


def last_kernel(where, *refs):
    z, mx = refs[0:8], refs[8:12]
    out, zs, xs, total, sem = refs[12:]
    x, zl, y = where[0], where[1], where[2]
    copies = []
    for at in range(8):
        copies.append(pltpu.make_async_copy(z[at], zs.at[:, at], sem.at[at]))
    for j in range(4):
        copies.append(pltpu.make_async_copy(mx[j], xs.at[:, (x + 4 - j) % 4], sem.at[8 + j]))
    for c in copies:
        c.start()
    for c in copies:
        c.wait()
    sums = jnp.zeros((256, 256), F32)
    for w in range(6):
        lhs = zs[w].reshape(256, zs.shape[3])
        rhs = xs[w].reshape(256, xs.shape[3])
        sums = sums + lax.dot_general(lhs, rhs, NT, preferred_element_type=F32)
    for z_of in range(2):
        for y_of in range(4):
            to = ((zl + z_of) % 2 * 4 + (y + y_of) % 4) * 8
            for r in range(4):
                at = ((z_of * 4 + y_of) * 4 + r) * 8
                total[pl.ds(pl.multiple_of(r * 64 + to, 8), 8), :] = sums[at : at + 8]
    turned = total[...].T
    for j in range(4):
        for p in range(4):
            cols = slice(64 * p, 64 * p + 64)
            halves = [turned[64 * j + at : 64 * j + at + 32, cols] for at in (0, 32)]
            out[4 * j + p] = jnp.concatenate(halves, axis=1)


def last(where, z, mixed):
    g = mixed[0].shape[2]
    return pl.pallas_call(
        last_kernel,
        in_specs=[SMEM] + [ANY] * 12,
        out_specs=VMEM,
        out_shape=jax.ShapeDtypeStruct((16, 32, 128), F32),
        scratch_shapes=[
            pltpu.VMEM((6, 8, 32, g), BF16),
            pltpu.VMEM((6, 4, 64, g), BF16),
            pltpu.VMEM((256, 256), F32),
            pltpu.SemaphoreType.DMA((12,)),
        ],
        compiler_params=pltpu.CompilerParams(vmem_limit_bytes=VMEM_LIMIT),
        cost_estimate=pl.CostEstimate(flops=2 * 256 * 256 * 6 * g, bytes_accessed=8000000, transcendentals=0),
        name="last",
    )(where, *z, *mixed)


def shards(cond_pairs, vectors, screened, val_pairs):
    g = cond_pairs.shape[2]
    axes = ("x", "zl", "y", "zh", "core")
    where = jnp.stack([lax.axis_index(a) for a in axes]).astype(jnp.int32)

    m_own = jnp.transpose(val_pairs, (1, 0, 2)).reshape(192, g)
    m = lax.all_gather(m_own, "x", axis=0, tiled=True)

    w_own = screened.T
    w = start_gather(w_own)

    own = jnp.transpose(vectors, (2, 1, 0)).reshape(1, 8, 192).astype(F32)
    x_all = lax.all_to_all(jnp.broadcast_to(own, (32, 8, 192)), ("x", "zl", "y"), split_axis=0, concat_axis=0, tiled=True)

    w, x_all = lax.optimization_barrier((w, x_all.reshape(256, 192)))
    w = end_gather(w_own, *w)
    mixed = mix(where, x_all, cond_pairs)
    m, w, mixed = lax.optimization_barrier((m, w, list(mixed)))
    mixed[1], mixed[3] = shift_to(mixed[1], "x", 1), shift_to(mixed[3], "x", 3)

    send, keep = make_z(where, m, w)
    part = (keep + swap(send, "core")).astype(BF16)
    got = []
    for a in range(2):
        perm = [
            (x * 4 + zh * 2 + c, (2 * c + (zh ^ a)) * 4 + x) for x in range(4) for zh in range(2) for c in range(2)
        ]
        got.append(lax.ppermute(part[a], ("x", "zh", "core"), perm))
    got, mixed = lax.optimization_barrier((got, mixed))
    mixed[2] = shift_to(mixed[2], "x", 2)
    z_own = (got[0].astype(F32) + got[1].astype(F32)).astype(BF16).reshape(6, 32, g)
    z = end_gather(z_own, *start_gather(z_own))

    sums = last(where, z, mixed)
    sums = lax.all_to_all(sums, ("x", "zh", "core"), split_axis=0, concat_axis=0, tiled=True)
    total = jnp.sum(sums, axis=0)
    total = jnp.stack([total[:, :64], total[:, 64:]])
    return jnp.transpose(total.reshape(8, 8, 64), (1, 2, 0))


def solution(mesh):
    fine = Mesh(mesh.devices.reshape(4, 2, 4, 2, 2), ("x", "zl", "y", "zh", "core"))
    band, pw = ("x", "zl", "y"), ("zh", "core")
    return jax.shard_map(
        shards,
        mesh=fine,
        in_specs=(P(band, None, pw), P(None, None, band), P(pw, band), P(band, None, pw)),
        out_specs=P(None, pw, band),
        check_vma=False,
    )
```

time: 197 us -> 167 us (0.85)
  waiting for transfers between devices: 94.6 us -> 51.1 us
  blocking collectives: 0 us -> 36.4 us
  starting transfers between devices: 67.2 us -> 33.7 us
  between operations: 0.41 us -> 13.6 us
    all_to_all x0 -> x2, blocking collectives: none -> 36.4 us  [the longest x1 18.6 us: shards(): lax.all_to_all(sums, ('x', 'zh', 'core'), split_axis=0, concat_axis=0, ti...]
    ppermute x6 -> x5, waiting for transfers between devices: 40.7 us -> 4.92 us  [swap(): return lax.ppermute(a, axis, [(0, 1), (1, 0)])]
    ppermute x24 -> x10, waiting for transfers between devices: 40.7 us -> 22.1 us  [shift_from(): return lax.ppermute(a, axis, [(i, (i - s) % 4) for i in range(4)])]
    ppermute x2, waiting for transfers between devices: 0.01 us -> 13.7 us  [shards(): got.append(lax.ppermute(part[a], ('x', 'zh', 'core'), perm))]
    ppermute x24 -> x10, starting transfers between devices: 28.1 us -> 15.3 us  [shift_from(): return lax.ppermute(a, axis, [(i, (i - s) % 4) for i in range(4)])]
    ppermute x6 -> x5, starting transfers between devices: 16.5 us -> 5.65 us  [swap(): return lax.ppermute(a, axis, [(0, 1), (1, 0)])]
    ppermute x6 -> x3, starting transfers between devices: 11 us -> 4.19 us  [shift_to(): return lax.ppermute(a, axis, [(i, (i + s) % 4) for i in range(4)])]
    ppermute x2, starting transfers between devices: 11.7 us -> 8.53 us  [shards(): got.append(lax.ppermute(part[a], ('x', 'zh', 'core'), perm))]
  transfers between devices with their start and end apart: 38 -> 21, of which waited for: 14 -> 11; matrix products, arithmetic and copies ran while one was open for 2% -> 2% of each run, Pallas kernels for 4% -> 4%
where the time goes in v2:
time: 167 us
  waiting for transfers between devices  51.1 us (31%)
  blocking collectives  36.4 us (22%)
  starting transfers between devices  33.7 us (20%)
  Pallas kernels  23 us (14%)
  between operations  13.6 us (8%)
  local copies, waits for them, and re-layouts  6.11 us (4%)
  other arithmetic  2.64 us (2%)
    ppermute x10, waiting for transfers between devices, shift_from(): return lax.ppermute(a, axis, [(i, (i - s) % 4) for i in range(4)])  22.1 us
    all_to_all x1, blocking collectives, shards(): lax.all_to_all(sums, ('x', 'zh', 'core'), split_axis=0, concat_axis=0, ti...  18.6 us
    all_to_all x1, blocking collectives, shards(): lax.all_to_all(jnp.broadcast_to(own, (32, 8, 192)), ('x', 'zl', 'y'), spl...  17.8 us
    ppermute x10, starting transfers between devices, shift_from(): return lax.ppermute(a, axis, [(i, (i - s) % 4) for i in range(4)])  15.3 us
    ppermute x2, waiting for transfers between devices, shards(): got.append(lax.ppermute(part[a], ('x', 'zh', 'core'), perm))  13.7 us
    ppermute x3, waiting for transfers between devices, shift_to(): return lax.ppermute(a, axis, [(i, (i + s) % 4) for i in range(4)])  10.3 us
    pallas_call x1, Pallas kernels, make_z(): pl.pallas_call(z_kernel, in_specs=[SMEM] + [ANY] * 9, out_specs=[VMEM, VM...  9.68 us
    ppermute x2, starting transfers between devices, shards(): got.append(lax.ppermute(part[a], ('x', 'zh', 'core'), perm))  8.53 us
  transfers between devices with their start and end apart: 21, of which 11 were waited for; matrix products, arithmetic and copies ran while one was open for 2% of the time, Pallas kernels for 4%

profile of v2, /device:TPU:1, one launch (start us, length us, event | category | flops | bytes accessed | tf_op | source)
XLA Modules:
  0.0 166.6 jit_solution(11701460806024708678)
XLA Ops:
  6.5 1.9 %copy.10 = bf16[24,8,1280]{2,1,0:T(8,128)(2,1)} copy(bf16[24,8,1280]{2,0,1:T(8,128)(2,1)} %bitcast.32) | data formatting | bytes 983040 | tf_op jit(solution)/shard_map/transpose | solution.py:190
  8.5 3.8 %collective-permute-start.3 = (bf16[160,1280]{1,0:T(8,128)(2,1)}, bf16[160,1280]{1,0:T(8,128)(2,1)S(1)}, u32[]{:S(2)}, u32[]{:S(2)}) collective-permute-start(bf16[160,1280]{1,0:T(8,128)(2,1)} %bitcast.34), channel_id=1, source_target_pairs={{0,8},{4,12},{8,0},{12,4},{1,9},{5,13},{9,1},{13,5},{2,10},{6,14},... | collective-permute-start | bytes 1228808 | tf_op jit(solution)/shard_map/ppermute | solution.py:19
  12.3 0.4 collective-permute-start.2
  12.7 2.3 %collective-permute-start.1 = (bf16[160,1280]{1,0:T(8,128)(2,1)}, bf16[160,1280]{1,0:T(8,128)(2,1)S(1)}, u32[]{:S(2)}, u32[]{:S(2)}) collective-permute-start(bf16[160,1280]{1,0:T(8,128)(2,1)} %bitcast.36), channel_id=1, source_target_pairs={{0,12},{4,0},{8,4},{12,8},{1,13},{5,1},{9,5},{13,9},{2,14},{6,2},{... | collective-permute-start | bytes 1228808 | tf_op jit(solution)/shard_map/ppermute | solution.py:19
  15.0 1.6 collective-permute-start
  16.6 0.7 convert_bitcast_fusion
  17.3 0.1 copy.7
  17.4 0.1 reshape.26
  17.6 17.8 %all_to_all.10 = f32[32,8,192]{2,1,0:T(8,128)} all-to-all(f32[32,8,192]{2,1,0:T(8,128)S(1)} %broadcast_in_dim.2), channel_id=1, replica_groups=mesh['x'=4,'zl'=2,'y'=4,'zh'=2,'core'=2] {'x','zl','y'}, dimensions={0} | all-to-all | bytes 393216 | tf_op jit(solution)/shard_map/all_to_all | solution.py:197
  35.4 0.2 collective-permute-start.5
  35.6 1.5 collective-permute-start.6
  37.1 1.4 collective-permute-start.4
  38.5 0.7 stack.32.where
  39.2 7.1 %mix.1 = (bf16[6,64,1280]{2,1,0:T(8,128)(2,1)}, bf16[6,64,1280]{2,1,0:T(8,128)(2,1)}, bf16[6,64,1280]{2,1,0:T(8,128)(2,1)}, bf16[6,64,1280]{2,1,0:T(8,128)(2,1)}) custom-call(s32[5]{0:T(128)} %stack.32.where, f32[256,192]{1,0:T(8,128)} %bitcast.31, bf16[8,256,1280]{2,1,0:T(8,128)(2,1)} %b_ref.1), custom_call_target="tpu_custom_call" | custom-call | flops 1006632960 | bytes 9200000 | tf_op jit(solution)/shard_map/mix/pallas_call | solution.py:64
  46.3 0.4 collective-permute-done.6.refs_7_
  46.8 0.3 copy-done.18
  47.1 0.4 copy-done.19
  47.5 0.1 copy-done.20
  47.7 9.7 %make_z.1 = (f32[2,192,1280]{2,1,0:T(8,128)}, f32[2,192,1280]{2,1,0:T(8,128)}) custom-call(s32[5]{0:T(128)} %stack.32.where, bf16[768,1280]{1,0:T(8,128)(2,1)} %all-gather.2.cloned.1.call-done.m, bf16[160,1280]{1,0:T(8,128)(2,1)} %bitcast.38, bf16[160,1280]{1,0:T(8,128)(2,1)} %copy-done.16, bf16[160,1280]{1,0:T(8,128)(2,1)} %copy-done.14, ...), custom_call_target="tpu_custom_call" | custom-call | flops 2516582400 | bytes 9000000 | tf_op jit(solution)/shard_map/make_z/pallas_call | solution.py:117
  57.4 2.3 %collective-permute-start.7 = (f32[2,192,1280]{2,1,0:T(8,128)}, f32[2,192,1280]{2,1,0:T(8,128)S(1)}, u32[]{:S(2)}, u32[]{:S(2)}) collective-permute-start(f32[2,192,1280]{2,1,0:T(8,128)} %get-tuple-element.54), channel_id=1, source_target_pairs={{0,1},{1,0},{2,3},{3,2},{4,5},{5,4},{6,7},{7,6},{8,9},{9,8},{10,11... | collective-permute-start | bytes 5898248 | tf_op jit(solution)/shard_map/ppermute | solution.py:27
  59.7 1.2 collective-permute-start.10
  60.9 1.5 collective-permute-start.11
  62.4 1.1 collective-permute-done.7
  63.5 1.8 %add_convert_fusion = bf16[2,192,1280]{2,1,0:T(8,128)(2,1)S(1)} fusion(f32[2,192,1280]{2,1,0:T(8,128)} %get-tuple-element.53, f32[2,192,1280]{2,1,0:T(8,128)S(1)} %collective-permute-done.7), kind=kLoop, calls=%fused_computation | loop fusion | flops 983040 | bytes 4915200 | tf_op jit(solution)/shard_map/convert_element_type | solution.py:206
  65.3 2.8 %collective-permute-start.9 = (bf16[192,1280]{1,0:T(8,128)(2,1)S(1)}, bf16[192,1280]{1,0:T(8,128)(2,1)S(1)}, u32[]{:S(2)}, u32[]{:S(2)}) collective-permute-start(bf16[192,1280]{1,0:T(8,128)(2,1)S(1)} %get-tuple-element.65), channel_id=1, source_target_pairs={{0,32},{1,96},{2,0},{3,64},{32,33},{33,97},{34,1},{35,65},{64,34},... | collective-permute-start | bytes 1474568 | tf_op jit(solution)/shard_map/ppermute | solution.py:212
  68.1 5.7 %collective-permute-start.8 = (bf16[192,1280]{1,0:T(8,128)(2,1)S(1)}, bf16[192,1280]{1,0:T(8,128)(2,1)S(1)}, u32[]{:S(2)}, u32[]{:S(2)}) collective-permute-start(bf16[192,1280]{1,0:T(8,128)(2,1)S(1)} %get-tuple-element.66), channel_id=1, source_target_pairs={{0,0},{1,64},{2,32},{3,96},{32,1},{33,65},{34,33},{35,97},{64,2},{... | collective-permute-start | bytes 1474568 | tf_op jit(solution)/shard_map/ppermute | solution.py:212
  73.9 10.3 %collective-permute-done.10.refs_9_ = bf16[6,64,1280]{2,1,0:T(8,128)(2,1)S(1)} collective-permute-done((bf16[6,64,1280]{2,1,0:T(8,128)(2,1)S(1)}, bf16[6,64,1280]{2,1,0:T(8,128)(2,1)S(1)}, u32[]{:S(2)}, u32[]{:S(2)}) %collective-permute-start.10) | collective-permute-done | bytes 983072 | tf_op jit(solution)/shard_map/ppermute | solution.py:23
  84.2 13.7 %collective-permute-done.9 = bf16[192,1280]{1,0:T(8,128)(2,1)S(1)} collective-permute-done((bf16[192,1280]{1,0:T(8,128)(2,1)S(1)}, bf16[192,1280]{1,0:T(8,128)(2,1)S(1)}, u32[]{:S(2)}, u32[]{:S(2)}) %collective-permute-start.9) | collective-permute-done | bytes 491552 | tf_op jit(solution)/shard_map/ppermute | solution.py:212
  97.9 0.1 add_convert_fusion.1
  98.1 0.6 collective-permute-start.15
  98.6 0.6 collective-permute-start.14
  99.2 3.1 %collective-permute-start.13 = (bf16[6,32,1280]{2,1,0:T(8,128)(2,1)S(1)}, bf16[6,32,1280]{2,1,0:T(8,128)(2,1)S(1)}, u32[]{:S(2)}, u32[]{:S(2)}) collective-permute-start(bf16[6,32,1280]{2,1,0:T(8,128)(2,1)S(1)} %bitcast.28), channel_id=1, source_target_pairs={{0,8},{4,12},{8,0},{12,4},{1,9},{5,13},{9,1},{13,5},{2,10},{6,14},... | collective-permute-start | bytes 1474568 | tf_op jit(solution)/shard_map/ppermute | solution.py:19
  102.3 1.5 collective-permute-start.19
  103.8 0.8 collective-permute-start.12
  104.6 2.9 %collective-permute-done.15.refs_4_ = bf16[6,32,1280]{2,1,0:T(8,128)(2,1)S(1)} collective-permute-done((bf16[6,32,1280]{2,1,0:T(8,128)(2,1)S(1)}, bf16[6,32,1280]{2,1,0:T(8,128)(2,1)S(1)}, u32[]{:S(2)}, u32[]{:S(2)}) %collective-permute-start.15) | collective-permute-done | bytes 491552 | tf_op jit(solution)/shard_map/ppermute | solution.py:27
  107.6 0.6 collective-permute-start.18
  108.1 5.5 %collective-permute-done.14.refs_3_ = bf16[6,32,1280]{2,1,0:T(8,128)(2,1)S(1)} collective-permute-done((bf16[6,32,1280]{2,1,0:T(8,128)(2,1)S(1)}, bf16[6,32,1280]{2,1,0:T(8,128)(2,1)S(1)}, u32[]{:S(2)}, u32[]{:S(2)}) %collective-permute-start.14) | collective-permute-done | bytes 491552 | tf_op jit(solution)/shard_map/ppermute | solution.py:19
  113.6 0.8 collective-permute-start.16
  114.5 10.3 %collective-permute-done.13.refs_2_ = bf16[6,32,1280]{2,1,0:T(8,128)(2,1)S(1)} collective-permute-done((bf16[6,32,1280]{2,1,0:T(8,128)(2,1)S(1)}, bf16[6,32,1280]{2,1,0:T(8,128)(2,1)S(1)}, u32[]{:S(2)}, u32[]{:S(2)}) %collective-permute-start.13) | collective-permute-done | bytes 491552 | tf_op jit(solution)/shard_map/ppermute | solution.py:19
  124.8 1.0 collective-permute-start.17
  125.7 5.0 %collective-permute-done.18.refs_7_ = bf16[6,32,1280]{2,1,0:T(8,128)(2,1)S(1)} collective-permute-done((bf16[6,32,1280]{2,1,0:T(8,128)(2,1)S(1)}, bf16[6,32,1280]{2,1,0:T(8,128)(2,1)S(1)}, u32[]{:S(2)}, u32[]{:S(2)}) %collective-permute-start.18) | collective-permute-done | bytes 491552 | tf_op jit(solution)/shard_map/ppermute | solution.py:19
  130.7 0.9 collective-permute-done.16.refs_5_
  131.6 0.9 collective-permute-done.17.refs_6_
  132.5 0.7 copy-done.10
  133.2 1.0 copy-done.3
  134.2 6.2 %last.1 = f32[16,32,128]{2,1,0:T(8,128)} custom-call(s32[5]{0:T(128)} %stack.32.where, bf16[6,32,1280]{2,1,0:T(8,128)(2,1)} %bitcast.30, bf16[6,32,1280]{2,1,0:T(8,128)(2,1)} %copy-done.7, bf16[6,32,1280]{2,1,0:T(8,128)(2,1)} %copy-done.6, bf16[6,32,1280]{2,1,0:T(8,128)(2,1)} %copy-done.5, bf16[6,32,1280]{2,1,0:T(8,128)(2,1)} %copy-done.4, ...), custom_call_target="tpu_custom_call" | custom-call | flops 1006632960 | bytes 8000000 | tf_op jit(solution)/shard_map/last/pallas_call | solution.py:168
  140.4 18.6 %all_to_all.11 = f32[16,32,128]{2,1,0:T(8,128)S(1)} all-to-all(f32[16,32,128]{2,1,0:T(8,128)} %last.1), channel_id=1, replica_groups=mesh['x'=4,'zl'=2,'y'=4,'zh'=2,'core'=2] {'x','zh','core'}, dimensions={0} | all-to-all | bytes 524288 | tf_op jit(solution)/shard_map/all_to_all | solution.py:219
  159.1 0.6 copy.8
  (55 shorter events, 0.4 us)
Async XLA Ops:
  6.5 40.3 %all-gather.2.cloned.1.call-start = ((), (), s32[]{:S(2)}) async-start(), calls=%async_computation.2 | async-start | bytes 2457600 | tf_op jit(solution)/shard_map/all_gather | solution.py:191
  8.5 26.9 %collective-permute-start.3 = (bf16[160,1280]{1,0:T(8,128)(2,1)}, bf16[160,1280]{1,0:T(8,128)(2,1)S(1)}, u32[]{:S(2)}, u32[]{:S(2)}) collective-permute-start(bf16[160,1280]{1,0:T(8,128)(2,1)} %bitcast.34), channel_id=1, source_target_pairs={{0,8},{4,12},{8,0},{12,4},{1,9},{5,13},{9,1},{13,5},{2,10},{6,14},... | collective-permute-start | bytes 1228808 | tf_op jit(solution)/shard_map/ppermute | solution.py:19
  12.3 23.1 %collective-permute-start.2 = (bf16[160,1280]{1,0:T(8,128)(2,1)}, bf16[160,1280]{1,0:T(8,128)(2,1)S(1)}, u32[]{:S(2)}, u32[]{:S(2)}) collective-permute-start(bf16[160,1280]{1,0:T(8,128)(2,1)} %bitcast.35), channel_id=1, source_target_pairs={{0,4},{4,8},{8,12},{12,0},{1,5},{5,9},{9,13},{13,1},{2,6},{6,10},{... | collective-permute-start | bytes 1228808 | tf_op jit(solution)/shard_map/ppermute | solution.py:19
  12.7 22.7 %collective-permute-start.1 = (bf16[160,1280]{1,0:T(8,128)(2,1)}, bf16[160,1280]{1,0:T(8,128)(2,1)S(1)}, u32[]{:S(2)}, u32[]{:S(2)}) collective-permute-start(bf16[160,1280]{1,0:T(8,128)(2,1)} %bitcast.36), channel_id=1, source_target_pairs={{0,12},{4,0},{8,4},{12,8},{1,13},{5,1},{9,5},{13,9},{2,14},{6,2},{... | collective-permute-start | bytes 1228808 | tf_op jit(solution)/shard_map/ppermute | solution.py:19
  15.0 20.4 %collective-permute-start = (bf16[160,1280]{1,0:T(8,128)(2,1)}, bf16[160,1280]{1,0:T(8,128)(2,1)S(1)}, u32[]{:S(2)}, u32[]{:S(2)}) collective-permute-start(bf16[160,1280]{1,0:T(8,128)(2,1)} %bitcast.37), channel_id=1, source_target_pairs={{0,16},{16,0},{1,17},{17,1},{2,18},{18,2},{3,19},{19,3},{4,20},{20... | collective-permute-start | bytes 1228808 | tf_op jit(solution)/shard_map/ppermute | solution.py:27
  35.4 10.9 %copy-start.14 = (bf16[160,1280]{1,0:T(8,128)(2,1)}, bf16[160,1280]{1,0:T(8,128)(2,1)S(1)}, u32[]{:S(2)}) copy-start(bf16[160,1280]{1,0:T(8,128)(2,1)S(1)} %collective-permute-done.3.refs_2_) | copy-start | bytes 1228804
  35.4 10.9 %copy-start.15 = (bf16[160,1280]{1,0:T(8,128)(2,1)}, bf16[160,1280]{1,0:T(8,128)(2,1)S(1)}, u32[]{:S(2)}) copy-start(bf16[160,1280]{1,0:T(8,128)(2,1)S(1)} %collective-permute-done.2.refs_3_) | copy-start | bytes 1228804
  35.4 10.9 %copy-start.16 = (bf16[160,1280]{1,0:T(8,128)(2,1)}, bf16[160,1280]{1,0:T(8,128)(2,1)S(1)}, u32[]{:S(2)}) copy-start(bf16[160,1280]{1,0:T(8,128)(2,1)S(1)} %collective-permute-done.1.refs_1_) | copy-start | bytes 1228804
  35.4 10.9 %copy-start.17 = (bf16[160,1280]{1,0:T(8,128)(2,1)}, bf16[160,1280]{1,0:T(8,128)(2,1)S(1)}, u32[]{:S(2)}) copy-start(bf16[160,1280]{1,0:T(8,128)(2,1)S(1)} %collective-permute-done.refs_4_) | copy-start | bytes 1228804
  35.4 10.9 %collective-permute-start.5 = (bf16[160,1280]{1,0:T(8,128)(2,1)S(1)}, bf16[160,1280]{1,0:T(8,128)(2,1)S(1)}, u32[]{:S(2)}, u32[]{:S(2)}) collective-permute-start(bf16[160,1280]{1,0:T(8,128)(2,1)S(1)} %collective-permute-done.3.refs_2_), channel_id=1, source_target_pairs={{0,16},{16,0},{1,17},{17,1},{2,18},{18,2},{3,19},{19,3},{4,20},{20... | collective-permute-start | bytes 1228808 | tf_op jit(solution)/shard_map/ppermute | solution.py:27
  35.6 11.1 %collective-permute-start.6 = (bf16[160,1280]{1,0:T(8,128)(2,1)S(1)}, bf16[160,1280]{1,0:T(8,128)(2,1)S(1)}, u32[]{:S(2)}, u32[]{:S(2)}) collective-permute-start(bf16[160,1280]{1,0:T(8,128)(2,1)S(1)} %collective-permute-done.refs_4_), channel_id=1, source_target_pairs={{0,4},{4,8},{8,12},{12,0},{1,5},{5,9},{9,13},{13,1},{2,6},{6,10},{... | collective-permute-start | bytes 1228808 | tf_op jit(solution)/shard_map/ppermute | solution.py:19
  37.1 9.7 %collective-permute-start.4 = (bf16[160,1280]{1,0:T(8,128)(2,1)S(1)}, bf16[160,1280]{1,0:T(8,128)(2,1)S(1)}, u32[]{:S(2)}, u32[]{:S(2)}) collective-permute-start(bf16[160,1280]{1,0:T(8,128)(2,1)S(1)} %collective-permute-done.refs_4_), channel_id=1, source_target_pairs={{0,12},{4,0},{8,4},{12,8},{1,13},{5,1},{9,5},{13,9},{2,14},{6,2},{... | collective-permute-start | bytes 1228808 | tf_op jit(solution)/shard_map/ppermute | solution.py:19
  46.3 0.8 copy-start.18
  46.7 0.8 copy-start.19
  46.8 0.8 copy-start.20
  47.7 12.0 %copy-start.13 = (bf16[6,64,1280]{2,1,0:T(8,128)(2,1)S(1)}, bf16[6,64,1280]{2,1,0:T(8,128)(2,1)}, u32[]{:S(2)}) copy-start(bf16[6,64,1280]{2,1,0:T(8,128)(2,1)} %get-tuple-element.56) | copy-start | bytes 2949124
  47.7 13.2 %copy-start.12 = (bf16[6,64,1280]{2,1,0:T(8,128)(2,1)S(1)}, bf16[6,64,1280]{2,1,0:T(8,128)(2,1)}, u32[]{:S(2)}) copy-start(bf16[6,64,1280]{2,1,0:T(8,128)(2,1)} %get-tuple-element.58) | copy-start | bytes 2949124
  57.4 6.1 %collective-permute-start.7 = (f32[2,192,1280]{2,1,0:T(8,128)}, f32[2,192,1280]{2,1,0:T(8,128)S(1)}, u32[]{:S(2)}, u32[]{:S(2)}) collective-permute-start(f32[2,192,1280]{2,1,0:T(8,128)} %get-tuple-element.54), channel_id=1, source_target_pairs={{0,1},{1,0},{2,3},{3,2},{4,5},{5,4},{6,7},{7,6},{8,9},{9,8},{10,11... | collective-permute-start | bytes 5898248 | tf_op jit(solution)/shard_map/ppermute | solution.py:27
  59.7 24.5 %collective-permute-start.10 = (bf16[6,64,1280]{2,1,0:T(8,128)(2,1)S(1)}, bf16[6,64,1280]{2,1,0:T(8,128)(2,1)S(1)}, u32[]{:S(2)}, u32[]{:S(2)}) collective-permute-start(bf16[6,64,1280]{2,1,0:T(8,128)(2,1)S(1)} %copy-done.13), channel_id=1, source_target_pairs={{0,32},{32,64},{64,96},{96,0},{1,33},{33,65},{65,97},{97,1},{2,34}... | collective-permute-start | bytes 2949128 | tf_op jit(solution)/shard_map/ppermute | solution.py:23
  60.9 23.3 %collective-permute-start.11 = (bf16[6,64,1280]{2,1,0:T(8,128)(2,1)S(1)}, bf16[6,64,1280]{2,1,0:T(8,128)(2,1)S(1)}, u32[]{:S(2)}, u32[]{:S(2)}) collective-permute-start(bf16[6,64,1280]{2,1,0:T(8,128)(2,1)S(1)} %copy-done.12), channel_id=1, source_target_pairs={{0,96},{32,0},{64,32},{96,64},{1,97},{33,1},{65,33},{97,65},{2,98}... | collective-permute-start | bytes 2949128 | tf_op jit(solution)/shard_map/ppermute | solution.py:23
  65.3 37.1 %copy-start.11 = (bf16[6,64,1280]{2,1,0:T(8,128)(2,1)S(1)}, bf16[6,64,1280]{2,1,0:T(8,128)(2,1)}, u32[]{:S(2)}) copy-start(bf16[6,64,1280]{2,1,0:T(8,128)(2,1)} %get-tuple-element.63) | copy-start | bytes 2949124
  65.3 32.6 %collective-permute-start.9 = (bf16[192,1280]{1,0:T(8,128)(2,1)S(1)}, bf16[192,1280]{1,0:T(8,128)(2,1)S(1)}, u32[]{:S(2)}, u32[]{:S(2)}) collective-permute-start(bf16[192,1280]{1,0:T(8,128)(2,1)S(1)} %get-tuple-element.65), channel_id=1, source_target_pairs={{0,32},{1,96},{2,0},{3,64},{32,33},{33,97},{34,1},{35,65},{64,34},... | collective-permute-start | bytes 1474568 | tf_op jit(solution)/shard_map/ppermute | solution.py:212
  68.1 29.8 %collective-permute-start.8 = (bf16[192,1280]{1,0:T(8,128)(2,1)S(1)}, bf16[192,1280]{1,0:T(8,128)(2,1)S(1)}, u32[]{:S(2)}, u32[]{:S(2)}) collective-permute-start(bf16[192,1280]{1,0:T(8,128)(2,1)S(1)} %get-tuple-element.66), channel_id=1, source_target_pairs={{0,0},{1,64},{2,32},{3,96},{32,1},{33,65},{34,33},{35,97},{64,2},{... | collective-permute-start | bytes 1474568 | tf_op jit(solution)/shard_map/ppermute | solution.py:212
  84.2 48.3 %copy-start.1 = (bf16[6,64,1280]{2,1,0:T(8,128)(2,1)}, bf16[6,64,1280]{2,1,0:T(8,128)(2,1)S(1)}, u32[]{:S(2)}) copy-start(bf16[6,64,1280]{2,1,0:T(8,128)(2,1)S(1)} %collective-permute-done.10.refs_9_) | copy-start | bytes 2949124
  84.2 48.3 %copy-start.2 = (bf16[6,64,1280]{2,1,0:T(8,128)(2,1)}, bf16[6,64,1280]{2,1,0:T(8,128)(2,1)S(1)}, u32[]{:S(2)}) copy-start(bf16[6,64,1280]{2,1,0:T(8,128)(2,1)S(1)} %collective-permute-done.11.refs_11_) | copy-start | bytes 2949124
  98.0 34.4 %copy-start = (bf16[192,1280]{1,0:T(8,128)(2,1)}, bf16[192,1280]{1,0:T(8,128)(2,1)S(1)}, u32[]{:S(2)}) copy-start(bf16[192,1280]{1,0:T(8,128)(2,1)S(1)} %add_convert_fusion.1) | copy-start | bytes 1474564
  98.1 9.5 %collective-permute-start.15 = (bf16[6,32,1280]{2,1,0:T(8,128)(2,1)S(1)}, bf16[6,32,1280]{2,1,0:T(8,128)(2,1)S(1)}, u32[]{:S(2)}, u32[]{:S(2)}) collective-permute-start(bf16[6,32,1280]{2,1,0:T(8,128)(2,1)S(1)} %bitcast.26), channel_id=1, source_target_pairs={{0,16},{16,0},{1,17},{17,1},{2,18},{18,2},{3,19},{19,3},{4,20},{20... | collective-permute-start | bytes 1474568 | tf_op jit(solution)/shard_map/ppermute | solution.py:27
  98.6 15.0 %collective-permute-start.14 = (bf16[6,32,1280]{2,1,0:T(8,128)(2,1)S(1)}, bf16[6,32,1280]{2,1,0:T(8,128)(2,1)S(1)}, u32[]{:S(2)}, u32[]{:S(2)}) collective-permute-start(bf16[6,32,1280]{2,1,0:T(8,128)(2,1)S(1)} %bitcast.27), channel_id=1, source_target_pairs={{0,4},{4,8},{8,12},{12,0},{1,5},{5,9},{9,13},{13,1},{2,6},{6,10},{... | collective-permute-start | bytes 1474568 | tf_op jit(solution)/shard_map/ppermute | solution.py:19
  99.2 25.5 %collective-permute-start.13 = (bf16[6,32,1280]{2,1,0:T(8,128)(2,1)S(1)}, bf16[6,32,1280]{2,1,0:T(8,128)(2,1)S(1)}, u32[]{:S(2)}, u32[]{:S(2)}) collective-permute-start(bf16[6,32,1280]{2,1,0:T(8,128)(2,1)S(1)} %bitcast.28), channel_id=1, source_target_pairs={{0,8},{4,12},{8,0},{12,4},{1,9},{5,13},{9,1},{13,5},{2,10},{6,14},... | collective-permute-start | bytes 1474568 | tf_op jit(solution)/shard_map/ppermute | solution.py:19
  102.3 30.1 %collective-permute-start.19 = (bf16[6,64,1280]{2,1,0:T(8,128)(2,1)S(1)}, bf16[6,64,1280]{2,1,0:T(8,128)(2,1)S(1)}, u32[]{:S(2)}, u32[]{:S(2)}) collective-permute-start(bf16[6,64,1280]{2,1,0:T(8,128)(2,1)S(1)} %copy-done.11), channel_id=1, source_target_pairs={{0,64},{32,96},{64,0},{96,32},{1,65},{33,97},{65,1},{97,33},{2,66}... | collective-permute-start | bytes 2949128 | tf_op jit(solution)/shard_map/ppermute | solution.py:23
  103.8 21.9 %collective-permute-start.12 = (bf16[6,32,1280]{2,1,0:T(8,128)(2,1)S(1)}, bf16[6,32,1280]{2,1,0:T(8,128)(2,1)S(1)}, u32[]{:S(2)}, u32[]{:S(2)}) collective-permute-start(bf16[6,32,1280]{2,1,0:T(8,128)(2,1)S(1)} %bitcast.29), channel_id=1, source_target_pairs={{0,12},{4,0},{8,4},{12,8},{1,13},{5,1},{9,5},{13,9},{2,14},{6,2},{... | collective-permute-start | bytes 1474568 | tf_op jit(solution)/shard_map/ppermute | solution.py:19
  107.6 24.9 %copy-start.4 = (bf16[6,32,1280]{2,1,0:T(8,128)(2,1)}, bf16[6,32,1280]{2,1,0:T(8,128)(2,1)S(1)}, u32[]{:S(2)}) copy-start(bf16[6,32,1280]{2,1,0:T(8,128)(2,1)S(1)} %collective-permute-done.15.refs_4_) | copy-start | bytes 1474564
  107.6 23.1 %collective-permute-start.18 = (bf16[6,32,1280]{2,1,0:T(8,128)(2,1)S(1)}, bf16[6,32,1280]{2,1,0:T(8,128)(2,1)S(1)}, u32[]{:S(2)}, u32[]{:S(2)}) collective-permute-start(bf16[6,32,1280]{2,1,0:T(8,128)(2,1)S(1)} %collective-permute-done.15.refs_4_), channel_id=1, source_target_pairs={{0,4},{4,8},{8,12},{12,0},{1,5},{5,9},{9,13},{13,1},{2,6},{6,10},{... | collective-permute-start | bytes 1474568 | tf_op jit(solution)/shard_map/ppermute | solution.py:19
  113.6 18.9 %copy-start.5 = (bf16[6,32,1280]{2,1,0:T(8,128)(2,1)}, bf16[6,32,1280]{2,1,0:T(8,128)(2,1)S(1)}, u32[]{:S(2)}) copy-start(bf16[6,32,1280]{2,1,0:T(8,128)(2,1)S(1)} %collective-permute-done.14.refs_3_) | copy-start | bytes 1474564
  113.6 18.0 %collective-permute-start.16 = (bf16[6,32,1280]{2,1,0:T(8,128)(2,1)S(1)}, bf16[6,32,1280]{2,1,0:T(8,128)(2,1)S(1)}, u32[]{:S(2)}, u32[]{:S(2)}) collective-permute-start(bf16[6,32,1280]{2,1,0:T(8,128)(2,1)S(1)} %collective-permute-done.15.refs_4_), channel_id=1, source_target_pairs={{0,12},{4,0},{8,4},{12,8},{1,13},{5,1},{9,5},{13,9},{2,14},{6,2},{... | collective-permute-start | bytes 1474568 | tf_op jit(solution)/shard_map/ppermute | solution.py:19
  124.8 7.7 %copy-start.6 = (bf16[6,32,1280]{2,1,0:T(8,128)(2,1)}, bf16[6,32,1280]{2,1,0:T(8,128)(2,1)S(1)}, u32[]{:S(2)}) copy-start(bf16[6,32,1280]{2,1,0:T(8,128)(2,1)S(1)} %collective-permute-done.13.refs_2_) | copy-start | bytes 1474564
  124.8 7.7 %collective-permute-start.17 = (bf16[6,32,1280]{2,1,0:T(8,128)(2,1)S(1)}, bf16[6,32,1280]{2,1,0:T(8,128)(2,1)S(1)}, u32[]{:S(2)}, u32[]{:S(2)}) collective-permute-start(bf16[6,32,1280]{2,1,0:T(8,128)(2,1)S(1)} %collective-permute-done.13.refs_2_), channel_id=1, source_target_pairs={{0,16},{16,0},{1,17},{17,1},{2,18},{18,2},{3,19},{19,3},{4,20},{20... | collective-permute-start | bytes 1474568 | tf_op jit(solution)/shard_map/ppermute | solution.py:27
  125.7 6.8 %copy-start.7 = (bf16[6,32,1280]{2,1,0:T(8,128)(2,1)}, bf16[6,32,1280]{2,1,0:T(8,128)(2,1)S(1)}, u32[]{:S(2)}) copy-start(bf16[6,32,1280]{2,1,0:T(8,128)(2,1)S(1)} %collective-permute-done.12.refs_1_) | copy-start | bytes 1474564
  130.7 1.8 %copy-start.8 = (bf16[6,32,1280]{2,1,0:T(8,128)(2,1)}, bf16[6,32,1280]{2,1,0:T(8,128)(2,1)S(1)}, u32[]{:S(2)}) copy-start(bf16[6,32,1280]{2,1,0:T(8,128)(2,1)S(1)} %collective-permute-done.18.refs_7_) | copy-start | bytes 1474564
  131.6 0.9 copy-start.9
  132.4 0.8 copy-start.10
  133.2 1.0 copy-start.3
Sparse Core Ops, SparseCore 0:
  9.0 35.4 all-gather.1

commit v3 on v2

v3 whole, which is shorter than its diff:
```python
import jax
import jax.numpy as jnp
from jax import lax
from jax.experimental import pallas as pl
from jax.experimental.pallas import tpu as pltpu
from jax.sharding import Mesh, PartitionSpec as P

F32, BF16 = jnp.float32, jnp.bfloat16
ANY = pl.BlockSpec(memory_space=pl.ANY)
SMEM = pl.BlockSpec(memory_space=pltpu.SMEM)
VMEM = pl.BlockSpec(memory_space=pltpu.VMEM)
VMEM_LIMIT = 60 * 1024 * 1024

NX, NY = 4, 4
NT = (((1,), (1,)), ((), ()))


def shift_from(a, axis, s):
    return lax.ppermute(a, axis, [(i, (i - s) % 4) for i in range(4)])


def shift_to(a, axis, s):
    return lax.ppermute(a, axis, [(i, (i + s) % 4) for i in range(4)])


def swap(a, axis):
    return lax.ppermute(a, axis, [(0, 1), (1, 0)])


def end_gather(own, other, two):
    pair = jnp.stack([own, other])
    return [own, other, two, swap(two, "zl"), shift_from(pair, "y", 1), shift_from(pair, "y", 3)]


def blocks_of(refs):
    own, other, two, other_two, one, three = refs
    return [own, one.at[0], two, three.at[0], other, one.at[1], other_two, three.at[1]]


def mixed_kernel(where, x_ref, b_ref, *refs):
    outs, xs, rows = refs[:6], refs[6], refs[7]

    @pl.when(pl.program_id(0) == 0)
    def _():
        x = where[0]
        rows[...] = x_ref[...].astype(F32).T
        for j in range(4):
            q = (x + j) % 4
            xs[j * 48 : j * 48 + 48, :] = rows[pl.ds(pl.multiple_of(q * 48, 48), 48), :].astype(BF16)

    lhs = xs[...]
    for n in range(b_ref.shape[2] // 256):
        cols = slice(256 * n, 256 * n + 256)
        two = [jnp.dot(lhs, b_ref[i, :, cols], preferred_element_type=F32) for i in range(2)]
        for j in range(4):
            for w in range(6):
                at = (j * 6 + w) * 8
                both = jnp.concatenate([t[at : at + 8] for t in two], axis=0)
                if j % 2:
                    outs[j + 1 + w // 3][w % 3, :, cols] = both.astype(BF16)
                else:
                    outs[j // 2][w, :, cols] = both.astype(BF16)


def mix(where, x_all, cond):
    g = cond.shape[2]
    return pl.pallas_call(
        mixed_kernel,
        grid=(4,),
        in_specs=[
            SMEM,
            pl.BlockSpec((256, 192), lambda i: (0, 0)),
            pl.BlockSpec((2, 256, g), lambda i: (i, 0, 0)),
        ],
        out_specs=[pl.BlockSpec((6, 16, g), lambda i: (0, i, 0))] * 2
        + [pl.BlockSpec((3, 16, g), lambda i: (0, i, 0))] * 4,
        out_shape=[jax.ShapeDtypeStruct((6, 64, g), BF16)] * 2 + [jax.ShapeDtypeStruct((3, 64, g), BF16)] * 4,
        scratch_shapes=[pltpu.VMEM((192, 256), BF16), pltpu.VMEM((192, 256), F32)],
        compiler_params=pltpu.CompilerParams(vmem_limit_bytes=VMEM_LIMIT),
        cost_estimate=pl.CostEstimate(flops=2 * 192 * 256 * 8 * g, bytes_accessed=9200000, transcendentals=0),
        name="mix",
    )(where, x_all, cond)


def z_kernel(where, m, *refs):
    w = blocks_of(refs[0:6])
    send, keep, ms, ws, sums, m_sem, w_sem, out_sem = refs[6:]
    zl, y, zh, core = where[1], where[2], where[3], where[4]
    copies = []
    for t in range(4):
        owner = 1 - core if t < 2 else core
        q = 2 * owner + (zh + t % 2) % 2
        for r in range(4):
            to = ms.at[pl.ds((t * 4 + r) * 48, 48)]
            at = pl.ds(pl.multiple_of(192 * r + q * 48, 48), 48)
            copies.append(pltpu.make_async_copy(m.at[at], to, m_sem.at[t * 4 + r]))
    for c in copies:
        c.start()
    for at in range(8):
        to = (zl + at // 4) % 2 * 4 + (y + at % 4) % 4
        pltpu.make_async_copy(w[at], ws.at[pl.ds(pl.multiple_of(to * 160, 160), 160)], w_sem.at[to]).start()
    for c in copies:
        c.wait()

    for i in range(8):
        pltpu.make_async_copy(w[0], ws.at[pl.ds(i * 160, 160)], w_sem.at[i]).wait()
    outs = []
    for half, out in enumerate((send, keep)):
        res = lax.dot_general(ms[384 * half : 384 * half + 384, :], ws[...], NT, preferred_element_type=F32)
        for a in range(2):
            t = 2 * half + a
            for k in range(6):
                for r in range(4):
                    at = ((a * 4 + r) * 6 + k) * 8
                    sums[t, (k * 4 + r) * 8 : (k * 4 + r) * 8 + 8, :] = res[at : at + 8]
            outs.append(pltpu.make_async_copy(sums.at[t], out.at[a], out_sem.at[t]))
            outs[-1].start()
    for c in outs:
        c.wait()


def make_z(where, m, w):
    g = m.shape[1]
    shape = jax.ShapeDtypeStruct((2, 192, g), F32)
    return pl.pallas_call(
        z_kernel,
        in_specs=[SMEM] + [ANY] * 7,
        out_specs=[ANY, ANY],
        out_shape=[shape, shape],
        scratch_shapes=[
            pltpu.VMEM((768, g), BF16),
            pltpu.VMEM((g, g), BF16),
            pltpu.VMEM((4, 192, g), F32),
            pltpu.SemaphoreType.DMA((16,)),
            pltpu.SemaphoreType.DMA((8,)),
            pltpu.SemaphoreType.DMA((4,)),
        ],
        compiler_params=pltpu.CompilerParams(vmem_limit_bytes=VMEM_LIMIT),
        cost_estimate=pl.CostEstimate(flops=2 * 768 * g * g, bytes_accessed=40000000, transcendentals=0),
        name="make_z",
    )(where, m, *w)


def last_kernel(where, *refs):
    z, mx = blocks_of(refs[0:6]), refs[6:12]
    out, zs, xs, total, sem = refs[12:]
    x, zl, y = where[0], where[1], where[2]
    thirds = [[], [], []]
    for third in range(3):
        part = pl.ds(2 * third, 2)
        for at in range(8):
            thirds[third].append(pltpu.make_async_copy(z[at].at[part], zs.at[part, at], sem.at[third, at]))
        for j in (0, 2):
            to = xs.at[part, (x + 4 - j) % 4]
            thirds[third].append(pltpu.make_async_copy(mx[j // 2].at[part], to, sem.at[third, 8 + j]))
        for j in (1, 3):
            to = (x + 4 - j) % 4
            for w in range(2 * third, 2 * third + 2):
                own = mx[j + 1 + w // 3].at[w % 3]
                thirds[third].append(pltpu.make_async_copy(own, xs.at[w, to], sem.at[third, 8 + j + 4 * (w % 2)]))
        for c in thirds[third]:
            c.start()
    sums = jnp.zeros((256, 256), F32)
    for third in range(3):
        for c in thirds[third]:
            c.wait()
        for w in range(2 * third, 2 * third + 2):
            lhs = zs[w].reshape(256, zs.shape[3])
            rhs = xs[w].reshape(256, xs.shape[3])
            sums = sums + lax.dot_general(lhs, rhs, NT, preferred_element_type=F32)
    for z_of in range(2):
        for y_of in range(4):
            to = ((zl + z_of) % 2 * 4 + (y + y_of) % 4) * 8
            for r in range(4):
                at = ((z_of * 4 + y_of) * 4 + r) * 8
                total[pl.ds(pl.multiple_of(r * 64 + to, 8), 8), :] = sums[at : at + 8]
    turned = total[...].T
    for j in range(4):
        for p in range(4):
            cols = slice(64 * p, 64 * p + 64)
            halves = [turned[64 * j + at : 64 * j + at + 32, cols] for at in (0, 32)]
            out[4 * j + p] = jnp.concatenate(halves, axis=1)


def last(where, z, mixed):
    g = mixed[0].shape[2]
    return pl.pallas_call(
        last_kernel,
        in_specs=[SMEM] + [ANY] * 12,
        out_specs=VMEM,
        out_shape=jax.ShapeDtypeStruct((16, 32, 128), F32),
        scratch_shapes=[
            pltpu.VMEM((6, 8, 32, g), BF16),
            pltpu.VMEM((6, 4, 64, g), BF16),
            pltpu.VMEM((256, 256), F32),
            pltpu.SemaphoreType.DMA((3, 16)),
        ],
        compiler_params=pltpu.CompilerParams(vmem_limit_bytes=VMEM_LIMIT),
        cost_estimate=pl.CostEstimate(flops=2 * 256 * 256 * 6 * g, bytes_accessed=8000000, transcendentals=0),
        name="last",
    )(where, *z, *mixed)


def shards(cond_pairs, vectors, screened, val_pairs):
    g = cond_pairs.shape[2]
    axes = ("x", "zl", "y", "zh", "core")
    where = jnp.stack([lax.axis_index(a) for a in axes]).astype(jnp.int32)

    m_own = jnp.transpose(val_pairs, (1, 0, 2)).reshape(192, g)
    m = lax.all_gather(m_own, "x", axis=0, tiled=True)

    w_own = screened.T
    other, two = swap(w_own, "zl"), shift_from(w_own, "y", 2)

    own = jnp.transpose(vectors, (2, 1, 0)).reshape(1, 8, 192)
    line = lax.all_to_all(jnp.broadcast_to(own, (4, 8, 192)), "y", split_axis=0, concat_axis=0, tiled=True)
    other, two, line = lax.optimization_barrier((other, two, line))
    w = end_gather(w_own, other, two)
    lines = jnp.broadcast_to(line.reshape(1, 32, 192), (8, 32, 192))
    x_all = lax.all_to_all(lines, ("x", "zl"), split_axis=0, concat_axis=0, tiled=True).reshape(256, 192)

    mixed = mix(where, x_all, cond_pairs)
    mixed = list(mixed)
    m, w, mixed[0] = lax.optimization_barrier((m, w, mixed[0]))
    mixed[2], mixed[4] = shift_to(mixed[2], "x", 1), shift_to(mixed[4], "x", 3)

    send, keep = make_z(where, m, w)
    send, keep, mixed = lax.optimization_barrier((send, keep, mixed))
    part = (keep + swap(send, "core")).astype(BF16)
    got = []
    for a in range(2):
        perm = [
            (x * 4 + zh * 2 + c, (2 * c + (zh ^ a)) * 4 + x) for x in range(4) for zh in range(2) for c in range(2)
        ]
        got.append(lax.ppermute(part[a], ("x", "zh", "core"), perm))
    got, mixed = lax.optimization_barrier((got, mixed))
    z_own = (got[0].astype(F32) + got[1].astype(F32)).astype(BF16).reshape(6, 32, g)
    other, two = swap(z_own, "zl"), shift_from(z_own, "y", 2)
    mixed[3], mixed[5] = shift_to(mixed[3], "x", 1), shift_to(mixed[5], "x", 3)
    z_own, other, two, mixed = lax.optimization_barrier((z_own, other, two, mixed))
    z = end_gather(z_own, other, two)
    mixed[1] = shift_to(mixed[1], "x", 2)

    sums = last(where, z, mixed)
    sums = lax.all_to_all(sums, ("x", "zh", "core"), split_axis=0, concat_axis=0, tiled=True)
    total = jnp.sum(sums, axis=0)
    total = jnp.stack([total[:, :64], total[:, 64:]])
    return jnp.transpose(total.reshape(8, 8, 64), (1, 2, 0))


def solution(mesh):
    fine = Mesh(mesh.devices.reshape(4, 2, 4, 2, 2), ("x", "zl", "y", "zh", "core"))
    band, pw = ("x", "zl", "y"), ("zh", "core")
    return jax.shard_map(
        shards,
        mesh=fine,
        in_specs=(P(band, None, pw), P(None, None, band), P(pw, band), P(band, None, pw)),
        out_specs=P(None, pw, band),
        check_vma=False,
    )
```

time: 167 us -> 164 us (0.982)
  blocking collectives: 36.4 us -> 27.3 us
  starting transfers between devices: 33.7 us -> 39.3 us
  Pallas kernels: 23 us -> 19.6 us
  local copies, waits for them, and re-layouts: 6.11 us -> 8.21 us
    ppermute x5, waiting for transfers between devices: 4.92 us -> 18.1 us  [swap(): return lax.ppermute(a, axis, [(0, 1), (1, 0)])]
    all_to_all x1, blocking collectives: 17.8 us -> 7.03 us  [shards(): lax.all_to_all(jnp.broadcast_to(own, (4, 8, 192)), 'y', split_axis=0, con...]
    ppermute x2, waiting for transfers between devices: 13.7 us -> 7.87 us  [shards(): got.append(lax.ppermute(part[a], ('x', 'zh', 'core'), perm))]
    ppermute x3 -> x5, waiting for transfers between devices: 10.3 us -> 4.49 us  [shift_to(): return lax.ppermute(a, axis, [(i, (i + s) % 4) for i in range(4)])]
    all_to_all x0 -> x1, starting transfers between devices: none -> 4.95 us  [shards(): lax.all_to_all(lines, ('x', 'zl'), split_axis=0, concat_axis=0, tiled=True)]
    ppermute x10 -> x6, waiting for transfers between devices: 22.1 us -> 17.2 us  [shift_from(): return lax.ppermute(a, axis, [(i, (i - s) % 4) for i in range(4)])]
    ppermute x10 -> x6, starting transfers between devices: 15.3 us -> 10.4 us  [shift_from(): return lax.ppermute(a, axis, [(i, (i - s) % 4) for i in range(4)])]
    all_to_all x0 -> x1, waiting for transfers between devices: none -> 4.13 us  [shards(): lax.all_to_all(lines, ('x', 'zl'), split_axis=0, concat_axis=0, tiled=True)]
  transfers between devices with their start and end apart: 21 -> 20, of which waited for: 11 -> 11; matrix products, arithmetic and copies ran while one was open for 2% -> 2% of each run, Pallas kernels for 4% -> 8%
where the time goes in v3:
time: 164 us; the launch traced here: 163 us
  waiting for transfers between devices  51.8 us (32%)
  starting transfers between devices  39.3 us (24%)
  blocking collectives  27.3 us (17%)
  Pallas kernels  19.6 us (12%)
  between operations  13.6 us (8%)
  local copies, waits for them, and re-layouts  8.21 us (5%)
  other arithmetic  3.25 us (2%)
    all_to_all x1, blocking collectives, shards(): lax.all_to_all(sums, ('x', 'zh', 'core'), split_axis=0, concat_axis=0, ti...  20.3 us
    ppermute x5, waiting for transfers between devices, swap(): return lax.ppermute(a, axis, [(0, 1), (1, 0)])  18.1 us
    ppermute x6, waiting for transfers between devices, shift_from(): return lax.ppermute(a, axis, [(i, (i - s) % 4) for i in range(4)])  17.2 us
    ppermute x6, starting transfers between devices, shift_from(): return lax.ppermute(a, axis, [(i, (i - s) % 4) for i in range(4)])  10.4 us
    ppermute x5, starting transfers between devices, swap(): return lax.ppermute(a, axis, [(0, 1), (1, 0)])  9.6 us
    ppermute x2, waiting for transfers between devices, shards(): got.append(lax.ppermute(part[a], ('x', 'zh', 'core'), perm))  7.87 us
    ppermute x5, starting transfers between devices, shift_to(): return lax.ppermute(a, axis, [(i, (i + s) % 4) for i in range(4)])  7.71 us
    pallas_call x1, Pallas kernels, make_z(): pl.pallas_call(z_kernel, in_specs=[SMEM] + [ANY] * 7, out_specs=[ANY, ANY...  7.56 us
  transfers between devices with their start and end apart: 20, of which 11 were waited for; matrix products, arithmetic and copies ran while one was open for 2% of the time, Pallas kernels for 8%

profile of v3, /device:TPU:1, one launch (start us, length us, event | category | flops | bytes accessed | tf_op | source)
XLA Modules:
  0.0 163.2 jit_solution(13560316527827894349)
XLA Ops:
  6.5 1.9 %copy.10 = bf16[24,8,1280]{2,1,0:T(8,128)(2,1)} copy(bf16[24,8,1280]{2,0,1:T(8,128)(2,1)} %bitcast.37) | data formatting | bytes 983040 | tf_op jit(solution)/shard_map/transpose | solution.py:209
  8.5 3.8 %collective-permute-start.1 = (bf16[160,1280]{1,0:T(8,128)(2,1)}, bf16[160,1280]{1,0:T(8,128)(2,1)S(1)}, u32[]{:S(2)}, u32[]{:S(2)}) collective-permute-start(bf16[160,1280]{1,0:T(8,128)(2,1)} %bitcast.38), channel_id=1, source_target_pairs={{0,8},{4,12},{8,0},{12,4},{1,9},{5,13},{9,1},{13,5},{2,10},{6,14},... | collective-permute-start | bytes 1228808 | tf_op jit(solution)/shard_map/ppermute | solution.py:19
  12.3 1.6 %collective-permute-start = (bf16[160,1280]{1,0:T(8,128)(2,1)}, bf16[160,1280]{1,0:T(8,128)(2,1)S(1)}, u32[]{:S(2)}, u32[]{:S(2)}) collective-permute-start(bf16[160,1280]{1,0:T(8,128)(2,1)} %bitcast.39), channel_id=1, source_target_pairs={{0,16},{16,0},{1,17},{17,1},{2,18},{18,2},{3,19},{19,3},{4,20},{20... | collective-permute-start | bytes 1228808 | tf_op jit(solution)/shard_map/ppermute | solution.py:27
  13.9 0.8 copy.7
  14.7 0.1 broadcast_in_dim.14
  14.9 7.0 %all_to_all.15 = bf16[4,8,192]{2,1,0:T(8,128)(2,1)S(1)} all-to-all(bf16[4,8,192]{2,1,0:T(8,128)(2,1)S(1)} %broadcast_in_dim.15), channel_id=1, replica_groups=mesh['x'=4,'zl'=2,'y'=4,'zh'=2,'core'=2] {'y'}, dimensions={0} | all-to-all | bytes 24576 | tf_op jit(solution)/shard_map/all_to_all | solution.py:216
  21.9 1.1 collective-permute-done.refs_1_
  23.0 1.2 pad_maximum_fusion.1
  24.2 0.5 collective-permute-start.4
  24.7 2.3 %collective-permute-start.3 = (bf16[2,160,1280]{2,1,0:T(8,128)(2,1)S(1)}, bf16[2,160,1280]{2,1,0:T(8,128)(2,1)}, u32[]{:S(2)}, u32[]{:S(2)}) collective-permute-start(bf16[2,160,1280]{2,1,0:T(8,128)(2,1)S(1)} %pad_maximum_fusion.1), channel_id=1, source_target_pairs={{0,12},{4,0},{8,4},{12,8},{1,13},{5,1},{9,5},{13,9},{2,14},{6,2},{... | collective-permute-start | bytes 2457608 | tf_op jit(solution)/shard_map/ppermute | solution.py:19
  26.9 0.7 broadcast_in_dim.17
  27.6 4.9 %all-to-all-start.1 = ((bf16[8,32,192]{2,1,0:T(8,128)(2,1)}), bf16[8,32,192]{2,1,0:T(8,128)(2,1)S(1)}, u32[]{:S(2)}, u32[]{:S(2)}) async-start(bf16[8,32,192]{2,1,0:T(8,128)(2,1)} %broadcast_in_dim.17), calls=%async_computation.1 | async-start | bytes 262144 | tf_op jit(solution)/shard_map/all_to_all | solution.py:220
  32.6 1.5 collective-permute-start.2
  34.0 0.7 stack.50.where
  34.7 4.1 %all-to-all-done.1 = bf16[8,32,192]{2,1,0:T(8,128)(2,1)S(1)} async-done(((bf16[8,32,192]{2,1,0:T(8,128)(2,1)}), bf16[8,32,192]{2,1,0:T(8,128)(2,1)S(1)}, u32[]{:S(2)}, u32[]{:S(2)}) %all-to-all-start.1) | async-done | bytes 98336 | tf_op jit(solution)/shard_map/all_to_all | solution.py:220
  38.8 0.6 copy-done.5
  39.5 5.8 %mix.1 = (bf16[6,64,1280]{2,1,0:T(8,128)(2,1)}, bf16[6,64,1280]{2,1,0:T(8,128)(2,1)}, bf16[3,64,1280]{2,1,0:T(8,128)(2,1)}, bf16[3,64,1280]{2,1,0:T(8,128)(2,1)}...) custom-call(s32[5]{0:T(128)} %stack.50.where, bf16[256,192]{1,0:T(8,128)(2,1)} %bitcast.36, ...), custom_call_target="tpu_custom_call" | custom-call | flops 1006632960 | bytes 9200000 | tf_op jit(solution)/shard_map/mix/pallas_call | solution.py:67
  45.3 0.6 collective-permute-start.5
  45.9 2.1 %collective-permute-start.6 = (bf16[3,64,1280]{2,1,0:T(8,128)(2,1)}, bf16[3,64,1280]{2,1,0:T(8,128)(2,1)S(1)}, u32[]{:S(2)}, u32[]{:S(2)}) collective-permute-start(bf16[3,64,1280]{2,1,0:T(8,128)(2,1)} %get-tuple-element.66), channel_id=1, source_target_pairs={{0,96},{32,0},{64,32},{96,64},{1,97},{33,1},{65,33},{97,65},{2,98}... | collective-permute-start | bytes 1474568 | tf_op jit(solution)/shard_map/ppermute | solution.py:23
  48.1 0.9 copy-done.14
  49.0 7.6 %make_z.1 = (f32[2,192,1280]{2,1,0:T(8,128)}, f32[2,192,1280]{2,1,0:T(8,128)}) custom-call(s32[5]{0:T(128)} %stack.50.where, bf16[768,1280]{1,0:T(8,128)(2,1)} %all-gather.2.cloned.1.call-done.m, bf16[160,1280]{1,0:T(8,128)(2,1)} %bitcast.41, bf16[160,1280]{1,0:T(8,128)(2,1)} %copy-done.12, bf16[160,1280]{1,0:T(8,128)(2,1)} %copy-done.17, ...), custom_call_target="tpu_custom_call" | custom-call | flops 2516582400 | bytes 40000000 | tf_op jit(solution)/shard_map/make_z/pallas_call | solution.py:125
  56.6 4.4 %collective-permute-start.7 = (f32[2,192,1280]{2,1,0:T(8,128)}, f32[2,192,1280]{2,1,0:T(8,128)S(1)}, u32[]{:S(2)}, u32[]{:S(2)}) collective-permute-start(f32[2,192,1280]{2,1,0:T(8,128)} %get-tuple-element.69), channel_id=1, source_target_pairs={{0,1},{1,0},{2,3},{3,2},{4,5},{5,4},{6,7},{7,6},{8,9},{9,8},{10,11... | collective-permute-start | bytes 5898248 | tf_op jit(solution)/shard_map/ppermute | solution.py:27
  61.0 3.8 %collective-permute-done.7 = f32[2,192,1280]{2,1,0:T(8,128)S(1)} collective-permute-done((f32[2,192,1280]{2,1,0:T(8,128)}, f32[2,192,1280]{2,1,0:T(8,128)S(1)}, u32[]{:S(2)}, u32[]{:S(2)}) %collective-permute-start.7) | collective-permute-done | bytes 1966112 | tf_op jit(solution)/shard_map/ppermute | solution.py:27
  64.8 1.8 %add_convert_fusion = bf16[2,192,1280]{2,1,0:T(8,128)(2,1)S(1)} fusion(f32[2,192,1280]{2,1,0:T(8,128)} %get-tuple-element.68, f32[2,192,1280]{2,1,0:T(8,128)S(1)} %collective-permute-done.7), kind=kLoop, calls=%fused_computation | loop fusion | flops 983040 | bytes 4915200 | tf_op jit(solution)/shard_map/convert_element_type | solution.py:229
  66.7 2.4 %collective-permute-start.9 = (bf16[192,1280]{1,0:T(8,128)(2,1)S(1)}, bf16[192,1280]{1,0:T(8,128)(2,1)S(1)}, u32[]{:S(2)}, u32[]{:S(2)}) collective-permute-start(bf16[192,1280]{1,0:T(8,128)(2,1)S(1)} %get-tuple-element.93), channel_id=1, source_target_pairs={{0,32},{1,96},{2,0},{3,64},{32,33},{33,97},{34,1},{35,65},{64,34},... | collective-permute-start | bytes 1474568 | tf_op jit(solution)/shard_map/ppermute | solution.py:235
  69.2 4.3 %collective-permute-start.8 = (bf16[192,1280]{1,0:T(8,128)(2,1)S(1)}, bf16[192,1280]{1,0:T(8,128)(2,1)S(1)}, u32[]{:S(2)}, u32[]{:S(2)}) collective-permute-start(bf16[192,1280]{1,0:T(8,128)(2,1)S(1)} %get-tuple-element.94), channel_id=1, source_target_pairs={{0,0},{1,64},{2,32},{3,96},{32,1},{33,65},{34,33},{35,97},{64,2},{... | collective-permute-start | bytes 1474568 | tf_op jit(solution)/shard_map/ppermute | solution.py:235
  73.4 6.8 %collective-permute-done.9 = bf16[192,1280]{1,0:T(8,128)(2,1)S(1)} collective-permute-done((bf16[192,1280]{1,0:T(8,128)(2,1)S(1)}, bf16[192,1280]{1,0:T(8,128)(2,1)S(1)}, u32[]{:S(2)}, u32[]{:S(2)}) %collective-permute-start.9) | collective-permute-done | bytes 491552 | tf_op jit(solution)/shard_map/ppermute | solution.py:235
  80.2 1.1 collective-permute-done.8
  81.3 0.1 add_convert_fusion.1
  81.4 1.1 collective-permute-start.11
  82.5 1.2 collective-permute-start.10
  83.7 4.3 %collective-permute-start.12 = (bf16[3,64,1280]{2,1,0:T(8,128)(2,1)S(1)}, bf16[3,64,1280]{2,1,0:T(8,128)(2,1)S(1)}, u32[]{:S(2)}, u32[]{:S(2)}) collective-permute-start(bf16[3,64,1280]{2,1,0:T(8,128)(2,1)S(1)} %copy-done.16), channel_id=1, source_target_pairs={{0,32},{32,64},{64,96},{96,0},{1,33},{33,65},{65,97},{97,1},{2,34}... | collective-permute-start | bytes 1474568 | tf_op jit(solution)/shard_map/ppermute | solution.py:23
  88.0 6.2 %collective-permute-done.11.refs_2_ = bf16[6,32,1280]{2,1,0:T(8,128)(2,1)S(1)} collective-permute-done((bf16[6,32,1280]{2,1,0:T(8,128)(2,1)S(1)}, bf16[6,32,1280]{2,1,0:T(8,128)(2,1)S(1)}, u32[]{:S(2)}, u32[]{:S(2)}) %collective-permute-start.11) | collective-permute-done | bytes 491552 | tf_op jit(solution)/shard_map/ppermute | solution.py:19
  94.2 4.1 %collective-permute-done.10.refs_1_ = bf16[6,32,1280]{2,1,0:T(8,128)(2,1)S(1)} collective-permute-done((bf16[6,32,1280]{2,1,0:T(8,128)(2,1)S(1)}, bf16[6,32,1280]{2,1,0:T(8,128)(2,1)S(1)}, u32[]{:S(2)}, u32[]{:S(2)}) %collective-permute-start.10) | collective-permute-done | bytes 491552 | tf_op jit(solution)/shard_map/ppermute | solution.py:27
  98.3 2.2 %collective-permute-done.13.refs_11_ = bf16[3,64,1280]{2,1,0:T(8,128)(2,1)S(1)} collective-permute-done((bf16[3,64,1280]{2,1,0:T(8,128)(2,1)S(1)}, bf16[3,64,1280]{2,1,0:T(8,128)(2,1)S(1)}, u32[]{:S(2)}, u32[]{:S(2)}) %collective-permute-start.13) | collective-permute-done | bytes 491552 | tf_op jit(solution)/shard_map/ppermute | solution.py:23
  100.5 0.8 copy-done.10
  101.3 0.1 pad_maximum_fusion
  101.4 0.5 collective-permute-start.16
  101.8 2.3 %collective-permute-start.15 = (bf16[2,6,32,1280]{3,2,1,0:T(8,128)(2,1)S(1)}, bf16[2,6,32,1280]{3,2,1,0:T(8,128)(2,1)S(1)}, u32[]{:S(2)}, u32[]{:S(2)}) collective-permute-start(bf16[2,6,32,1280]{3,2,1,0:T(8,128)(2,1)S(1)} %pad_maximum_fusion), channel_id=1, source_target_pairs={{0,12},{4,0},{8,4},{12,8},{1,13},{5,1},{9,5},{13,9},{2,14},{6,2},{... | collective-permute-start | bytes 2949128 | tf_op jit(solution)/shard_map/ppermute | solution.py:19
  104.1 0.6 collective-permute-start.17
  104.7 0.9 collective-permute-start.14
  105.6 9.1 %collective-permute-done.14.refs_3_ = bf16[6,32,1280]{2,1,0:T(8,128)(2,1)S(1)} collective-permute-done((bf16[6,32,1280]{2,1,0:T(8,128)(2,1)S(1)}, bf16[6,32,1280]{2,1,0:T(8,128)(2,1)S(1)}, u32[]{:S(2)}, u32[]{:S(2)}) %collective-permute-start.14) | collective-permute-done | bytes 491552 | tf_op jit(solution)/shard_map/ppermute | solution.py:27
  114.7 11.0 %collective-permute-done.16.refs_5_ = bf16[2,6,32,1280]{3,2,1,0:T(8,128)(2,1)S(1)} collective-permute-done((bf16[2,6,32,1280]{3,2,1,0:T(8,128)(2,1)S(1)}, bf16[2,6,32,1280]{3,2,1,0:T(8,128)(2,1)S(1)}, u32[]{:S(2)}, u32[]{:S(2)}) %collective-permute-start.16) | collective-permute-done | bytes 983072 | tf_op jit(solution)/shard_map/ppermute | solution.py:19
  125.8 2.3 %collective-permute-done.17.refs_7_ = bf16[6,64,1280]{2,1,0:T(8,128)(2,1)S(1)} collective-permute-done((bf16[6,64,1280]{2,1,0:T(8,128)(2,1)S(1)}, bf16[6,64,1280]{2,1,0:T(8,128)(2,1)S(1)}, u32[]{:S(2)}, u32[]{:S(2)}) %collective-permute-start.17) | collective-permute-done | bytes 983072 | tf_op jit(solution)/shard_map/ppermute | solution.py:23
  128.1 1.0 copy-done.4
  129.1 6.2 %last.1 = f32[16,32,128]{2,1,0:T(8,128)} custom-call(s32[5]{0:T(128)} %stack.50.where, bf16[6,32,1280]{2,1,0:T(8,128)(2,1)} %bitcast.33, bf16[6,32,1280]{2,1,0:T(8,128)(2,1)} %copy-done.1, bf16[6,32,1280]{2,1,0:T(8,128)(2,1)} %copy-done.8, bf16[6,32,1280]{2,1,0:T(8,128)(2,1)} %copy-done.11, bf16[2,6,32,1280]{3,2,1,0:T(8,128)(2,1)} %copy-done.3, ...), custom_call_target="tpu_custom_call" | custom-call | flops 1006632960 | bytes 8000000 | tf_op jit(solution)/shard_map/last/pallas_call | solution.py:187
  135.3 20.3 %all_to_all.16 = f32[16,32,128]{2,1,0:T(8,128)S(1)} all-to-all(f32[16,32,128]{2,1,0:T(8,128)} %last.1), channel_id=1, replica_groups=mesh['x'=4,'zl'=2,'y'=4,'zh'=2,'core'=2] {'x','zh','core'}, dimensions={0} | all-to-all | bytes 524288 | tf_op jit(solution)/shard_map/all_to_all | solution.py:245
  155.7 0.6 copy.8
  (49 shorter events, 0.3 us)
Async XLA Ops:
  6.5 41.6 %all-gather.2.cloned.1.call-start = ((), (), s32[]{:S(2)}) async-start(), calls=%async_computation.3 | async-start | bytes 2457600 | tf_op jit(solution)/shard_map/all_gather | solution.py:210
  8.5 13.4 %collective-permute-start.1 = (bf16[160,1280]{1,0:T(8,128)(2,1)}, bf16[160,1280]{1,0:T(8,128)(2,1)S(1)}, u32[]{:S(2)}, u32[]{:S(2)}) collective-permute-start(bf16[160,1280]{1,0:T(8,128)(2,1)} %bitcast.38), channel_id=1, source_target_pairs={{0,8},{4,12},{8,0},{12,4},{1,9},{5,13},{9,1},{13,5},{2,10},{6,14},... | collective-permute-start | bytes 1228808 | tf_op jit(solution)/shard_map/ppermute | solution.py:19
  12.3 10.7 %collective-permute-start = (bf16[160,1280]{1,0:T(8,128)(2,1)}, bf16[160,1280]{1,0:T(8,128)(2,1)S(1)}, u32[]{:S(2)}, u32[]{:S(2)}) collective-permute-start(bf16[160,1280]{1,0:T(8,128)(2,1)} %bitcast.39), channel_id=1, source_target_pairs={{0,16},{16,0},{1,17},{17,1},{2,18},{18,2},{3,19},{19,3},{4,20},{20... | collective-permute-start | bytes 1228808 | tf_op jit(solution)/shard_map/ppermute | solution.py:27
  21.9 23.4 %copy-start.17 = (bf16[160,1280]{1,0:T(8,128)(2,1)}, bf16[160,1280]{1,0:T(8,128)(2,1)S(1)}, u32[]{:S(2)}) copy-start(bf16[160,1280]{1,0:T(8,128)(2,1)S(1)} %collective-permute-done.1.refs_2_) | copy-start | bytes 1228804
  23.0 22.3 %copy-start.12 = (bf16[160,1280]{1,0:T(8,128)(2,1)}, bf16[160,1280]{1,0:T(8,128)(2,1)S(1)}, u32[]{:S(2)}) copy-start(bf16[160,1280]{1,0:T(8,128)(2,1)S(1)} %collective-permute-done.refs_1_) | copy-start | bytes 1228804
  24.2 23.9 %collective-permute-start.4 = (bf16[2,160,1280]{2,1,0:T(8,128)(2,1)S(1)}, bf16[2,160,1280]{2,1,0:T(8,128)(2,1)S(1)}, u32[]{:S(2)}, u32[]{:S(2)}) collective-permute-start(bf16[2,160,1280]{2,1,0:T(8,128)(2,1)S(1)} %pad_maximum_fusion.1), channel_id=1, source_target_pairs={{0,4},{4,8},{8,12},{12,0},{1,5},{5,9},{9,13},{13,1},{2,6},{6,10},{... | collective-permute-start | bytes 2457608 | tf_op jit(solution)/shard_map/ppermute | solution.py:19
  24.7 23.4 %collective-permute-start.3 = (bf16[2,160,1280]{2,1,0:T(8,128)(2,1)S(1)}, bf16[2,160,1280]{2,1,0:T(8,128)(2,1)}, u32[]{:S(2)}, u32[]{:S(2)}) collective-permute-start(bf16[2,160,1280]{2,1,0:T(8,128)(2,1)S(1)} %pad_maximum_fusion.1), channel_id=1, source_target_pairs={{0,12},{4,0},{8,4},{12,8},{1,13},{5,1},{9,5},{13,9},{2,14},{6,2},{... | collective-permute-start | bytes 2457608 | tf_op jit(solution)/shard_map/ppermute | solution.py:19
  27.6 11.2 %all-to-all-start.1 = ((bf16[8,32,192]{2,1,0:T(8,128)(2,1)}), bf16[8,32,192]{2,1,0:T(8,128)(2,1)S(1)}, u32[]{:S(2)}, u32[]{:S(2)}) async-start(bf16[8,32,192]{2,1,0:T(8,128)(2,1)} %broadcast_in_dim.17), calls=%async_computation.1 | async-start | bytes 262144 | tf_op jit(solution)/shard_map/all_to_all | solution.py:220
  32.6 15.5 %collective-permute-start.2 = (bf16[160,1280]{1,0:T(8,128)(2,1)S(1)}, bf16[160,1280]{1,0:T(8,128)(2,1)}, u32[]{:S(2)}, u32[]{:S(2)}) collective-permute-start(bf16[160,1280]{1,0:T(8,128)(2,1)S(1)} %collective-permute-done.1.refs_2_), channel_id=1, source_target_pairs={{0,16},{16,0},{1,17},{17,1},{2,18},{18,2},{3,19},{19,3},{4,20},{20... | collective-permute-start | bytes 1228808 | tf_op jit(solution)/shard_map/ppermute | solution.py:27
  38.8 0.6 copy-start.5
  45.3 11.2 %collective-permute-start.5 = (bf16[3,64,1280]{2,1,0:T(8,128)(2,1)}, bf16[3,64,1280]{2,1,0:T(8,128)(2,1)S(1)}, u32[]{:S(2)}, u32[]{:S(2)}) collective-permute-start(bf16[3,64,1280]{2,1,0:T(8,128)(2,1)} %get-tuple-element.64), channel_id=1, source_target_pairs={{0,32},{32,64},{64,96},{96,0},{1,33},{33,65},{65,97},{97,1},{2,34}... | collective-permute-start | bytes 1474568 | tf_op jit(solution)/shard_map/ppermute | solution.py:23
  45.9 10.7 %collective-permute-start.6 = (bf16[3,64,1280]{2,1,0:T(8,128)(2,1)}, bf16[3,64,1280]{2,1,0:T(8,128)(2,1)S(1)}, u32[]{:S(2)}, u32[]{:S(2)}) collective-permute-start(bf16[3,64,1280]{2,1,0:T(8,128)(2,1)} %get-tuple-element.66), channel_id=1, source_target_pairs={{0,96},{32,0},{64,32},{96,64},{1,97},{33,1},{65,33},{97,65},{2,98}... | collective-permute-start | bytes 1474568 | tf_op jit(solution)/shard_map/ppermute | solution.py:23
  48.1 0.9 copy-start.14
  56.6 10.0 %copy-start.6 = (bf16[3,64,1280]{2,1,0:T(8,128)(2,1)}, bf16[3,64,1280]{2,1,0:T(8,128)(2,1)S(1)}, u32[]{:S(2)}) copy-start(bf16[3,64,1280]{2,1,0:T(8,128)(2,1)S(1)} %collective-permute-done.5.refs_8_) | copy-start | bytes 1474564
  56.6 10.0 %copy-start.7 = (bf16[3,64,1280]{2,1,0:T(8,128)(2,1)}, bf16[3,64,1280]{2,1,0:T(8,128)(2,1)S(1)}, u32[]{:S(2)}) copy-start(bf16[3,64,1280]{2,1,0:T(8,128)(2,1)S(1)} %collective-permute-done.6.refs_10_) | copy-start | bytes 1474564
  56.6 8.2 %collective-permute-start.7 = (f32[2,192,1280]{2,1,0:T(8,128)}, f32[2,192,1280]{2,1,0:T(8,128)S(1)}, u32[]{:S(2)}, u32[]{:S(2)}) collective-permute-start(f32[2,192,1280]{2,1,0:T(8,128)} %get-tuple-element.69), channel_id=1, source_target_pairs={{0,1},{1,0},{2,3},{3,2},{4,5},{5,4},{6,7},{7,6},{8,9},{9,8},{10,11... | collective-permute-start | bytes 5898248 | tf_op jit(solution)/shard_map/ppermute | solution.py:27
  66.6 17.1 %copy-start.16 = (bf16[3,64,1280]{2,1,0:T(8,128)(2,1)S(1)}, bf16[3,64,1280]{2,1,0:T(8,128)(2,1)}, u32[]{:S(2)}) copy-start(bf16[3,64,1280]{2,1,0:T(8,128)(2,1)} %get-tuple-element.81) | copy-start | bytes 1474564
  66.6 21.4 %copy-start.15 = (bf16[3,64,1280]{2,1,0:T(8,128)(2,1)S(1)}, bf16[3,64,1280]{2,1,0:T(8,128)(2,1)}, u32[]{:S(2)}) copy-start(bf16[3,64,1280]{2,1,0:T(8,128)(2,1)} %get-tuple-element.83) | copy-start | bytes 1474564
  66.7 37.4 %copy-start.13 = (bf16[6,64,1280]{2,1,0:T(8,128)(2,1)S(1)}, bf16[6,64,1280]{2,1,0:T(8,128)(2,1)}, u32[]{:S(2)}) copy-start(bf16[6,64,1280]{2,1,0:T(8,128)(2,1)} %get-tuple-element.88) | copy-start | bytes 2949124
  66.7 13.5 %collective-permute-start.9 = (bf16[192,1280]{1,0:T(8,128)(2,1)S(1)}, bf16[192,1280]{1,0:T(8,128)(2,1)S(1)}, u32[]{:S(2)}, u32[]{:S(2)}) collective-permute-start(bf16[192,1280]{1,0:T(8,128)(2,1)S(1)} %get-tuple-element.93), channel_id=1, source_target_pairs={{0,32},{1,96},{2,0},{3,64},{32,33},{33,97},{34,1},{35,65},{64,34},... | collective-permute-start | bytes 1474568 | tf_op jit(solution)/shard_map/ppermute | solution.py:235
  69.2 12.1 %collective-permute-start.8 = (bf16[192,1280]{1,0:T(8,128)(2,1)S(1)}, bf16[192,1280]{1,0:T(8,128)(2,1)S(1)}, u32[]{:S(2)}, u32[]{:S(2)}) collective-permute-start(bf16[192,1280]{1,0:T(8,128)(2,1)S(1)} %get-tuple-element.94), channel_id=1, source_target_pairs={{0,0},{1,64},{2,32},{3,96},{32,1},{33,65},{34,33},{35,97},{64,2},{... | collective-permute-start | bytes 1474568 | tf_op jit(solution)/shard_map/ppermute | solution.py:235
  81.4 46.7 %copy-start = (bf16[192,1280]{1,0:T(8,128)(2,1)}, bf16[192,1280]{1,0:T(8,128)(2,1)S(1)}, u32[]{:S(2)}) copy-start(bf16[192,1280]{1,0:T(8,128)(2,1)S(1)} %add_convert_fusion.1) | copy-start | bytes 1474564
  81.4 12.8 %collective-permute-start.11 = (bf16[6,32,1280]{2,1,0:T(8,128)(2,1)S(1)}, bf16[6,32,1280]{2,1,0:T(8,128)(2,1)S(1)}, u32[]{:S(2)}, u32[]{:S(2)}) collective-permute-start(bf16[6,32,1280]{2,1,0:T(8,128)(2,1)S(1)} %bitcast.30), channel_id=1, source_target_pairs={{0,8},{4,12},{8,0},{12,4},{1,9},{5,13},{9,1},{13,5},{2,10},{6,14},... | collective-permute-start | bytes 1474568 | tf_op jit(solution)/shard_map/ppermute | solution.py:19
  82.5 15.8 %collective-permute-start.10 = (bf16[6,32,1280]{2,1,0:T(8,128)(2,1)S(1)}, bf16[6,32,1280]{2,1,0:T(8,128)(2,1)S(1)}, u32[]{:S(2)}, u32[]{:S(2)}) collective-permute-start(bf16[6,32,1280]{2,1,0:T(8,128)(2,1)S(1)} %bitcast.31), channel_id=1, source_target_pairs={{0,16},{16,0},{1,17},{17,1},{2,18},{18,2},{3,19},{19,3},{4,20},{20... | collective-permute-start | bytes 1474568 | tf_op jit(solution)/shard_map/ppermute | solution.py:27
  83.7 14.6 %collective-permute-start.12 = (bf16[3,64,1280]{2,1,0:T(8,128)(2,1)S(1)}, bf16[3,64,1280]{2,1,0:T(8,128)(2,1)S(1)}, u32[]{:S(2)}, u32[]{:S(2)}) collective-permute-start(bf16[3,64,1280]{2,1,0:T(8,128)(2,1)S(1)} %copy-done.16), channel_id=1, source_target_pairs={{0,32},{32,64},{64,96},{96,0},{1,33},{33,65},{65,97},{97,1},{2,34}... | collective-permute-start | bytes 1474568 | tf_op jit(solution)/shard_map/ppermute | solution.py:23
  88.0 12.5 %collective-permute-start.13 = (bf16[3,64,1280]{2,1,0:T(8,128)(2,1)S(1)}, bf16[3,64,1280]{2,1,0:T(8,128)(2,1)S(1)}, u32[]{:S(2)}, u32[]{:S(2)}) collective-permute-start(bf16[3,64,1280]{2,1,0:T(8,128)(2,1)S(1)} %copy-done.15), channel_id=1, source_target_pairs={{0,96},{32,0},{64,32},{96,64},{1,97},{33,1},{65,33},{97,65},{2,98}... | collective-permute-start | bytes 1474568 | tf_op jit(solution)/shard_map/ppermute | solution.py:23
  94.2 31.5 %copy-start.8 = (bf16[6,32,1280]{2,1,0:T(8,128)(2,1)}, bf16[6,32,1280]{2,1,0:T(8,128)(2,1)S(1)}, u32[]{:S(2)}) copy-start(bf16[6,32,1280]{2,1,0:T(8,128)(2,1)S(1)} %collective-permute-done.11.refs_2_) | copy-start | bytes 1474564
  98.3 29.8 %copy-start.1 = (bf16[6,32,1280]{2,1,0:T(8,128)(2,1)}, bf16[6,32,1280]{2,1,0:T(8,128)(2,1)S(1)}, u32[]{:S(2)}) copy-start(bf16[6,32,1280]{2,1,0:T(8,128)(2,1)S(1)} %collective-permute-done.10.refs_1_) | copy-start | bytes 1474564
  98.3 2.2 %copy-start.9 = (bf16[3,64,1280]{2,1,0:T(8,128)(2,1)}, bf16[3,64,1280]{2,1,0:T(8,128)(2,1)S(1)}, u32[]{:S(2)}) copy-start(bf16[3,64,1280]{2,1,0:T(8,128)(2,1)S(1)} %collective-permute-done.12.refs_9_) | copy-start | bytes 1474564
  100.5 0.8 copy-start.10
  101.4 24.4 %collective-permute-start.16 = (bf16[2,6,32,1280]{3,2,1,0:T(8,128)(2,1)S(1)}, bf16[2,6,32,1280]{3,2,1,0:T(8,128)(2,1)S(1)}, u32[]{:S(2)}, u32[]{:S(2)}) collective-permute-start(bf16[2,6,32,1280]{3,2,1,0:T(8,128)(2,1)S(1)} %pad_maximum_fusion), channel_id=1, source_target_pairs={{0,4},{4,8},{8,12},{12,0},{1,5},{5,9},{9,13},{13,1},{2,6},{6,10},{... | collective-permute-start | bytes 2949128 | tf_op jit(solution)/shard_map/ppermute | solution.py:19
  101.8 23.9 %collective-permute-start.15 = (bf16[2,6,32,1280]{3,2,1,0:T(8,128)(2,1)S(1)}, bf16[2,6,32,1280]{3,2,1,0:T(8,128)(2,1)S(1)}, u32[]{:S(2)}, u32[]{:S(2)}) collective-permute-start(bf16[2,6,32,1280]{3,2,1,0:T(8,128)(2,1)S(1)} %pad_maximum_fusion), channel_id=1, source_target_pairs={{0,12},{4,0},{8,4},{12,8},{1,13},{5,1},{9,5},{13,9},{2,14},{6,2},{... | collective-permute-start | bytes 2949128 | tf_op jit(solution)/shard_map/ppermute | solution.py:19
  104.1 24.0 %collective-permute-start.17 = (bf16[6,64,1280]{2,1,0:T(8,128)(2,1)S(1)}, bf16[6,64,1280]{2,1,0:T(8,128)(2,1)S(1)}, u32[]{:S(2)}, u32[]{:S(2)}) collective-permute-start(bf16[6,64,1280]{2,1,0:T(8,128)(2,1)S(1)} %copy-done.13), channel_id=1, source_target_pairs={{0,64},{32,96},{64,0},{96,32},{1,65},{33,97},{65,1},{97,33},{2,66}... | collective-permute-start | bytes 2949128 | tf_op jit(solution)/shard_map/ppermute | solution.py:23
  104.7 10.0 %collective-permute-start.14 = (bf16[6,32,1280]{2,1,0:T(8,128)(2,1)S(1)}, bf16[6,32,1280]{2,1,0:T(8,128)(2,1)S(1)}, u32[]{:S(2)}, u32[]{:S(2)}) collective-permute-start(bf16[6,32,1280]{2,1,0:T(8,128)(2,1)S(1)} %collective-permute-done.11.refs_2_), channel_id=1, source_target_pairs={{0,16},{16,0},{1,17},{17,1},{2,18},{18,2},{3,19},{19,3},{4,20},{20... | collective-permute-start | bytes 1474568 | tf_op jit(solution)/shard_map/ppermute | solution.py:27
  114.7 11.0 %copy-start.11 = (bf16[6,32,1280]{2,1,0:T(8,128)(2,1)}, bf16[6,32,1280]{2,1,0:T(8,128)(2,1)S(1)}, u32[]{:S(2)}) copy-start(bf16[6,32,1280]{2,1,0:T(8,128)(2,1)S(1)} %collective-permute-done.14.refs_3_) | copy-start | bytes 1474564
  125.7 2.3 %copy-start.2 = (bf16[2,6,32,1280]{3,2,1,0:T(8,128)(2,1)}, bf16[2,6,32,1280]{3,2,1,0:T(8,128)(2,1)S(1)}, u32[]{:S(2)}) copy-start(bf16[2,6,32,1280]{3,2,1,0:T(8,128)(2,1)S(1)} %collective-permute-done.16.refs_5_) | copy-start | bytes 2949124
  125.8 2.3 %copy-start.3 = (bf16[2,6,32,1280]{3,2,1,0:T(8,128)(2,1)}, bf16[2,6,32,1280]{3,2,1,0:T(8,128)(2,1)S(1)}, u32[]{:S(2)}) copy-start(bf16[2,6,32,1280]{3,2,1,0:T(8,128)(2,1)S(1)} %collective-permute-done.15.refs_4_) | copy-start | bytes 2949124
  128.1 1.0 copy-start.4
Sparse Core Ops, SparseCore 0:
  9.0 34.3 all-gather.1

commit v4 on v3

--- a/solution.py
+++ b/solution.py
@@ -38,12 +38,16 @@
 
 
 def mixed_kernel(where, x_ref, b_ref, *refs):
-    outs, xs, rows = refs[:6], refs[6], refs[7]
+    outs, xs, rows, square = refs[:6], refs[6], refs[7], refs[8]
 
     @pl.when(pl.program_id(0) == 0)
     def _():
-        x = where[0]
-        rows[...] = x_ref[...].astype(F32).T
+        x, y = where[0], where[2]
+        given = x_ref[...].astype(F32)
+        for at in range(32):
+            to = at // 4 * 32 + (y + at % 4) % 4 * 8
+            square[pl.ds(pl.multiple_of(to, 8), 8), :] = given[at * 8 : at * 8 + 8]
+        rows[...] = square[...].T
         for j in range(4):
             q = (x + j) % 4
             xs[j * 48 : j * 48 + 48, :] = rows[pl.ds(pl.multiple_of(q * 48, 48), 48), :].astype(BF16)
@@ -73,9 +77,9 @@
             pl.BlockSpec((2, 256, g), lambda i: (i, 0, 0)),
         ],
         out_specs=[pl.BlockSpec((6, 16, g), lambda i: (0, i, 0))] * 2
-        + [pl.BlockSpec((3, 16, g), lambda i: (0, i, 0))] * 4,
-        out_shape=[jax.ShapeDtypeStruct((6, 64, g), BF16)] * 2 + [jax.ShapeDtypeStruct((3, 64, g), BF16)] * 4,
-        scratch_shapes=[pltpu.VMEM((192, 256), BF16), pltpu.VMEM((192, 256), F32)],
+        + [pl.BlockSpec((n, 16, g), lambda i: (0, i, 0)) for n in (3, 3, 3, 3)],
+        out_shape=[jax.ShapeDtypeStruct((n, 64, g), BF16) for n in (6, 6, 3, 3, 3, 3)],
+        scratch_shapes=[pltpu.VMEM((192, 256), BF16), pltpu.VMEM((192, 256), F32), pltpu.VMEM((256, 192), F32)],
         compiler_params=pltpu.CompilerParams(vmem_limit_bytes=VMEM_LIMIT),
         cost_estimate=pl.CostEstimate(flops=2 * 192 * 256 * 8 * g, bytes_accessed=9200000, transcendentals=0),
         name="mix",
@@ -206,27 +210,31 @@
     axes = ("x", "zl", "y", "zh", "core")
     where = jnp.stack([lax.axis_index(a) for a in axes]).astype(jnp.int32)
 
+    own = jnp.transpose(vectors, (2, 1, 0)).reshape(8, 192)
+    line = [own] + [shift_from(own, "y", s) for s in (1, 2, 3)]
+    line, screened_far = lax.optimization_barrier((line, screened))
+    lines = jnp.broadcast_to(jnp.concatenate(line)[None], (8, 32, 192))
+
+    w_own = screened_far.T
+    other, two = swap(screened.T, "zl"), shift_from(w_own, "y", 2)
+
     m_own = jnp.transpose(val_pairs, (1, 0, 2)).reshape(192, g)
     m = lax.all_gather(m_own, "x", axis=0, tiled=True)
 
-    w_own = screened.T
-    other, two = swap(w_own, "zl"), shift_from(w_own, "y", 2)
-
-    own = jnp.transpose(vectors, (2, 1, 0)).reshape(1, 8, 192)
-    line = lax.all_to_all(jnp.broadcast_to(own, (4, 8, 192)), "y", split_axis=0, concat_axis=0, tiled=True)
-    other, two, line = lax.optimization_barrier((other, two, line))
+    x_all = lax.all_to_all(lines, ("x", "zl"), split_axis=0, concat_axis=0, tiled=True).reshape(256, 192)
+    other, two, x_all = lax.optimization_barrier((other, two, x_all))
     w = end_gather(w_own, other, two)
-    lines = jnp.broadcast_to(line.reshape(1, 32, 192), (8, 32, 192))
-    x_all = lax.all_to_all(lines, ("x", "zl"), split_axis=0, concat_axis=0, tiled=True).reshape(256, 192)
 
     mixed = mix(where, x_all, cond_pairs)
     mixed = list(mixed)
+    w[3], mixed[2], mixed[4] = lax.optimization_barrier((w[3], mixed[2], mixed[4]))
     m, w, mixed[0] = lax.optimization_barrier((m, w, mixed[0]))
     mixed[2], mixed[4] = shift_to(mixed[2], "x", 1), shift_to(mixed[4], "x", 3)
 
     send, keep = make_z(where, m, w)
     send, keep, mixed = lax.optimization_barrier((send, keep, mixed))
-    part = (keep + swap(send, "core")).astype(BF16)
+    got = swap(send, "core")
+    part = [(keep[a] + got[a]).astype(BF16) for a in range(2)]
     got = []
     for a in range(2):
         perm = [
@@ -237,7 +245,8 @@
     z_own = (got[0].astype(F32) + got[1].astype(F32)).astype(BF16).reshape(6, 32, g)
     other, two = swap(z_own, "zl"), shift_from(z_own, "y", 2)
     mixed[3], mixed[5] = shift_to(mixed[3], "x", 1), shift_to(mixed[5], "x", 3)
-    z_own, other, two, mixed = lax.optimization_barrier((z_own, other, two, mixed))
+    z_own, other, two = lax.optimization_barrier((z_own, other, two))
+    mixed = lax.optimization_barrier(mixed)
     z = end_gather(z_own, other, two)
     mixed[1] = shift_to(mixed[1], "x", 2)
 

time: 164 us -> 157 us (0.957)
  waiting for transfers between devices: 51.8 us -> 46.3 us
    all_to_all x1 -> x0, starting transfers between devices: 4.95 us -> none  [shards(): lax.all_to_all(lines, ('x', 'zl'), split_axis=0, concat_axis=0, tiled=True)]
    all_to_all x1, blocking collectives: 7.03 us -> 11.5 us  [shards(): lax.all_to_all(lines, ('x', 'zl'), split_axis=0, concat_axis=0, tiled=True)]
    all_to_all x1 -> x0, waiting for transfers between devices: 4.13 us -> none  [shards(): lax.all_to_all(lines, ('x', 'zl'), split_axis=0, concat_axis=0, tiled=True)]
    all_to_all x1, blocking collectives: 20.3 us -> 17 us  [shards(): lax.all_to_all(sums, ('x', 'zh', 'core'), split_axis=0, concat_axis=0, ti...]
    ppermute x5, waiting for transfers between devices: 18.1 us -> 21.2 us  [swap(): return lax.ppermute(a, axis, [(0, 1), (1, 0)])]
    ppermute x6 -> x9, starting transfers between devices: 10.4 us -> 13.2 us  [shift_from(): return lax.ppermute(a, axis, [(i, (i - s) % 4) for i in range(4)])]
    ppermute x5, waiting for transfers between devices: 4.49 us -> 2.4 us  [shift_to(): return lax.ppermute(a, axis, [(i, (i + s) % 4) for i in range(4)])]
    ppermute x2, waiting for transfers between devices: 7.87 us -> 5.8 us  [shards(): got.append(lax.ppermute(part[a], ('x', 'zh', 'core'), perm))]
  transfers between devices with their start and end apart: 20 -> 22, of which waited for: 11 -> 9; matrix products, arithmetic and copies ran while one was open for 2% -> 1% of each run, Pallas kernels for 8% -> 9%
where the time goes in v4:
time: 157 us; the launch traced here: 156 us
  waiting for transfers between devices  46.3 us (29%)
  starting transfers between devices  39.1 us (25%)
  blocking collectives  28.5 us (18%)
  Pallas kernels  19.8 us (13%)
  between operations  13.7 us (9%)
  local copies, waits for them, and re-layouts  6.93 us (4%)
  other arithmetic  2.06 us (1%)
    ppermute x5, waiting for transfers between devices, swap(): return lax.ppermute(a, axis, [(0, 1), (1, 0)])  21.2 us
    all_to_all x1, blocking collectives, shards(): lax.all_to_all(sums, ('x', 'zh', 'core'), split_axis=0, concat_axis=0, ti...  17 us
    ppermute x9, waiting for transfers between devices, shift_from(): return lax.ppermute(a, axis, [(i, (i - s) % 4) for i in range(4)])  16.9 us
    ppermute x9, starting transfers between devices, shift_from(): return lax.ppermute(a, axis, [(i, (i - s) % 4) for i in range(4)])  13.2 us
    all_to_all x1, blocking collectives, shards(): lax.all_to_all(lines, ('x', 'zl'), split_axis=0, concat_axis=0, tiled=True)  11.5 us
    ppermute x5, starting transfers between devices, swap(): return lax.ppermute(a, axis, [(0, 1), (1, 0)])  9.6 us
    ppermute x5, starting transfers between devices, shift_to(): return lax.ppermute(a, axis, [(i, (i + s) % 4) for i in range(4)])  8.64 us
    ppermute x2, starting transfers between devices, shards(): got.append(lax.ppermute(part[a], ('x', 'zh', 'core'), perm))  7.65 us
  transfers between devices with their start and end apart: 22, of which 9 were waited for; matrix products, arithmetic and copies ran while one was open for 1% of the time, Pallas kernels for 9%

profile of v4, /device:TPU:1, one launch (start us, length us, event | category | flops | bytes accessed | tf_op | source)
XLA Modules:
  0.0 156.4 jit_solution(472377693965350310)
XLA Ops:
  6.5 2.0 %copy.10 = bf16[24,8,1280]{2,1,0:T(8,128)(2,1)} copy(bf16[24,8,1280]{2,0,1:T(8,128)(2,1)} %bitcast.37) | data formatting | bytes 983040 | tf_op jit(solution)/shard_map/transpose | solution.py:221
  8.5 0.8 copy.7
  9.3 0.1 reshape.21
  9.4 2.2 %collective-permute-start.2 = (bf16[8,192]{1,0:T(8,128)(2,1)S(1)}, bf16[8,192]{1,0:T(8,128)(2,1)S(1)}, u32[]{:S(2)}, u32[]{:S(2)}) collective-permute-start(bf16[8,192]{1,0:T(8,128)(2,1)S(1)} %reshape.21), channel_id=1, source_target_pairs={{0,4},{4,8},{8,12},{12,0},{1,5},{5,9},{9,13},{13,1},{2,6},{6,10},{... | collective-permute-start | bytes 9224 | tf_op jit(solution)/shard_map/ppermute | solution.py:19
  11.6 2.6 %collective-permute-start.1 = (bf16[8,192]{1,0:T(8,128)(2,1)S(1)}, bf16[8,192]{1,0:T(8,128)(2,1)S(1)}, u32[]{:S(2)}, u32[]{:S(2)}) collective-permute-start(bf16[8,192]{1,0:T(8,128)(2,1)S(1)} %reshape.21), channel_id=1, source_target_pairs={{0,8},{4,12},{8,0},{12,4},{1,9},{5,13},{9,1},{13,5},{2,10},{6,14},... | collective-permute-start | bytes 9224 | tf_op jit(solution)/shard_map/ppermute | solution.py:19
  14.3 1.1 collective-permute-start
  15.3 1.6 %collective-permute-start.3 = (bf16[160,1280]{1,0:T(8,128)(2,1)}, bf16[160,1280]{1,0:T(8,128)(2,1)S(1)}, u32[]{:S(2)}, u32[]{:S(2)}) collective-permute-start(bf16[160,1280]{1,0:T(8,128)(2,1)} %bitcast.38), channel_id=1, source_target_pairs={{0,16},{16,0},{1,17},{17,1},{2,18},{18,2},{3,19},{19,3},{4,20},{20... | collective-permute-start | bytes 1228808 | tf_op jit(solution)/shard_map/ppermute | solution.py:27
  17.0 0.0 collective-permute-done
  17.0 1.2 collective-permute-start.4
  18.2 11.5 %all_to_all.10 = bf16[8,32,192]{2,1,0:T(8,128)(2,1)} all-to-all(bf16[8,32,192]{2,1,0:T(8,128)(2,1)S(1)} %broadcast_in_dim.2), channel_id=1, replica_groups=mesh['x'=4,'zl'=2,'y'=4,'zh'=2,'core'=2] {'x','zl'}, dimensions={0} | all-to-all | bytes 196608 | tf_op jit(solution)/shard_map/all_to_all | solution.py:224
  29.8 0.1 pad_maximum_fusion.1
  29.9 1.3 collective-permute-start.7
  31.1 1.5 collective-permute-start.6
  32.6 1.2 collective-permute-start.5
  33.8 0.6 stack.50.where
  34.4 6.1 %mix.1 = (bf16[6,64,1280]{2,1,0:T(8,128)(2,1)}, bf16[6,64,1280]{2,1,0:T(8,128)(2,1)}, bf16[3,64,1280]{2,1,0:T(8,128)(2,1)}, bf16[3,64,1280]{2,1,0:T(8,128)(2,1)}...) custom-call(s32[5]{0:T(128)} %stack.50.where, bf16[256,192]{1,0:T(8,128)(2,1)} %bitcast.36, ...), custom_call_target="tpu_custom_call" | custom-call | flops 1006632960 | bytes 9200000 | tf_op jit(solution)/shard_map/mix/pallas_call | solution.py:71
  40.5 0.8 copy-done.18
  41.3 0.2 collective-permute-start.8
  41.5 2.5 %collective-permute-start.9 = (bf16[3,64,1280]{2,1,0:T(8,128)(2,1)}, bf16[3,64,1280]{2,1,0:T(8,128)(2,1)S(1)}, u32[]{:S(2)}, u32[]{:S(2)}) collective-permute-start(bf16[3,64,1280]{2,1,0:T(8,128)(2,1)} %get-tuple-element.82), channel_id=1, source_target_pairs={{0,96},{32,0},{64,32},{96,64},{1,97},{33,1},{65,33},{97,65},{2,98}... | collective-permute-start | bytes 1474568 | tf_op jit(solution)/shard_map/ppermute | solution.py:23
  44.0 3.1 %collective-permute-done.7.refs_5_ = bf16[2,160,1280]{2,1,0:T(8,128)(2,1)S(1)} collective-permute-done((bf16[2,160,1280]{2,1,0:T(8,128)(2,1)S(1)}, bf16[2,160,1280]{2,1,0:T(8,128)(2,1)S(1)}, u32[]{:S(2)}, u32[]{:S(2)}) %collective-permute-start.7) | collective-permute-done | bytes 819232 | tf_op jit(solution)/shard_map/ppermute | solution.py:19
  47.1 0.9 copy-done.14
  48.0 7.6 %make_z.1 = (f32[2,192,1280]{2,1,0:T(8,128)}, f32[2,192,1280]{2,1,0:T(8,128)}) custom-call(s32[5]{0:T(128)} %stack.50.where, bf16[768,1280]{1,0:T(8,128)(2,1)} %all-gather.2.cloned.1.call-done.m, bf16[160,1280]{1,0:T(8,128)(2,1)} %bitcast.40, bf16[160,1280]{1,0:T(8,128)(2,1)} %copy-done.12, bf16[160,1280]{1,0:T(8,128)(2,1)} %copy-done.17, ...), custom_call_target="tpu_custom_call" | custom-call | flops 2516582400 | bytes 40000000 | tf_op jit(solution)/shard_map/make_z/pallas_call | solution.py:129
  55.6 4.8 %collective-permute-start.10 = (f32[2,192,1280]{2,1,0:T(8,128)}, f32[2,192,1280]{2,1,0:T(8,128)S(1)}, u32[]{:S(2)}, u32[]{:S(2)}) collective-permute-start(f32[2,192,1280]{2,1,0:T(8,128)} %get-tuple-element.85), channel_id=1, source_target_pairs={{0,1},{1,0},{2,3},{3,2},{4,5},{5,4},{6,7},{7,6},{8,9},{9,8},{10,11... | collective-permute-start | bytes 5898248 | tf_op jit(solution)/shard_map/ppermute | solution.py:27
  60.4 3.8 %collective-permute-done.10 = f32[2,192,1280]{2,1,0:T(8,128)S(1)} collective-permute-done((f32[2,192,1280]{2,1,0:T(8,128)}, f32[2,192,1280]{2,1,0:T(8,128)S(1)}, u32[]{:S(2)}, u32[]{:S(2)}) %collective-permute-start.10) | collective-permute-done | bytes 1966112 | tf_op jit(solution)/shard_map/ppermute | solution.py:27
  64.2 1.7 %fusion.3 = (bf16[192,1280]{1,0:T(8,128)(2,1)S(1)}, bf16[192,1280]{1,0:T(8,128)(2,1)S(1)}) fusion(f32[2,192,1280]{2,1,0:T(8,128)S(1)} %collective-permute-done.10, f32[2,192,1280]{2,1,0:T(8,128)} %get-tuple-element.84), kind=kLoop, calls=%fused_computation.8 | loop fusion | flops 983040 | bytes 4915200 | tf_op jit(solution)/shard_map/convert_element_type | solution.py:237
  66.0 1.2 collective-permute-start.12
  67.2 6.5 %collective-permute-start.11 = (bf16[192,1280]{1,0:T(8,128)(2,1)S(1)}, bf16[192,1280]{1,0:T(8,128)(2,1)S(1)}, u32[]{:S(2)}, u32[]{:S(2)}) collective-permute-start(bf16[192,1280]{1,0:T(8,128)(2,1)S(1)} %get-tuple-element.110), channel_id=1, source_target_pairs={{0,0},{1,64},{2,32},{3,96},{32,1},{33,65},{34,33},{35,97},{64,2},{... | collective-permute-start | bytes 1474568 | tf_op jit(solution)/shard_map/ppermute | solution.py:243
  73.7 4.5 %collective-permute-done.12 = bf16[192,1280]{1,0:T(8,128)(2,1)S(1)} collective-permute-done((bf16[192,1280]{1,0:T(8,128)(2,1)S(1)}, bf16[192,1280]{1,0:T(8,128)(2,1)S(1)}, u32[]{:S(2)}, u32[]{:S(2)}) %collective-permute-start.12) | collective-permute-done | bytes 491552 | tf_op jit(solution)/shard_map/ppermute | solution.py:243
  78.2 1.3 collective-permute-done.11
  79.5 0.1 add_convert_fusion
  79.6 0.6 collective-permute-start.14
  80.2 1.3 collective-permute-start.13
  81.5 5.1 %collective-permute-start.18 = (bf16[3,64,1280]{2,1,0:T(8,128)(2,1)S(1)}, bf16[3,64,1280]{2,1,0:T(8,128)(2,1)S(1)}, u32[]{:S(2)}, u32[]{:S(2)}) collective-permute-start(bf16[3,64,1280]{2,1,0:T(8,128)(2,1)S(1)} %copy-done.16), channel_id=1, source_target_pairs={{0,32},{32,64},{64,96},{96,0},{1,33},{33,65},{65,97},{97,1},{2,34}... | collective-permute-start | bytes 1474568 | tf_op jit(solution)/shard_map/ppermute | solution.py:23
  86.6 4.5 %collective-permute-done.14.refs_2_ = bf16[6,32,1280]{2,1,0:T(8,128)(2,1)S(1)} collective-permute-done((bf16[6,32,1280]{2,1,0:T(8,128)(2,1)S(1)}, bf16[6,32,1280]{2,1,0:T(8,128)(2,1)S(1)}, u32[]{:S(2)}, u32[]{:S(2)}) %collective-permute-start.14) | collective-permute-done | bytes 491552 | tf_op jit(solution)/shard_map/ppermute | solution.py:19
  91.1 6.8 %collective-permute-done.13.refs_1_ = bf16[6,32,1280]{2,1,0:T(8,128)(2,1)S(1)} collective-permute-done((bf16[6,32,1280]{2,1,0:T(8,128)(2,1)S(1)}, bf16[6,32,1280]{2,1,0:T(8,128)(2,1)S(1)}, u32[]{:S(2)}, u32[]{:S(2)}) %collective-permute-start.13) | collective-permute-done | bytes 491552 | tf_op jit(solution)/shard_map/ppermute | solution.py:27
  97.9 0.1 pad_maximum_fusion
  98.0 0.1 collective-permute-start.17
  98.1 2.7 %collective-permute-start.16 = (bf16[2,6,32,1280]{3,2,1,0:T(8,128)(2,1)S(1)}, bf16[2,6,32,1280]{3,2,1,0:T(8,128)(2,1)S(1)}, u32[]{:S(2)}, u32[]{:S(2)}) collective-permute-start(bf16[2,6,32,1280]{3,2,1,0:T(8,128)(2,1)S(1)} %pad_maximum_fusion), channel_id=1, source_target_pairs={{0,12},{4,0},{8,4},{12,8},{1,13},{5,1},{9,5},{13,9},{2,14},{6,2},{... | collective-permute-start | bytes 2949128 | tf_op jit(solution)/shard_map/ppermute | solution.py:19
  100.8 0.9 collective-permute-start.20
  101.7 0.7 collective-permute-start.15
  102.4 10.5 %collective-permute-done.15.refs_3_ = bf16[6,32,1280]{2,1,0:T(8,128)(2,1)S(1)} collective-permute-done((bf16[6,32,1280]{2,1,0:T(8,128)(2,1)S(1)}, bf16[6,32,1280]{2,1,0:T(8,128)(2,1)S(1)}, u32[]{:S(2)}, u32[]{:S(2)}) %collective-permute-start.15) | collective-permute-done | bytes 491552 | tf_op jit(solution)/shard_map/ppermute | solution.py:27
  112.9 9.2 %collective-permute-done.17.refs_5_ = bf16[2,6,32,1280]{3,2,1,0:T(8,128)(2,1)S(1)} collective-permute-done((bf16[2,6,32,1280]{3,2,1,0:T(8,128)(2,1)S(1)}, bf16[2,6,32,1280]{3,2,1,0:T(8,128)(2,1)S(1)}, u32[]{:S(2)}, u32[]{:S(2)}) %collective-permute-start.17) | collective-permute-done | bytes 983072 | tf_op jit(solution)/shard_map/ppermute | solution.py:19
  122.2 2.4 %collective-permute-done.20.refs_7_ = bf16[6,64,1280]{2,1,0:T(8,128)(2,1)S(1)} collective-permute-done((bf16[6,64,1280]{2,1,0:T(8,128)(2,1)S(1)}, bf16[6,64,1280]{2,1,0:T(8,128)(2,1)S(1)}, u32[]{:S(2)}, u32[]{:S(2)}) %collective-permute-start.20) | collective-permute-done | bytes 983072 | tf_op jit(solution)/shard_map/ppermute | solution.py:23
  124.6 1.0 copy-done.4
  125.6 6.2 %last.1 = f32[16,32,128]{2,1,0:T(8,128)} custom-call(s32[5]{0:T(128)} %stack.50.where, bf16[6,32,1280]{2,1,0:T(8,128)(2,1)} %bitcast.33, bf16[6,32,1280]{2,1,0:T(8,128)(2,1)} %copy-done.1, bf16[6,32,1280]{2,1,0:T(8,128)(2,1)} %copy-done.7, bf16[6,32,1280]{2,1,0:T(8,128)(2,1)} %copy-done.10, bf16[2,6,32,1280]{3,2,1,0:T(8,128)(2,1)} %copy-done.3, ...), custom_call_target="tpu_custom_call" | custom-call | flops 1006632960 | bytes 8000000 | tf_op jit(solution)/shard_map/last/pallas_call | solution.py:191
  131.8 17.0 %all_to_all.11 = f32[16,32,128]{2,1,0:T(8,128)S(1)} all-to-all(f32[16,32,128]{2,1,0:T(8,128)} %last.1), channel_id=1, replica_groups=mesh['x'=4,'zl'=2,'y'=4,'zh'=2,'core'=2] {'x','zh','core'}, dimensions={0} | all-to-all | bytes 524288 | tf_op jit(solution)/shard_map/all_to_all | solution.py:254
  148.9 0.1 slice_bitcast_fusion.1
  148.9 0.6 copy.8
  (54 shorter events, 0.2 us)
Async XLA Ops:
  6.5 23.2 %copy-start.11 = (bf16[1280,160]{0,1:T(8,128)(2,1)S(1)}, bf16[1280,160]{0,1:T(8,128)(2,1)}, u32[]{:S(2)}) copy-start(bf16[1280,160]{0,1:T(8,128)(2,1)} %param.6) | copy-start | bytes 1228804
  6.5 40.6 %all-gather.2.cloned.1.call-start = ((), (), s32[]{:S(2)}) async-start(), calls=%async_computation.2 | async-start | bytes 2457600 | tf_op jit(solution)/shard_map/all_gather | solution.py:222
  9.4 7.5 %collective-permute-start.2 = (bf16[8,192]{1,0:T(8,128)(2,1)S(1)}, bf16[8,192]{1,0:T(8,128)(2,1)S(1)}, u32[]{:S(2)}, u32[]{:S(2)}) collective-permute-start(bf16[8,192]{1,0:T(8,128)(2,1)S(1)} %reshape.21), channel_id=1, source_target_pairs={{0,4},{4,8},{8,12},{12,0},{1,5},{5,9},{9,13},{13,1},{2,6},{6,10},{... | collective-permute-start | bytes 9224 | tf_op jit(solution)/shard_map/ppermute | solution.py:19
  11.6 5.3 %collective-permute-start.1 = (bf16[8,192]{1,0:T(8,128)(2,1)S(1)}, bf16[8,192]{1,0:T(8,128)(2,1)S(1)}, u32[]{:S(2)}, u32[]{:S(2)}) collective-permute-start(bf16[8,192]{1,0:T(8,128)(2,1)S(1)} %reshape.21), channel_id=1, source_target_pairs={{0,8},{4,12},{8,0},{12,4},{1,9},{5,13},{9,1},{13,5},{2,10},{6,14},... | collective-permute-start | bytes 9224 | tf_op jit(solution)/shard_map/ppermute | solution.py:19
  14.3 2.8 %collective-permute-start = (bf16[8,192]{1,0:T(8,128)(2,1)S(1)}, bf16[8,192]{1,0:T(8,128)(2,1)S(1)}, u32[]{:S(2)}, u32[]{:S(2)}) collective-permute-start(bf16[8,192]{1,0:T(8,128)(2,1)S(1)} %reshape.21), channel_id=1, source_target_pairs={{0,12},{4,0},{8,4},{12,8},{1,13},{5,1},{9,5},{13,9},{2,14},{6,2},{... | collective-permute-start | bytes 9224 | tf_op jit(solution)/shard_map/ppermute | solution.py:19
  15.3 14.4 %collective-permute-start.3 = (bf16[160,1280]{1,0:T(8,128)(2,1)}, bf16[160,1280]{1,0:T(8,128)(2,1)S(1)}, u32[]{:S(2)}, u32[]{:S(2)}) collective-permute-start(bf16[160,1280]{1,0:T(8,128)(2,1)} %bitcast.38), channel_id=1, source_target_pairs={{0,16},{16,0},{1,17},{17,1},{2,18},{18,2},{3,19},{19,3},{4,20},{20... | collective-permute-start | bytes 1228808 | tf_op jit(solution)/shard_map/ppermute | solution.py:27
  17.0 12.7 %collective-permute-start.4 = (bf16[160,1280]{1,0:T(8,128)(2,1)}, bf16[160,1280]{1,0:T(8,128)(2,1)S(1)}, u32[]{:S(2)}, u32[]{:S(2)}) collective-permute-start(bf16[160,1280]{1,0:T(8,128)(2,1)} %bitcast.39), channel_id=1, source_target_pairs={{0,8},{4,12},{8,0},{12,4},{1,9},{5,13},{9,1},{13,5},{2,10},{6,14},... | collective-permute-start | bytes 1228808 | tf_op jit(solution)/shard_map/ppermute | solution.py:19
  29.7 10.7 %copy-start.12 = (bf16[160,1280]{1,0:T(8,128)(2,1)}, bf16[160,1280]{1,0:T(8,128)(2,1)S(1)}, u32[]{:S(2)}) copy-start(bf16[160,1280]{1,0:T(8,128)(2,1)S(1)} %collective-permute-done.3.refs_1_) | copy-start | bytes 1228804
  29.8 10.7 %copy-start.17 = (bf16[160,1280]{1,0:T(8,128)(2,1)}, bf16[160,1280]{1,0:T(8,128)(2,1)S(1)}, u32[]{:S(2)}) copy-start(bf16[160,1280]{1,0:T(8,128)(2,1)S(1)} %collective-permute-done.4.refs_2_) | copy-start | bytes 1228804
  29.9 17.2 %collective-permute-start.7 = (bf16[2,160,1280]{2,1,0:T(8,128)(2,1)S(1)}, bf16[2,160,1280]{2,1,0:T(8,128)(2,1)S(1)}, u32[]{:S(2)}, u32[]{:S(2)}) collective-permute-start(bf16[2,160,1280]{2,1,0:T(8,128)(2,1)S(1)} %pad_maximum_fusion.1), channel_id=1, source_target_pairs={{0,4},{4,8},{8,12},{12,0},{1,5},{5,9},{9,13},{13,1},{2,6},{6,10},{... | collective-permute-start | bytes 2457608 | tf_op jit(solution)/shard_map/ppermute | solution.py:19
  31.1 16.0 %collective-permute-start.6 = (bf16[2,160,1280]{2,1,0:T(8,128)(2,1)S(1)}, bf16[2,160,1280]{2,1,0:T(8,128)(2,1)}, u32[]{:S(2)}, u32[]{:S(2)}) collective-permute-start(bf16[2,160,1280]{2,1,0:T(8,128)(2,1)S(1)} %pad_maximum_fusion.1), channel_id=1, source_target_pairs={{0,12},{4,0},{8,4},{12,8},{1,13},{5,1},{9,5},{13,9},{2,14},{6,2},{... | collective-permute-start | bytes 2457608 | tf_op jit(solution)/shard_map/ppermute | solution.py:19
  32.6 7.9 %collective-permute-start.5 = (bf16[160,1280]{1,0:T(8,128)(2,1)S(1)}, bf16[160,1280]{1,0:T(8,128)(2,1)S(1)}, u32[]{:S(2)}, u32[]{:S(2)}) collective-permute-start(bf16[160,1280]{1,0:T(8,128)(2,1)S(1)} %collective-permute-done.4.refs_2_), channel_id=1, source_target_pairs={{0,16},{16,0},{1,17},{17,1},{2,18},{18,2},{3,19},{19,3},{4,20},{20... | collective-permute-start | bytes 1228808 | tf_op jit(solution)/shard_map/ppermute | solution.py:27
  40.5 0.8 copy-start.18
  41.3 14.3 %collective-permute-start.8 = (bf16[3,64,1280]{2,1,0:T(8,128)(2,1)}, bf16[3,64,1280]{2,1,0:T(8,128)(2,1)S(1)}, u32[]{:S(2)}, u32[]{:S(2)}) collective-permute-start(bf16[3,64,1280]{2,1,0:T(8,128)(2,1)} %get-tuple-element.80), channel_id=1, source_target_pairs={{0,32},{32,64},{64,96},{96,0},{1,33},{33,65},{65,97},{97,1},{2,34}... | collective-permute-start | bytes 1474568 | tf_op jit(solution)/shard_map/ppermute | solution.py:23
  41.5 14.1 %collective-permute-start.9 = (bf16[3,64,1280]{2,1,0:T(8,128)(2,1)}, bf16[3,64,1280]{2,1,0:T(8,128)(2,1)S(1)}, u32[]{:S(2)}, u32[]{:S(2)}) collective-permute-start(bf16[3,64,1280]{2,1,0:T(8,128)(2,1)} %get-tuple-element.82), channel_id=1, source_target_pairs={{0,96},{32,0},{64,32},{96,64},{1,97},{33,1},{65,33},{97,65},{2,98}... | collective-permute-start | bytes 1474568 | tf_op jit(solution)/shard_map/ppermute | solution.py:23
  47.1 0.9 copy-start.14
  55.6 10.4 %copy-start.5 = (bf16[3,64,1280]{2,1,0:T(8,128)(2,1)}, bf16[3,64,1280]{2,1,0:T(8,128)(2,1)S(1)}, u32[]{:S(2)}) copy-start(bf16[3,64,1280]{2,1,0:T(8,128)(2,1)S(1)} %collective-permute-done.8.refs_8_) | copy-start | bytes 1474564
  55.6 10.4 %copy-start.6 = (bf16[3,64,1280]{2,1,0:T(8,128)(2,1)}, bf16[3,64,1280]{2,1,0:T(8,128)(2,1)S(1)}, u32[]{:S(2)}) copy-start(bf16[3,64,1280]{2,1,0:T(8,128)(2,1)S(1)} %collective-permute-done.9.refs_10_) | copy-start | bytes 1474564
  55.6 25.9 %copy-start.16 = (bf16[3,64,1280]{2,1,0:T(8,128)(2,1)S(1)}, bf16[3,64,1280]{2,1,0:T(8,128)(2,1)}, u32[]{:S(2)}) copy-start(bf16[3,64,1280]{2,1,0:T(8,128)(2,1)} %get-tuple-element.100) | copy-start | bytes 1474564
  55.6 31.0 %copy-start.15 = (bf16[3,64,1280]{2,1,0:T(8,128)(2,1)S(1)}, bf16[3,64,1280]{2,1,0:T(8,128)(2,1)}, u32[]{:S(2)}) copy-start(bf16[3,64,1280]{2,1,0:T(8,128)(2,1)} %get-tuple-element.102) | copy-start | bytes 1474564
  55.6 8.6 %collective-permute-start.10 = (f32[2,192,1280]{2,1,0:T(8,128)}, f32[2,192,1280]{2,1,0:T(8,128)S(1)}, u32[]{:S(2)}, u32[]{:S(2)}) collective-permute-start(f32[2,192,1280]{2,1,0:T(8,128)} %get-tuple-element.85), channel_id=1, source_target_pairs={{0,1},{1,0},{2,3},{3,2},{4,5},{5,4},{6,7},{7,6},{8,9},{9,8},{10,11... | collective-permute-start | bytes 5898248 | tf_op jit(solution)/shard_map/ppermute | solution.py:27
  66.0 34.8 %copy-start.13 = (bf16[6,64,1280]{2,1,0:T(8,128)(2,1)S(1)}, bf16[6,64,1280]{2,1,0:T(8,128)(2,1)}, u32[]{:S(2)}) copy-start(bf16[6,64,1280]{2,1,0:T(8,128)(2,1)} %get-tuple-element.104) | copy-start | bytes 2949124
  66.0 12.2 %collective-permute-start.12 = (bf16[192,1280]{1,0:T(8,128)(2,1)S(1)}, bf16[192,1280]{1,0:T(8,128)(2,1)S(1)}, u32[]{:S(2)}, u32[]{:S(2)}) collective-permute-start(bf16[192,1280]{1,0:T(8,128)(2,1)S(1)} %get-tuple-element.109), channel_id=1, source_target_pairs={{0,32},{1,96},{2,0},{3,64},{32,33},{33,97},{34,1},{35,65},{64,34},... | collective-permute-start | bytes 1474568 | tf_op jit(solution)/shard_map/ppermute | solution.py:243
  67.2 12.3 %collective-permute-start.11 = (bf16[192,1280]{1,0:T(8,128)(2,1)S(1)}, bf16[192,1280]{1,0:T(8,128)(2,1)S(1)}, u32[]{:S(2)}, u32[]{:S(2)}) collective-permute-start(bf16[192,1280]{1,0:T(8,128)(2,1)S(1)} %get-tuple-element.110), channel_id=1, source_target_pairs={{0,0},{1,64},{2,32},{3,96},{32,1},{33,65},{34,33},{35,97},{64,2},{... | collective-permute-start | bytes 1474568 | tf_op jit(solution)/shard_map/ppermute | solution.py:243
  79.6 45.0 %copy-start = (bf16[192,1280]{1,0:T(8,128)(2,1)}, bf16[192,1280]{1,0:T(8,128)(2,1)S(1)}, u32[]{:S(2)}) copy-start(bf16[192,1280]{1,0:T(8,128)(2,1)S(1)} %add_convert_fusion) | copy-start | bytes 1474564
  79.6 11.5 %collective-permute-start.14 = (bf16[6,32,1280]{2,1,0:T(8,128)(2,1)S(1)}, bf16[6,32,1280]{2,1,0:T(8,128)(2,1)S(1)}, u32[]{:S(2)}, u32[]{:S(2)}) collective-permute-start(bf16[6,32,1280]{2,1,0:T(8,128)(2,1)S(1)} %bitcast.30), channel_id=1, source_target_pairs={{0,8},{4,12},{8,0},{12,4},{1,9},{5,13},{9,1},{13,5},{2,10},{6,14},... | collective-permute-start | bytes 1474568 | tf_op jit(solution)/shard_map/ppermute | solution.py:19
  80.2 17.8 %collective-permute-start.13 = (bf16[6,32,1280]{2,1,0:T(8,128)(2,1)S(1)}, bf16[6,32,1280]{2,1,0:T(8,128)(2,1)S(1)}, u32[]{:S(2)}, u32[]{:S(2)}) collective-permute-start(bf16[6,32,1280]{2,1,0:T(8,128)(2,1)S(1)} %bitcast.31), channel_id=1, source_target_pairs={{0,16},{16,0},{1,17},{17,1},{2,18},{18,2},{3,19},{19,3},{4,20},{20... | collective-permute-start | bytes 1474568 | tf_op jit(solution)/shard_map/ppermute | solution.py:27
  81.5 19.3 %collective-permute-start.18 = (bf16[3,64,1280]{2,1,0:T(8,128)(2,1)S(1)}, bf16[3,64,1280]{2,1,0:T(8,128)(2,1)S(1)}, u32[]{:S(2)}, u32[]{:S(2)}) collective-permute-start(bf16[3,64,1280]{2,1,0:T(8,128)(2,1)S(1)} %copy-done.16), channel_id=1, source_target_pairs={{0,32},{32,64},{64,96},{96,0},{1,33},{33,65},{65,97},{97,1},{2,34}... | collective-permute-start | bytes 1474568 | tf_op jit(solution)/shard_map/ppermute | solution.py:23
  86.6 14.2 %collective-permute-start.19 = (bf16[3,64,1280]{2,1,0:T(8,128)(2,1)S(1)}, bf16[3,64,1280]{2,1,0:T(8,128)(2,1)S(1)}, u32[]{:S(2)}, u32[]{:S(2)}) collective-permute-start(bf16[3,64,1280]{2,1,0:T(8,128)(2,1)S(1)} %copy-done.15), channel_id=1, source_target_pairs={{0,96},{32,0},{64,32},{96,64},{1,97},{33,1},{65,33},{97,65},{2,98}... | collective-permute-start | bytes 1474568 | tf_op jit(solution)/shard_map/ppermute | solution.py:23
  91.1 31.1 %copy-start.7 = (bf16[6,32,1280]{2,1,0:T(8,128)(2,1)}, bf16[6,32,1280]{2,1,0:T(8,128)(2,1)S(1)}, u32[]{:S(2)}) copy-start(bf16[6,32,1280]{2,1,0:T(8,128)(2,1)S(1)} %collective-permute-done.14.refs_2_) | copy-start | bytes 1474564
  97.9 26.7 %copy-start.1 = (bf16[6,32,1280]{2,1,0:T(8,128)(2,1)}, bf16[6,32,1280]{2,1,0:T(8,128)(2,1)S(1)}, u32[]{:S(2)}) copy-start(bf16[6,32,1280]{2,1,0:T(8,128)(2,1)S(1)} %collective-permute-done.13.refs_1_) | copy-start | bytes 1474564
  98.0 24.1 %collective-permute-start.17 = (bf16[2,6,32,1280]{3,2,1,0:T(8,128)(2,1)S(1)}, bf16[2,6,32,1280]{3,2,1,0:T(8,128)(2,1)S(1)}, u32[]{:S(2)}, u32[]{:S(2)}) collective-permute-start(bf16[2,6,32,1280]{3,2,1,0:T(8,128)(2,1)S(1)} %pad_maximum_fusion), channel_id=1, source_target_pairs={{0,4},{4,8},{8,12},{12,0},{1,5},{5,9},{9,13},{13,1},{2,6},{6,10},{... | collective-permute-start | bytes 2949128 | tf_op jit(solution)/shard_map/ppermute | solution.py:19
  98.1 24.0 %collective-permute-start.16 = (bf16[2,6,32,1280]{3,2,1,0:T(8,128)(2,1)S(1)}, bf16[2,6,32,1280]{3,2,1,0:T(8,128)(2,1)S(1)}, u32[]{:S(2)}, u32[]{:S(2)}) collective-permute-start(bf16[2,6,32,1280]{3,2,1,0:T(8,128)(2,1)S(1)} %pad_maximum_fusion), channel_id=1, source_target_pairs={{0,12},{4,0},{8,4},{12,8},{1,13},{5,1},{9,5},{13,9},{2,14},{6,2},{... | collective-permute-start | bytes 2949128 | tf_op jit(solution)/shard_map/ppermute | solution.py:19
  100.8 21.4 %copy-start.8 = (bf16[3,64,1280]{2,1,0:T(8,128)(2,1)}, bf16[3,64,1280]{2,1,0:T(8,128)(2,1)S(1)}, u32[]{:S(2)}) copy-start(bf16[3,64,1280]{2,1,0:T(8,128)(2,1)S(1)} %collective-permute-done.18.refs_9_) | copy-start | bytes 1474564
  100.8 21.4 %copy-start.9 = (bf16[3,64,1280]{2,1,0:T(8,128)(2,1)}, bf16[3,64,1280]{2,1,0:T(8,128)(2,1)S(1)}, u32[]{:S(2)}) copy-start(bf16[3,64,1280]{2,1,0:T(8,128)(2,1)S(1)} %collective-permute-done.19.refs_11_) | copy-start | bytes 1474564
  100.8 23.8 %collective-permute-start.20 = (bf16[6,64,1280]{2,1,0:T(8,128)(2,1)S(1)}, bf16[6,64,1280]{2,1,0:T(8,128)(2,1)S(1)}, u32[]{:S(2)}, u32[]{:S(2)}) collective-permute-start(bf16[6,64,1280]{2,1,0:T(8,128)(2,1)S(1)} %copy-done.13), channel_id=1, source_target_pairs={{0,64},{32,96},{64,0},{96,32},{1,65},{33,97},{65,1},{97,33},{2,66}... | collective-permute-start | bytes 2949128 | tf_op jit(solution)/shard_map/ppermute | solution.py:23
  101.7 11.2 %collective-permute-start.15 = (bf16[6,32,1280]{2,1,0:T(8,128)(2,1)S(1)}, bf16[6,32,1280]{2,1,0:T(8,128)(2,1)S(1)}, u32[]{:S(2)}, u32[]{:S(2)}) collective-permute-start(bf16[6,32,1280]{2,1,0:T(8,128)(2,1)S(1)} %collective-permute-done.14.refs_2_), channel_id=1, source_target_pairs={{0,16},{16,0},{1,17},{17,1},{2,18},{18,2},{3,19},{19,3},{4,20},{20... | collective-permute-start | bytes 1474568 | tf_op jit(solution)/shard_map/ppermute | solution.py:27
  112.9 9.3 %copy-start.10 = (bf16[6,32,1280]{2,1,0:T(8,128)(2,1)}, bf16[6,32,1280]{2,1,0:T(8,128)(2,1)S(1)}, u32[]{:S(2)}) copy-start(bf16[6,32,1280]{2,1,0:T(8,128)(2,1)S(1)} %collective-permute-done.15.refs_3_) | copy-start | bytes 1474564
  122.1 2.5 %copy-start.2 = (bf16[2,6,32,1280]{3,2,1,0:T(8,128)(2,1)}, bf16[2,6,32,1280]{3,2,1,0:T(8,128)(2,1)S(1)}, u32[]{:S(2)}) copy-start(bf16[2,6,32,1280]{3,2,1,0:T(8,128)(2,1)S(1)} %collective-permute-done.17.refs_5_) | copy-start | bytes 2949124
  122.2 2.4 %copy-start.3 = (bf16[2,6,32,1280]{3,2,1,0:T(8,128)(2,1)}, bf16[2,6,32,1280]{3,2,1,0:T(8,128)(2,1)S(1)}, u32[]{:S(2)}) copy-start(bf16[2,6,32,1280]{3,2,1,0:T(8,128)(2,1)S(1)} %collective-permute-done.16.refs_4_) | copy-start | bytes 2949124
  124.6 1.0 copy-start.4
Sparse Core Ops, SparseCore 0:
  9.0 34.3 all-gather.1

commit v5 on v4

--- a/solution.py
+++ b/solution.py
@@ -88,7 +88,8 @@
 
 def z_kernel(where, m, *refs):
     w = blocks_of(refs[0:6])
-    send, keep, ms, ws, sums, m_sem, w_sem, out_sem = refs[6:]
+    send, keep, ms, ws, sums_send, sums_keep, m_sem, w_sem, out_sem = refs[6:]
+    sums = [sums_send, sums_keep]
     zl, y, zh, core = where[1], where[2], where[3], where[4]
     copies = []
     for t in range(4):
@@ -112,12 +113,11 @@
     for half, out in enumerate((send, keep)):
         res = lax.dot_general(ms[384 * half : 384 * half + 384, :], ws[...], NT, preferred_element_type=F32)
         for a in range(2):
-            t = 2 * half + a
             for k in range(6):
-                for r in range(4):
-                    at = ((a * 4 + r) * 6 + k) * 8
-                    sums[t, (k * 4 + r) * 8 : (k * 4 + r) * 8 + 8, :] = res[at : at + 8]
-            outs.append(pltpu.make_async_copy(sums.at[t], out.at[a], out_sem.at[t]))
+                rows = [((a * 4 + r) * 6 + k) * 8 for r in range(4)]
+                block = jnp.concatenate([res[at : at + 8] for at in rows], axis=0)
+                sums[half][a, 32 * k : 32 * k + 32, :] = block.astype(out.dtype)
+            outs.append(pltpu.make_async_copy(sums[half].at[a], out.at[a], out_sem.at[2 * half + a]))
             outs[-1].start()
     for c in outs:
         c.wait()
@@ -125,16 +125,16 @@
 
 def make_z(where, m, w):
     g = m.shape[1]
-    shape = jax.ShapeDtypeStruct((2, 192, g), F32)
     return pl.pallas_call(
         z_kernel,
         in_specs=[SMEM] + [ANY] * 7,
         out_specs=[ANY, ANY],
-        out_shape=[shape, shape],
+        out_shape=[jax.ShapeDtypeStruct((2, 192, g), kind) for kind in (BF16, F32)],
         scratch_shapes=[
             pltpu.VMEM((768, g), BF16),
             pltpu.VMEM((g, g), BF16),
-            pltpu.VMEM((4, 192, g), F32),
+            pltpu.VMEM((2, 192, g), BF16),
+            pltpu.VMEM((2, 192, g), F32),
             pltpu.SemaphoreType.DMA((16,)),
             pltpu.SemaphoreType.DMA((8,)),
             pltpu.SemaphoreType.DMA((4,)),
@@ -234,7 +234,7 @@
     send, keep = make_z(where, m, w)
     send, keep, mixed = lax.optimization_barrier((send, keep, mixed))
     got = swap(send, "core")
-    part = [(keep[a] + got[a]).astype(BF16) for a in range(2)]
+    part = [(keep[a] + got[a].astype(F32)).astype(BF16) for a in range(2)]
     got = []
     for a in range(2):
         perm = [

time: 157 us -> 155 us (0.987)
  no operation moved by 1% of the time
where the time goes in v5:
time: 155 us
  waiting for transfers between devices  45.8 us (30%)
  starting transfers between devices  39 us (25%)
  blocking collectives  28.5 us (18%)
  Pallas kernels  19.7 us (13%)
  between operations  13.7 us (9%)
  local copies, waits for them, and re-layouts  6.15 us (4%)
  other arithmetic  2.05 us (1%)
    ppermute x5, waiting for transfers between devices, swap(): return lax.ppermute(a, axis, [(0, 1), (1, 0)])  19.9 us
    ppermute x9, waiting for transfers between devices, shift_from(): return lax.ppermute(a, axis, [(i, (i - s) % 4) for i in range(4)])  17.7 us
    all_to_all x1, blocking collectives, shards(): lax.all_to_all(sums, ('x', 'zh', 'core'), split_axis=0, concat_axis=0, ti...  17 us
    ppermute x9, starting transfers between devices, shift_from(): return lax.ppermute(a, axis, [(i, (i - s) % 4) for i in range(4)])  13.2 us
    all_to_all x1, blocking collectives, shards(): lax.all_to_all(lines, ('x', 'zl'), split_axis=0, concat_axis=0, tiled=True)  11.5 us
    ppermute x5, starting transfers between devices, swap(): return lax.ppermute(a, axis, [(0, 1), (1, 0)])  9.53 us
    ppermute x5, starting transfers between devices, shift_to(): return lax.ppermute(a, axis, [(i, (i + s) % 4) for i in range(4)])  8.7 us
    ppermute x2, starting transfers between devices, shards(): got.append(lax.ppermute(part[a], ('x', 'zh', 'core'), perm))  7.64 us
  transfers between devices with their start and end apart: 22, of which 9 were waited for; matrix products, arithmetic and copies ran while one was open for 1% of the time, Pallas kernels for 9%

profile of v5, /device:TPU:1, one launch (start us, length us, event | category | flops | bytes accessed | tf_op | source)
XLA Modules:
  0.0 155.0 jit_solution(13110979145658976817)
XLA Ops:
  6.5 2.0 %copy.10 = bf16[24,8,1280]{2,1,0:T(8,128)(2,1)} copy(bf16[24,8,1280]{2,0,1:T(8,128)(2,1)} %bitcast.37) | data formatting | bytes 983040 | tf_op jit(solution)/shard_map/transpose | solution.py:221
  8.5 0.0 all-gather.2.cloned.1.call-update
  8.5 0.8 copy.7
  9.3 0.1 reshape.23
  9.4 2.2 %collective-permute-start.2 = (bf16[8,192]{1,0:T(8,128)(2,1)S(1)}, bf16[8,192]{1,0:T(8,128)(2,1)S(1)}, u32[]{:S(2)}, u32[]{:S(2)}) collective-permute-start(bf16[8,192]{1,0:T(8,128)(2,1)S(1)} %reshape.23), channel_id=1, source_target_pairs={{0,4},{4,8},{8,12},{12,0},{1,5},{5,9},{9,13},{13,1},{2,6},{6,10},{... | collective-permute-start | bytes 9224 | tf_op jit(solution)/shard_map/ppermute | solution.py:19
  11.6 2.6 %collective-permute-start.1 = (bf16[8,192]{1,0:T(8,128)(2,1)S(1)}, bf16[8,192]{1,0:T(8,128)(2,1)S(1)}, u32[]{:S(2)}, u32[]{:S(2)}) collective-permute-start(bf16[8,192]{1,0:T(8,128)(2,1)S(1)} %reshape.23), channel_id=1, source_target_pairs={{0,8},{4,12},{8,0},{12,4},{1,9},{5,13},{9,1},{13,5},{2,10},{6,14},... | collective-permute-start | bytes 9224 | tf_op jit(solution)/shard_map/ppermute | solution.py:19
  14.3 1.1 collective-permute-start
  15.3 1.6 %collective-permute-start.3 = (bf16[160,1280]{1,0:T(8,128)(2,1)}, bf16[160,1280]{1,0:T(8,128)(2,1)S(1)}, u32[]{:S(2)}, u32[]{:S(2)}) collective-permute-start(bf16[160,1280]{1,0:T(8,128)(2,1)} %bitcast.38), channel_id=1, source_target_pairs={{0,16},{16,0},{1,17},{17,1},{2,18},{18,2},{3,19},{19,3},{4,20},{20... | collective-permute-start | bytes 1228808 | tf_op jit(solution)/shard_map/ppermute | solution.py:27
  17.0 0.0 collective-permute-done
  17.0 1.2 collective-permute-start.4
  18.2 11.5 %all_to_all.10 = bf16[8,32,192]{2,1,0:T(8,128)(2,1)} all-to-all(bf16[8,32,192]{2,1,0:T(8,128)(2,1)S(1)} %broadcast_in_dim.2), channel_id=1, replica_groups=mesh['x'=4,'zl'=2,'y'=4,'zh'=2,'core'=2] {'x','zl'}, dimensions={0} | all-to-all | bytes 196608 | tf_op jit(solution)/shard_map/all_to_all | solution.py:224
  29.8 0.1 pad_maximum_fusion.1
  29.9 1.3 collective-permute-start.7
  31.1 1.5 collective-permute-start.6
  32.6 1.2 collective-permute-start.5
  33.8 0.6 stack.50.where
  34.4 6.0 %mix.1 = (bf16[6,64,1280]{2,1,0:T(8,128)(2,1)}, bf16[6,64,1280]{2,1,0:T(8,128)(2,1)}, bf16[3,64,1280]{2,1,0:T(8,128)(2,1)}, bf16[3,64,1280]{2,1,0:T(8,128)(2,1)}...) custom-call(s32[5]{0:T(128)} %stack.50.where, bf16[256,192]{1,0:T(8,128)(2,1)} %bitcast.36, ...), custom_call_target="tpu_custom_call" | custom-call | flops 1006632960 | bytes 9200000 | tf_op jit(solution)/shard_map/mix/pallas_call | solution.py:71
  40.4 0.3 collective-permute-start.8
  40.7 2.5 %collective-permute-start.9 = (bf16[3,64,1280]{2,1,0:T(8,128)(2,1)}, bf16[3,64,1280]{2,1,0:T(8,128)(2,1)S(1)}, u32[]{:S(2)}, u32[]{:S(2)}) collective-permute-start(bf16[3,64,1280]{2,1,0:T(8,128)(2,1)} %get-tuple-element.82), channel_id=1, source_target_pairs={{0,96},{32,0},{64,32},{96,64},{1,97},{33,1},{65,33},{97,65},{2,98}... | collective-permute-start | bytes 1474568 | tf_op jit(solution)/shard_map/ppermute | solution.py:23
  43.2 3.9 %collective-permute-done.7.refs_5_ = bf16[2,160,1280]{2,1,0:T(8,128)(2,1)S(1)} collective-permute-done((bf16[2,160,1280]{2,1,0:T(8,128)(2,1)S(1)}, bf16[2,160,1280]{2,1,0:T(8,128)(2,1)S(1)}, u32[]{:S(2)}, u32[]{:S(2)}) %collective-permute-start.7) | collective-permute-done | bytes 819232 | tf_op jit(solution)/shard_map/ppermute | solution.py:19
  47.1 0.9 copy-done.14
  48.0 7.5 %make_z.1 = (bf16[2,192,1280]{2,1,0:T(8,128)(2,1)}, f32[2,192,1280]{2,1,0:T(8,128)}) custom-call(s32[5]{0:T(128)} %stack.50.where, bf16[768,1280]{1,0:T(8,128)(2,1)} %all-gather.2.cloned.1.call-done.m, bf16[160,1280]{1,0:T(8,128)(2,1)} %bitcast.40, bf16[160,1280]{1,0:T(8,128)(2,1)} %copy-done.12, bf16[160,1280]{1,0:T(8,128)(2,1)} %copy-done.17, ...), custom_call_target="tpu_custom_call" | custom-call | flops 2516582400 | bytes 40000000 | tf_op jit(solution)/shard_map/make_z/pallas_call | solution.py:128
  55.6 4.8 %collective-permute-start.10 = (bf16[2,192,1280]{2,1,0:T(8,128)(2,1)}, bf16[2,192,1280]{2,1,0:T(8,128)(2,1)S(1)}, u32[]{:S(2)}, u32[]{:S(2)}) collective-permute-start(bf16[2,192,1280]{2,1,0:T(8,128)(2,1)} %get-tuple-element.85), channel_id=1, source_target_pairs={{0,1},{1,0},{2,3},{3,2},{4,5},{5,4},{6,7},{7,6},{8,9},{9,8},{10,11... | collective-permute-start | bytes 2949128 | tf_op jit(solution)/shard_map/ppermute | solution.py:27
  60.4 2.4 %collective-permute-done.10 = bf16[2,192,1280]{2,1,0:T(8,128)(2,1)S(1)} collective-permute-done((bf16[2,192,1280]{2,1,0:T(8,128)(2,1)}, bf16[2,192,1280]{2,1,0:T(8,128)(2,1)S(1)}, u32[]{:S(2)}, u32[]{:S(2)}) %collective-permute-start.10) | collective-permute-done | bytes 983072 | tf_op jit(solution)/shard_map/ppermute | solution.py:27
  62.8 1.7 %fusion.1 = (bf16[192,1280]{1,0:T(8,128)(2,1)S(1)}, bf16[192,1280]{1,0:T(8,128)(2,1)S(1)}) fusion(f32[2,192,1280]{2,1,0:T(8,128)} %get-tuple-element.84, bf16[2,192,1280]{2,1,0:T(8,128)(2,1)S(1)} %collective-permute-done.10), kind=kLoop, calls=%fused_computation.6 | loop fusion | flops 1474560 | bytes 3932160 | tf_op jit(solution)/shard_map/convert_element_type | solution.py:237
  64.6 1.2 collective-permute-start.12
  65.7 6.5 %collective-permute-start.11 = (bf16[192,1280]{1,0:T(8,128)(2,1)S(1)}, bf16[192,1280]{1,0:T(8,128)(2,1)S(1)}, u32[]{:S(2)}, u32[]{:S(2)}) collective-permute-start(bf16[192,1280]{1,0:T(8,128)(2,1)S(1)} %get-tuple-element.110), channel_id=1, source_target_pairs={{0,0},{1,64},{2,32},{3,96},{32,1},{33,65},{34,33},{35,97},{64,2},{... | collective-permute-start | bytes 1474568 | tf_op jit(solution)/shard_map/ppermute | solution.py:243
  72.2 4.5 %collective-permute-done.12 = bf16[192,1280]{1,0:T(8,128)(2,1)S(1)} collective-permute-done((bf16[192,1280]{1,0:T(8,128)(2,1)S(1)}, bf16[192,1280]{1,0:T(8,128)(2,1)S(1)}, u32[]{:S(2)}, u32[]{:S(2)}) %collective-permute-start.12) | collective-permute-done | bytes 491552 | tf_op jit(solution)/shard_map/ppermute | solution.py:243
  76.8 1.3 collective-permute-done.11
  78.0 0.1 add_convert_fusion
  78.1 0.6 collective-permute-start.14
  78.7 1.3 collective-permute-start.13
  80.0 5.1 %collective-permute-start.18 = (bf16[3,64,1280]{2,1,0:T(8,128)(2,1)S(1)}, bf16[3,64,1280]{2,1,0:T(8,128)(2,1)S(1)}, u32[]{:S(2)}, u32[]{:S(2)}) collective-permute-start(bf16[3,64,1280]{2,1,0:T(8,128)(2,1)S(1)} %copy-done.16), channel_id=1, source_target_pairs={{0,32},{32,64},{64,96},{96,0},{1,33},{33,65},{65,97},{97,1},{2,34}... | collective-permute-start | bytes 1474568 | tf_op jit(solution)/shard_map/ppermute | solution.py:23
  85.1 4.5 %collective-permute-done.14.refs_2_ = bf16[6,32,1280]{2,1,0:T(8,128)(2,1)S(1)} collective-permute-done((bf16[6,32,1280]{2,1,0:T(8,128)(2,1)S(1)}, bf16[6,32,1280]{2,1,0:T(8,128)(2,1)S(1)}, u32[]{:S(2)}, u32[]{:S(2)}) %collective-permute-start.14) | collective-permute-done | bytes 491552 | tf_op jit(solution)/shard_map/ppermute | solution.py:19
  89.6 6.9 %collective-permute-done.13.refs_1_ = bf16[6,32,1280]{2,1,0:T(8,128)(2,1)S(1)} collective-permute-done((bf16[6,32,1280]{2,1,0:T(8,128)(2,1)S(1)}, bf16[6,32,1280]{2,1,0:T(8,128)(2,1)S(1)}, u32[]{:S(2)}, u32[]{:S(2)}) %collective-permute-start.13) | collective-permute-done | bytes 491552 | tf_op jit(solution)/shard_map/ppermute | solution.py:27
  96.5 0.1 pad_maximum_fusion
  96.6 0.1 collective-permute-start.17
  96.7 2.7 %collective-permute-start.16 = (bf16[2,6,32,1280]{3,2,1,0:T(8,128)(2,1)S(1)}, bf16[2,6,32,1280]{3,2,1,0:T(8,128)(2,1)S(1)}, u32[]{:S(2)}, u32[]{:S(2)}) collective-permute-start(bf16[2,6,32,1280]{3,2,1,0:T(8,128)(2,1)S(1)} %pad_maximum_fusion), channel_id=1, source_target_pairs={{0,12},{4,0},{8,4},{12,8},{1,13},{5,1},{9,5},{13,9},{2,14},{6,2},{... | collective-permute-start | bytes 2949128 | tf_op jit(solution)/shard_map/ppermute | solution.py:19
  99.4 0.9 collective-permute-start.20
  100.2 0.7 collective-permute-start.15
  100.9 10.6 %collective-permute-done.15.refs_3_ = bf16[6,32,1280]{2,1,0:T(8,128)(2,1)S(1)} collective-permute-done((bf16[6,32,1280]{2,1,0:T(8,128)(2,1)S(1)}, bf16[6,32,1280]{2,1,0:T(8,128)(2,1)S(1)}, u32[]{:S(2)}, u32[]{:S(2)}) %collective-permute-start.15) | collective-permute-done | bytes 491552 | tf_op jit(solution)/shard_map/ppermute | solution.py:27
  111.5 9.2 %collective-permute-done.17.refs_5_ = bf16[2,6,32,1280]{3,2,1,0:T(8,128)(2,1)S(1)} collective-permute-done((bf16[2,6,32,1280]{3,2,1,0:T(8,128)(2,1)S(1)}, bf16[2,6,32,1280]{3,2,1,0:T(8,128)(2,1)S(1)}, u32[]{:S(2)}, u32[]{:S(2)}) %collective-permute-start.17) | collective-permute-done | bytes 983072 | tf_op jit(solution)/shard_map/ppermute | solution.py:19
  120.8 2.4 %collective-permute-done.20.refs_7_ = bf16[6,64,1280]{2,1,0:T(8,128)(2,1)S(1)} collective-permute-done((bf16[6,64,1280]{2,1,0:T(8,128)(2,1)S(1)}, bf16[6,64,1280]{2,1,0:T(8,128)(2,1)S(1)}, u32[]{:S(2)}, u32[]{:S(2)}) %collective-permute-start.20) | collective-permute-done | bytes 983072 | tf_op jit(solution)/shard_map/ppermute | solution.py:23
  123.2 1.0 copy-done.4
  124.1 6.2 %last.1 = f32[16,32,128]{2,1,0:T(8,128)} custom-call(s32[5]{0:T(128)} %stack.50.where, bf16[6,32,1280]{2,1,0:T(8,128)(2,1)} %bitcast.33, bf16[6,32,1280]{2,1,0:T(8,128)(2,1)} %copy-done.1, bf16[6,32,1280]{2,1,0:T(8,128)(2,1)} %copy-done.7, bf16[6,32,1280]{2,1,0:T(8,128)(2,1)} %copy-done.10, bf16[2,6,32,1280]{3,2,1,0:T(8,128)(2,1)} %copy-done.3, ...), custom_call_target="tpu_custom_call" | custom-call | flops 1006632960 | bytes 8000000 | tf_op jit(solution)/shard_map/last/pallas_call | solution.py:191
  130.4 17.0 %all_to_all.11 = f32[16,32,128]{2,1,0:T(8,128)S(1)} all-to-all(f32[16,32,128]{2,1,0:T(8,128)} %last.1), channel_id=1, replica_groups=mesh['x'=4,'zl'=2,'y'=4,'zh'=2,'core'=2] {'x','zh','core'}, dimensions={0} | all-to-all | bytes 524288 | tf_op jit(solution)/shard_map/all_to_all | solution.py:254
  147.4 0.1 slice_bitcast_fusion.1
  147.5 0.6 copy.8
  (54 shorter events, 0.2 us)
Async XLA Ops:
  6.5 23.2 %copy-start.11 = (bf16[1280,160]{0,1:T(8,128)(2,1)S(1)}, bf16[1280,160]{0,1:T(8,128)(2,1)}, u32[]{:S(2)}) copy-start(bf16[1280,160]{0,1:T(8,128)(2,1)} %param.6) | copy-start | bytes 1228804
  6.5 40.6 %all-gather.2.cloned.1.call-start = ((), (), s32[]{:S(2)}) async-start(), calls=%async_computation.2 | async-start | bytes 2457600 | tf_op jit(solution)/shard_map/all_gather | solution.py:222
  9.4 7.5 %collective-permute-start.2 = (bf16[8,192]{1,0:T(8,128)(2,1)S(1)}, bf16[8,192]{1,0:T(8,128)(2,1)S(1)}, u32[]{:S(2)}, u32[]{:S(2)}) collective-permute-start(bf16[8,192]{1,0:T(8,128)(2,1)S(1)} %reshape.23), channel_id=1, source_target_pairs={{0,4},{4,8},{8,12},{12,0},{1,5},{5,9},{9,13},{13,1},{2,6},{6,10},{... | collective-permute-start | bytes 9224 | tf_op jit(solution)/shard_map/ppermute | solution.py:19
  11.6 5.3 %collective-permute-start.1 = (bf16[8,192]{1,0:T(8,128)(2,1)S(1)}, bf16[8,192]{1,0:T(8,128)(2,1)S(1)}, u32[]{:S(2)}, u32[]{:S(2)}) collective-permute-start(bf16[8,192]{1,0:T(8,128)(2,1)S(1)} %reshape.23), channel_id=1, source_target_pairs={{0,8},{4,12},{8,0},{12,4},{1,9},{5,13},{9,1},{13,5},{2,10},{6,14},... | collective-permute-start | bytes 9224 | tf_op jit(solution)/shard_map/ppermute | solution.py:19
  14.3 2.8 %collective-permute-start = (bf16[8,192]{1,0:T(8,128)(2,1)S(1)}, bf16[8,192]{1,0:T(8,128)(2,1)S(1)}, u32[]{:S(2)}, u32[]{:S(2)}) collective-permute-start(bf16[8,192]{1,0:T(8,128)(2,1)S(1)} %reshape.23), channel_id=1, source_target_pairs={{0,12},{4,0},{8,4},{12,8},{1,13},{5,1},{9,5},{13,9},{2,14},{6,2},{... | collective-permute-start | bytes 9224 | tf_op jit(solution)/shard_map/ppermute | solution.py:19
  15.3 14.4 %collective-permute-start.3 = (bf16[160,1280]{1,0:T(8,128)(2,1)}, bf16[160,1280]{1,0:T(8,128)(2,1)S(1)}, u32[]{:S(2)}, u32[]{:S(2)}) collective-permute-start(bf16[160,1280]{1,0:T(8,128)(2,1)} %bitcast.38), channel_id=1, source_target_pairs={{0,16},{16,0},{1,17},{17,1},{2,18},{18,2},{3,19},{19,3},{4,20},{20... | collective-permute-start | bytes 1228808 | tf_op jit(solution)/shard_map/ppermute | solution.py:27
  17.0 12.7 %collective-permute-start.4 = (bf16[160,1280]{1,0:T(8,128)(2,1)}, bf16[160,1280]{1,0:T(8,128)(2,1)S(1)}, u32[]{:S(2)}, u32[]{:S(2)}) collective-permute-start(bf16[160,1280]{1,0:T(8,128)(2,1)} %bitcast.39), channel_id=1, source_target_pairs={{0,8},{4,12},{8,0},{12,4},{1,9},{5,13},{9,1},{13,5},{2,10},{6,14},... | collective-permute-start | bytes 1228808 | tf_op jit(solution)/shard_map/ppermute | solution.py:19
  29.7 10.6 %copy-start.12 = (bf16[160,1280]{1,0:T(8,128)(2,1)}, bf16[160,1280]{1,0:T(8,128)(2,1)S(1)}, u32[]{:S(2)}) copy-start(bf16[160,1280]{1,0:T(8,128)(2,1)S(1)} %collective-permute-done.3.refs_1_) | copy-start | bytes 1228804
  29.8 10.6 %copy-start.17 = (bf16[160,1280]{1,0:T(8,128)(2,1)}, bf16[160,1280]{1,0:T(8,128)(2,1)S(1)}, u32[]{:S(2)}) copy-start(bf16[160,1280]{1,0:T(8,128)(2,1)S(1)} %collective-permute-done.4.refs_2_) | copy-start | bytes 1228804
  29.9 17.2 %collective-permute-start.7 = (bf16[2,160,1280]{2,1,0:T(8,128)(2,1)S(1)}, bf16[2,160,1280]{2,1,0:T(8,128)(2,1)S(1)}, u32[]{:S(2)}, u32[]{:S(2)}) collective-permute-start(bf16[2,160,1280]{2,1,0:T(8,128)(2,1)S(1)} %pad_maximum_fusion.1), channel_id=1, source_target_pairs={{0,4},{4,8},{8,12},{12,0},{1,5},{5,9},{9,13},{13,1},{2,6},{6,10},{... | collective-permute-start | bytes 2457608 | tf_op jit(solution)/shard_map/ppermute | solution.py:19
  31.1 16.0 %collective-permute-start.6 = (bf16[2,160,1280]{2,1,0:T(8,128)(2,1)S(1)}, bf16[2,160,1280]{2,1,0:T(8,128)(2,1)}, u32[]{:S(2)}, u32[]{:S(2)}) collective-permute-start(bf16[2,160,1280]{2,1,0:T(8,128)(2,1)S(1)} %pad_maximum_fusion.1), channel_id=1, source_target_pairs={{0,12},{4,0},{8,4},{12,8},{1,13},{5,1},{9,5},{13,9},{2,14},{6,2},{... | collective-permute-start | bytes 2457608 | tf_op jit(solution)/shard_map/ppermute | solution.py:19
  32.6 7.8 %collective-permute-start.5 = (bf16[160,1280]{1,0:T(8,128)(2,1)S(1)}, bf16[160,1280]{1,0:T(8,128)(2,1)S(1)}, u32[]{:S(2)}, u32[]{:S(2)}) collective-permute-start(bf16[160,1280]{1,0:T(8,128)(2,1)S(1)} %collective-permute-done.4.refs_2_), channel_id=1, source_target_pairs={{0,16},{16,0},{1,17},{17,1},{2,18},{18,2},{3,19},{19,3},{4,20},{20... | collective-permute-start | bytes 1228808 | tf_op jit(solution)/shard_map/ppermute | solution.py:27
  40.4 6.7 %copy-start.18 = (bf16[160,1280]{1,0:T(8,128)(2,1)}, bf16[160,1280]{1,0:T(8,128)(2,1)S(1)}, u32[]{:S(2)}) copy-start(bf16[160,1280]{1,0:T(8,128)(2,1)S(1)} %collective-permute-done.5.refs_3_) | copy-start | bytes 1228804
  40.4 15.1 %collective-permute-start.8 = (bf16[3,64,1280]{2,1,0:T(8,128)(2,1)}, bf16[3,64,1280]{2,1,0:T(8,128)(2,1)S(1)}, u32[]{:S(2)}, u32[]{:S(2)}) collective-permute-start(bf16[3,64,1280]{2,1,0:T(8,128)(2,1)} %get-tuple-element.80), channel_id=1, source_target_pairs={{0,32},{32,64},{64,96},{96,0},{1,33},{33,65},{65,97},{97,1},{2,34}... | collective-permute-start | bytes 1474568 | tf_op jit(solution)/shard_map/ppermute | solution.py:23
  40.7 14.9 %collective-permute-start.9 = (bf16[3,64,1280]{2,1,0:T(8,128)(2,1)}, bf16[3,64,1280]{2,1,0:T(8,128)(2,1)S(1)}, u32[]{:S(2)}, u32[]{:S(2)}) collective-permute-start(bf16[3,64,1280]{2,1,0:T(8,128)(2,1)} %get-tuple-element.82), channel_id=1, source_target_pairs={{0,96},{32,0},{64,32},{96,64},{1,97},{33,1},{65,33},{97,65},{2,98}... | collective-permute-start | bytes 1474568 | tf_op jit(solution)/shard_map/ppermute | solution.py:23
  47.1 0.9 copy-start.14
  55.6 9.0 %copy-start.5 = (bf16[3,64,1280]{2,1,0:T(8,128)(2,1)}, bf16[3,64,1280]{2,1,0:T(8,128)(2,1)S(1)}, u32[]{:S(2)}) copy-start(bf16[3,64,1280]{2,1,0:T(8,128)(2,1)S(1)} %collective-permute-done.8.refs_8_) | copy-start | bytes 1474564
  55.6 9.0 %copy-start.6 = (bf16[3,64,1280]{2,1,0:T(8,128)(2,1)}, bf16[3,64,1280]{2,1,0:T(8,128)(2,1)S(1)}, u32[]{:S(2)}) copy-start(bf16[3,64,1280]{2,1,0:T(8,128)(2,1)S(1)} %collective-permute-done.9.refs_10_) | copy-start | bytes 1474564
  55.6 24.4 %copy-start.16 = (bf16[3,64,1280]{2,1,0:T(8,128)(2,1)S(1)}, bf16[3,64,1280]{2,1,0:T(8,128)(2,1)}, u32[]{:S(2)}) copy-start(bf16[3,64,1280]{2,1,0:T(8,128)(2,1)} %get-tuple-element.100) | copy-start | bytes 1474564
  55.6 29.5 %copy-start.15 = (bf16[3,64,1280]{2,1,0:T(8,128)(2,1)S(1)}, bf16[3,64,1280]{2,1,0:T(8,128)(2,1)}, u32[]{:S(2)}) copy-start(bf16[3,64,1280]{2,1,0:T(8,128)(2,1)} %get-tuple-element.102) | copy-start | bytes 1474564
  55.6 7.2 %collective-permute-start.10 = (bf16[2,192,1280]{2,1,0:T(8,128)(2,1)}, bf16[2,192,1280]{2,1,0:T(8,128)(2,1)S(1)}, u32[]{:S(2)}, u32[]{:S(2)}) collective-permute-start(bf16[2,192,1280]{2,1,0:T(8,128)(2,1)} %get-tuple-element.85), channel_id=1, source_target_pairs={{0,1},{1,0},{2,3},{3,2},{4,5},{5,4},{6,7},{7,6},{8,9},{9,8},{10,11... | collective-permute-start | bytes 2949128 | tf_op jit(solution)/shard_map/ppermute | solution.py:27
  64.5 34.8 %copy-start.13 = (bf16[6,64,1280]{2,1,0:T(8,128)(2,1)S(1)}, bf16[6,64,1280]{2,1,0:T(8,128)(2,1)}, u32[]{:S(2)}) copy-start(bf16[6,64,1280]{2,1,0:T(8,128)(2,1)} %get-tuple-element.104) | copy-start | bytes 2949124
  64.6 12.2 %collective-permute-start.12 = (bf16[192,1280]{1,0:T(8,128)(2,1)S(1)}, bf16[192,1280]{1,0:T(8,128)(2,1)S(1)}, u32[]{:S(2)}, u32[]{:S(2)}) collective-permute-start(bf16[192,1280]{1,0:T(8,128)(2,1)S(1)} %get-tuple-element.109), channel_id=1, source_target_pairs={{0,32},{1,96},{2,0},{3,64},{32,33},{33,97},{34,1},{35,65},{64,34},... | collective-permute-start | bytes 1474568 | tf_op jit(solution)/shard_map/ppermute | solution.py:243
  65.7 12.3 %collective-permute-start.11 = (bf16[192,1280]{1,0:T(8,128)(2,1)S(1)}, bf16[192,1280]{1,0:T(8,128)(2,1)S(1)}, u32[]{:S(2)}, u32[]{:S(2)}) collective-permute-start(bf16[192,1280]{1,0:T(8,128)(2,1)S(1)} %get-tuple-element.110), channel_id=1, source_target_pairs={{0,0},{1,64},{2,32},{3,96},{32,1},{33,65},{34,33},{35,97},{64,2},{... | collective-permute-start | bytes 1474568 | tf_op jit(solution)/shard_map/ppermute | solution.py:243
  78.1 45.0 %copy-start = (bf16[192,1280]{1,0:T(8,128)(2,1)}, bf16[192,1280]{1,0:T(8,128)(2,1)S(1)}, u32[]{:S(2)}) copy-start(bf16[192,1280]{1,0:T(8,128)(2,1)S(1)} %add_convert_fusion) | copy-start | bytes 1474564
  78.1 11.5 %collective-permute-start.14 = (bf16[6,32,1280]{2,1,0:T(8,128)(2,1)S(1)}, bf16[6,32,1280]{2,1,0:T(8,128)(2,1)S(1)}, u32[]{:S(2)}, u32[]{:S(2)}) collective-permute-start(bf16[6,32,1280]{2,1,0:T(8,128)(2,1)S(1)} %bitcast.30), channel_id=1, source_target_pairs={{0,8},{4,12},{8,0},{12,4},{1,9},{5,13},{9,1},{13,5},{2,10},{6,14},... | collective-permute-start | bytes 1474568 | tf_op jit(solution)/shard_map/ppermute | solution.py:19
  78.7 17.8 %collective-permute-start.13 = (bf16[6,32,1280]{2,1,0:T(8,128)(2,1)S(1)}, bf16[6,32,1280]{2,1,0:T(8,128)(2,1)S(1)}, u32[]{:S(2)}, u32[]{:S(2)}) collective-permute-start(bf16[6,32,1280]{2,1,0:T(8,128)(2,1)S(1)} %bitcast.31), channel_id=1, source_target_pairs={{0,16},{16,0},{1,17},{17,1},{2,18},{18,2},{3,19},{19,3},{4,20},{20... | collective-permute-start | bytes 1474568 | tf_op jit(solution)/shard_map/ppermute | solution.py:27
  80.0 19.3 %collective-permute-start.18 = (bf16[3,64,1280]{2,1,0:T(8,128)(2,1)S(1)}, bf16[3,64,1280]{2,1,0:T(8,128)(2,1)S(1)}, u32[]{:S(2)}, u32[]{:S(2)}) collective-permute-start(bf16[3,64,1280]{2,1,0:T(8,128)(2,1)S(1)} %copy-done.16), channel_id=1, source_target_pairs={{0,32},{32,64},{64,96},{96,0},{1,33},{33,65},{65,97},{97,1},{2,34}... | collective-permute-start | bytes 1474568 | tf_op jit(solution)/shard_map/ppermute | solution.py:23
  85.1 14.2 %collective-permute-start.19 = (bf16[3,64,1280]{2,1,0:T(8,128)(2,1)S(1)}, bf16[3,64,1280]{2,1,0:T(8,128)(2,1)S(1)}, u32[]{:S(2)}, u32[]{:S(2)}) collective-permute-start(bf16[3,64,1280]{2,1,0:T(8,128)(2,1)S(1)} %copy-done.15), channel_id=1, source_target_pairs={{0,96},{32,0},{64,32},{96,64},{1,97},{33,1},{65,33},{97,65},{2,98}... | collective-permute-start | bytes 1474568 | tf_op jit(solution)/shard_map/ppermute | solution.py:23
  89.6 31.1 %copy-start.7 = (bf16[6,32,1280]{2,1,0:T(8,128)(2,1)}, bf16[6,32,1280]{2,1,0:T(8,128)(2,1)S(1)}, u32[]{:S(2)}) copy-start(bf16[6,32,1280]{2,1,0:T(8,128)(2,1)S(1)} %collective-permute-done.14.refs_2_) | copy-start | bytes 1474564
  96.5 26.7 %copy-start.1 = (bf16[6,32,1280]{2,1,0:T(8,128)(2,1)}, bf16[6,32,1280]{2,1,0:T(8,128)(2,1)S(1)}, u32[]{:S(2)}) copy-start(bf16[6,32,1280]{2,1,0:T(8,128)(2,1)S(1)} %collective-permute-done.13.refs_1_) | copy-start | bytes 1474564
  96.6 24.1 %collective-permute-start.17 = (bf16[2,6,32,1280]{3,2,1,0:T(8,128)(2,1)S(1)}, bf16[2,6,32,1280]{3,2,1,0:T(8,128)(2,1)S(1)}, u32[]{:S(2)}, u32[]{:S(2)}) collective-permute-start(bf16[2,6,32,1280]{3,2,1,0:T(8,128)(2,1)S(1)} %pad_maximum_fusion), channel_id=1, source_target_pairs={{0,4},{4,8},{8,12},{12,0},{1,5},{5,9},{9,13},{13,1},{2,6},{6,10},{... | collective-permute-start | bytes 2949128 | tf_op jit(solution)/shard_map/ppermute | solution.py:19
  96.7 24.0 %collective-permute-start.16 = (bf16[2,6,32,1280]{3,2,1,0:T(8,128)(2,1)S(1)}, bf16[2,6,32,1280]{3,2,1,0:T(8,128)(2,1)S(1)}, u32[]{:S(2)}, u32[]{:S(2)}) collective-permute-start(bf16[2,6,32,1280]{3,2,1,0:T(8,128)(2,1)S(1)} %pad_maximum_fusion), channel_id=1, source_target_pairs={{0,12},{4,0},{8,4},{12,8},{1,13},{5,1},{9,5},{13,9},{2,14},{6,2},{... | collective-permute-start | bytes 2949128 | tf_op jit(solution)/shard_map/ppermute | solution.py:19
  99.4 21.4 %copy-start.8 = (bf16[3,64,1280]{2,1,0:T(8,128)(2,1)}, bf16[3,64,1280]{2,1,0:T(8,128)(2,1)S(1)}, u32[]{:S(2)}) copy-start(bf16[3,64,1280]{2,1,0:T(8,128)(2,1)S(1)} %collective-permute-done.18.refs_9_) | copy-start | bytes 1474564
  99.4 21.4 %copy-start.9 = (bf16[3,64,1280]{2,1,0:T(8,128)(2,1)}, bf16[3,64,1280]{2,1,0:T(8,128)(2,1)S(1)}, u32[]{:S(2)}) copy-start(bf16[3,64,1280]{2,1,0:T(8,128)(2,1)S(1)} %collective-permute-done.19.refs_11_) | copy-start | bytes 1474564
  99.4 23.8 %collective-permute-start.20 = (bf16[6,64,1280]{2,1,0:T(8,128)(2,1)S(1)}, bf16[6,64,1280]{2,1,0:T(8,128)(2,1)S(1)}, u32[]{:S(2)}, u32[]{:S(2)}) collective-permute-start(bf16[6,64,1280]{2,1,0:T(8,128)(2,1)S(1)} %copy-done.13), channel_id=1, source_target_pairs={{0,64},{32,96},{64,0},{96,32},{1,65},{33,97},{65,1},{97,33},{2,66}... | collective-permute-start | bytes 2949128 | tf_op jit(solution)/shard_map/ppermute | solution.py:23
  100.2 11.2 %collective-permute-start.15 = (bf16[6,32,1280]{2,1,0:T(8,128)(2,1)S(1)}, bf16[6,32,1280]{2,1,0:T(8,128)(2,1)S(1)}, u32[]{:S(2)}, u32[]{:S(2)}) collective-permute-start(bf16[6,32,1280]{2,1,0:T(8,128)(2,1)S(1)} %collective-permute-done.14.refs_2_), channel_id=1, source_target_pairs={{0,16},{16,0},{1,17},{17,1},{2,18},{18,2},{3,19},{19,3},{4,20},{20... | collective-permute-start | bytes 1474568 | tf_op jit(solution)/shard_map/ppermute | solution.py:27
  111.5 9.3 %copy-start.10 = (bf16[6,32,1280]{2,1,0:T(8,128)(2,1)}, bf16[6,32,1280]{2,1,0:T(8,128)(2,1)S(1)}, u32[]{:S(2)}) copy-start(bf16[6,32,1280]{2,1,0:T(8,128)(2,1)S(1)} %collective-permute-done.15.refs_3_) | copy-start | bytes 1474564
  120.7 2.5 %copy-start.2 = (bf16[2,6,32,1280]{3,2,1,0:T(8,128)(2,1)}, bf16[2,6,32,1280]{3,2,1,0:T(8,128)(2,1)S(1)}, u32[]{:S(2)}) copy-start(bf16[2,6,32,1280]{3,2,1,0:T(8,128)(2,1)S(1)} %collective-permute-done.17.refs_5_) | copy-start | bytes 2949124
  120.8 2.4 %copy-start.3 = (bf16[2,6,32,1280]{3,2,1,0:T(8,128)(2,1)}, bf16[2,6,32,1280]{3,2,1,0:T(8,128)(2,1)S(1)}, u32[]{:S(2)}) copy-start(bf16[2,6,32,1280]{3,2,1,0:T(8,128)(2,1)S(1)} %collective-permute-done.16.refs_4_) | copy-start | bytes 2949124
  123.2 1.0 copy-start.4
Sparse Core Ops, SparseCore 0:
  9.0 34.3 all-gather.1

commit v6 on v4

--- a/solution.py
+++ b/solution.py
@@ -244,11 +244,11 @@
     got, mixed = lax.optimization_barrier((got, mixed))
     z_own = (got[0].astype(F32) + got[1].astype(F32)).astype(BF16).reshape(6, 32, g)
     other, two = swap(z_own, "zl"), shift_from(z_own, "y", 2)
+    mixed[1] = shift_to(mixed[1], "x", 2)
+    mixed = lax.optimization_barrier(mixed)
     mixed[3], mixed[5] = shift_to(mixed[3], "x", 1), shift_to(mixed[5], "x", 3)
     z_own, other, two = lax.optimization_barrier((z_own, other, two))
-    mixed = lax.optimization_barrier(mixed)
     z = end_gather(z_own, other, two)
-    mixed[1] = shift_to(mixed[1], "x", 2)
 
     sums = last(where, z, mixed)
     sums = lax.all_to_all(sums, ("x", "zh", "core"), split_axis=0, concat_axis=0, tiled=True)

time: 157 us -> 156 us (level)
  waiting for transfers between devices: 46.3 us -> 42.7 us
  starting transfers between devices: 39.1 us -> 41.8 us
    ppermute x5, waiting for transfers between devices: 21.2 us -> 10.7 us  [swap(): return lax.ppermute(a, axis, [(0, 1), (1, 0)])]
    ppermute x5, waiting for transfers between devices: 2.4 us -> 10.3 us  [shift_to(): return lax.ppermute(a, axis, [(i, (i + s) % 4) for i in range(4)])]
    ppermute x5, starting transfers between devices: 8.64 us -> 11.6 us  [shift_to(): return lax.ppermute(a, axis, [(i, (i + s) % 4) for i in range(4)])]
where the time goes in v6:
time: 156 us
  waiting for transfers between devices  42.7 us (27%)
  starting transfers between devices  41.8 us (27%)
  blocking collectives  29.3 us (19%)
  Pallas kernels  19.7 us (13%)
  between operations  13.6 us (9%)
  local copies, waits for them, and re-layouts  6.74 us (4%)
  other arithmetic  2.06 us (1%)
    all_to_all x1, blocking collectives, shards(): lax.all_to_all(sums, ('x', 'zh', 'core'), split_axis=0, concat_axis=0, ti...  17.8 us
    ppermute x9, waiting for transfers between devices, shift_from(): return lax.ppermute(a, axis, [(i, (i - s) % 4) for i in range(4)])  16 us
    ppermute x9, starting transfers between devices, shift_from(): return lax.ppermute(a, axis, [(i, (i - s) % 4) for i in range(4)])  13.2 us
    ppermute x5, starting transfers between devices, shift_to(): return lax.ppermute(a, axis, [(i, (i + s) % 4) for i in range(4)])  11.6 us
    all_to_all x1, blocking collectives, shards(): lax.all_to_all(lines, ('x', 'zl'), split_axis=0, concat_axis=0, tiled=True)  11.5 us
    ppermute x5, waiting for transfers between devices, swap(): return lax.ppermute(a, axis, [(0, 1), (1, 0)])  10.7 us
    ppermute x5, waiting for transfers between devices, shift_to(): return lax.ppermute(a, axis, [(i, (i + s) % 4) for i in range(4)])  10.3 us
    ppermute x5, starting transfers between devices, swap(): return lax.ppermute(a, axis, [(0, 1), (1, 0)])  9.38 us
  transfers between devices with their start and end apart: 22, of which 9 were waited for; matrix products, arithmetic and copies ran while one was open for 1% of the time, Pallas kernels for 9%

profile of v6, /device:TPU:1, one launch (start us, length us, event | category | flops | bytes accessed | tf_op | source)
XLA Modules:
  0.0 156.0 jit_solution(14756691548199059195)
XLA Ops:
  6.5 2.0 %copy.10 = bf16[24,8,1280]{2,1,0:T(8,128)(2,1)} copy(bf16[24,8,1280]{2,0,1:T(8,128)(2,1)} %bitcast.37) | data formatting | bytes 983040 | tf_op jit(solution)/shard_map/transpose | solution.py:221
  8.5 0.8 copy.7
  9.3 0.1 reshape.21
  9.4 2.2 %collective-permute-start.2 = (bf16[8,192]{1,0:T(8,128)(2,1)S(1)}, bf16[8,192]{1,0:T(8,128)(2,1)S(1)}, u32[]{:S(2)}, u32[]{:S(2)}) collective-permute-start(bf16[8,192]{1,0:T(8,128)(2,1)S(1)} %reshape.21), channel_id=1, source_target_pairs={{0,4},{4,8},{8,12},{12,0},{1,5},{5,9},{9,13},{13,1},{2,6},{6,10},{... | collective-permute-start | bytes 9224 | tf_op jit(solution)/shard_map/ppermute | solution.py:19
  11.6 2.6 %collective-permute-start.1 = (bf16[8,192]{1,0:T(8,128)(2,1)S(1)}, bf16[8,192]{1,0:T(8,128)(2,1)S(1)}, u32[]{:S(2)}, u32[]{:S(2)}) collective-permute-start(bf16[8,192]{1,0:T(8,128)(2,1)S(1)} %reshape.21), channel_id=1, source_target_pairs={{0,8},{4,12},{8,0},{12,4},{1,9},{5,13},{9,1},{13,5},{2,10},{6,14},... | collective-permute-start | bytes 9224 | tf_op jit(solution)/shard_map/ppermute | solution.py:19
  14.3 1.1 collective-permute-start
  15.3 1.6 %collective-permute-start.3 = (bf16[160,1280]{1,0:T(8,128)(2,1)}, bf16[160,1280]{1,0:T(8,128)(2,1)S(1)}, u32[]{:S(2)}, u32[]{:S(2)}) collective-permute-start(bf16[160,1280]{1,0:T(8,128)(2,1)} %bitcast.38), channel_id=1, source_target_pairs={{0,16},{16,0},{1,17},{17,1},{2,18},{18,2},{3,19},{19,3},{4,20},{20... | collective-permute-start | bytes 1228808 | tf_op jit(solution)/shard_map/ppermute | solution.py:27
  17.0 0.0 collective-permute-done
  17.0 1.2 collective-permute-start.4
  18.2 11.5 %all_to_all.10 = bf16[8,32,192]{2,1,0:T(8,128)(2,1)} all-to-all(bf16[8,32,192]{2,1,0:T(8,128)(2,1)S(1)} %broadcast_in_dim.2), channel_id=1, replica_groups=mesh['x'=4,'zl'=2,'y'=4,'zh'=2,'core'=2] {'x','zl'}, dimensions={0} | all-to-all | bytes 196608 | tf_op jit(solution)/shard_map/all_to_all | solution.py:224
  29.8 0.1 pad_maximum_fusion.1
  29.9 1.3 collective-permute-start.7
  31.1 1.5 collective-permute-start.6
  32.6 1.1 collective-permute-start.5
  33.8 0.7 stack.50.where
  34.4 6.0 %mix.1 = (bf16[6,64,1280]{2,1,0:T(8,128)(2,1)}, bf16[6,64,1280]{2,1,0:T(8,128)(2,1)}, bf16[3,64,1280]{2,1,0:T(8,128)(2,1)}, bf16[3,64,1280]{2,1,0:T(8,128)(2,1)}...) custom-call(s32[5]{0:T(128)} %stack.50.where, bf16[256,192]{1,0:T(8,128)(2,1)} %bitcast.36, ...), custom_call_target="tpu_custom_call" | custom-call | flops 1006632960 | bytes 9200000 | tf_op jit(solution)/shard_map/mix/pallas_call | solution.py:71
  40.4 0.8 copy-done.17
  41.2 0.2 collective-permute-start.8
  41.4 2.5 %collective-permute-start.9 = (bf16[3,64,1280]{2,1,0:T(8,128)(2,1)}, bf16[3,64,1280]{2,1,0:T(8,128)(2,1)S(1)}, u32[]{:S(2)}, u32[]{:S(2)}) collective-permute-start(bf16[3,64,1280]{2,1,0:T(8,128)(2,1)} %get-tuple-element.82), channel_id=1, source_target_pairs={{0,96},{32,0},{64,32},{96,64},{1,97},{33,1},{65,33},{97,65},{2,98}... | collective-permute-start | bytes 1474568 | tf_op jit(solution)/shard_map/ppermute | solution.py:23
  43.9 3.2 %collective-permute-done.7.refs_5_ = bf16[2,160,1280]{2,1,0:T(8,128)(2,1)S(1)} collective-permute-done((bf16[2,160,1280]{2,1,0:T(8,128)(2,1)S(1)}, bf16[2,160,1280]{2,1,0:T(8,128)(2,1)S(1)}, u32[]{:S(2)}, u32[]{:S(2)}) %collective-permute-start.7) | collective-permute-done | bytes 819232 | tf_op jit(solution)/shard_map/ppermute | solution.py:19
  47.1 0.9 copy-done.13
  48.0 7.6 %make_z.1 = (f32[2,192,1280]{2,1,0:T(8,128)}, f32[2,192,1280]{2,1,0:T(8,128)}) custom-call(s32[5]{0:T(128)} %stack.50.where, bf16[768,1280]{1,0:T(8,128)(2,1)} %all-gather.2.cloned.1.call-done.m, bf16[160,1280]{1,0:T(8,128)(2,1)} %bitcast.40, bf16[160,1280]{1,0:T(8,128)(2,1)} %copy-done.11, bf16[160,1280]{1,0:T(8,128)(2,1)} %copy-done.16, ...), custom_call_target="tpu_custom_call" | custom-call | flops 2516582400 | bytes 40000000 | tf_op jit(solution)/shard_map/make_z/pallas_call | solution.py:129
  55.6 4.8 %collective-permute-start.10 = (f32[2,192,1280]{2,1,0:T(8,128)}, f32[2,192,1280]{2,1,0:T(8,128)S(1)}, u32[]{:S(2)}, u32[]{:S(2)}) collective-permute-start(f32[2,192,1280]{2,1,0:T(8,128)} %get-tuple-element.85), channel_id=1, source_target_pairs={{0,1},{1,0},{2,3},{3,2},{4,5},{5,4},{6,7},{7,6},{8,9},{9,8},{10,11... | collective-permute-start | bytes 5898248 | tf_op jit(solution)/shard_map/ppermute | solution.py:27
  60.4 3.8 %collective-permute-done.10 = f32[2,192,1280]{2,1,0:T(8,128)S(1)} collective-permute-done((f32[2,192,1280]{2,1,0:T(8,128)}, f32[2,192,1280]{2,1,0:T(8,128)S(1)}, u32[]{:S(2)}, u32[]{:S(2)}) %collective-permute-start.10) | collective-permute-done | bytes 1966112 | tf_op jit(solution)/shard_map/ppermute | solution.py:27
  64.2 1.7 %fusion.3 = (bf16[192,1280]{1,0:T(8,128)(2,1)S(1)}, bf16[192,1280]{1,0:T(8,128)(2,1)S(1)}) fusion(f32[2,192,1280]{2,1,0:T(8,128)S(1)} %collective-permute-done.10, f32[2,192,1280]{2,1,0:T(8,128)} %get-tuple-element.84), kind=kLoop, calls=%fused_computation.8 | loop fusion | flops 983040 | bytes 4915200 | tf_op jit(solution)/shard_map/convert_element_type | solution.py:237
  66.0 1.1 collective-permute-start.12
  67.1 6.5 %collective-permute-start.11 = (bf16[192,1280]{1,0:T(8,128)(2,1)S(1)}, bf16[192,1280]{1,0:T(8,128)(2,1)S(1)}, u32[]{:S(2)}, u32[]{:S(2)}) collective-permute-start(bf16[192,1280]{1,0:T(8,128)(2,1)S(1)} %get-tuple-element.110), channel_id=1, source_target_pairs={{0,0},{1,64},{2,32},{3,96},{32,1},{33,65},{34,33},{35,97},{64,2},{... | collective-permute-start | bytes 1474568 | tf_op jit(solution)/shard_map/ppermute | solution.py:243
  73.7 4.5 %collective-permute-done.12 = bf16[192,1280]{1,0:T(8,128)(2,1)S(1)} collective-permute-done((bf16[192,1280]{1,0:T(8,128)(2,1)S(1)}, bf16[192,1280]{1,0:T(8,128)(2,1)S(1)}, u32[]{:S(2)}, u32[]{:S(2)}) %collective-permute-start.12) | collective-permute-done | bytes 491552 | tf_op jit(solution)/shard_map/ppermute | solution.py:243
  78.2 1.3 collective-permute-done.11
  79.5 0.1 add_convert_fusion
  79.6 0.6 collective-permute-start.14
  80.2 1.3 collective-permute-start.13
  81.5 6.3 %collective-permute-start.18 = (bf16[6,64,1280]{2,1,0:T(8,128)(2,1)S(1)}, bf16[6,64,1280]{2,1,0:T(8,128)(2,1)S(1)}, u32[]{:S(2)}, u32[]{:S(2)}) collective-permute-start(bf16[6,64,1280]{2,1,0:T(8,128)(2,1)S(1)} %copy-done.12), channel_id=1, source_target_pairs={{0,64},{32,96},{64,0},{96,32},{1,65},{33,97},{65,1},{97,33},{2,66}... | collective-permute-start | bytes 2949128 | tf_op jit(solution)/shard_map/ppermute | solution.py:23
  87.8 3.3 %collective-permute-done.14.refs_2_ = bf16[6,32,1280]{2,1,0:T(8,128)(2,1)S(1)} collective-permute-done((bf16[6,32,1280]{2,1,0:T(8,128)(2,1)S(1)}, bf16[6,32,1280]{2,1,0:T(8,128)(2,1)S(1)}, u32[]{:S(2)}, u32[]{:S(2)}) %collective-permute-start.14) | collective-permute-done | bytes 491552 | tf_op jit(solution)/shard_map/ppermute | solution.py:19
  91.1 6.8 %collective-permute-done.13.refs_1_ = bf16[6,32,1280]{2,1,0:T(8,128)(2,1)S(1)} collective-permute-done((bf16[6,32,1280]{2,1,0:T(8,128)(2,1)S(1)}, bf16[6,32,1280]{2,1,0:T(8,128)(2,1)S(1)}, u32[]{:S(2)}, u32[]{:S(2)}) %collective-permute-start.13) | collective-permute-done | bytes 491552 | tf_op jit(solution)/shard_map/ppermute | solution.py:27
  97.9 0.1 pad_maximum_fusion
  98.0 0.1 collective-permute-start.17
  98.1 2.7 %collective-permute-start.16 = (bf16[2,6,32,1280]{3,2,1,0:T(8,128)(2,1)S(1)}, bf16[2,6,32,1280]{3,2,1,0:T(8,128)(2,1)S(1)}, u32[]{:S(2)}, u32[]{:S(2)}) collective-permute-start(bf16[2,6,32,1280]{3,2,1,0:T(8,128)(2,1)S(1)} %pad_maximum_fusion), channel_id=1, source_target_pairs={{0,12},{4,0},{8,4},{12,8},{1,13},{5,1},{9,5},{13,9},{2,14},{6,2},{... | collective-permute-start | bytes 2949128 | tf_op jit(solution)/shard_map/ppermute | solution.py:19
  100.8 0.5 collective-permute-start.15
  101.3 8.8 %collective-permute-done.18.refs_7_ = bf16[6,64,1280]{2,1,0:T(8,128)(2,1)S(1)} collective-permute-done((bf16[6,64,1280]{2,1,0:T(8,128)(2,1)S(1)}, bf16[6,64,1280]{2,1,0:T(8,128)(2,1)S(1)}, u32[]{:S(2)}, u32[]{:S(2)}) %collective-permute-start.18) | collective-permute-done | bytes 983072 | tf_op jit(solution)/shard_map/ppermute | solution.py:23
  110.1 2.7 %collective-permute-start.20 = (bf16[3,64,1280]{2,1,0:T(8,128)(2,1)S(1)}, bf16[3,64,1280]{2,1,0:T(8,128)(2,1)}, u32[]{:S(2)}, u32[]{:S(2)}) collective-permute-start(bf16[3,64,1280]{2,1,0:T(8,128)(2,1)S(1)} %copy-done.14), channel_id=1, source_target_pairs={{0,96},{32,0},{64,32},{96,64},{1,97},{33,1},{65,33},{97,65},{2,98}... | collective-permute-start | bytes 1474568 | tf_op jit(solution)/shard_map/ppermute | solution.py:23
  112.7 9.4 %collective-permute-done.17.refs_5_ = bf16[2,6,32,1280]{3,2,1,0:T(8,128)(2,1)S(1)} collective-permute-done((bf16[2,6,32,1280]{3,2,1,0:T(8,128)(2,1)S(1)}, bf16[2,6,32,1280]{3,2,1,0:T(8,128)(2,1)S(1)}, u32[]{:S(2)}, u32[]{:S(2)}) %collective-permute-start.17) | collective-permute-done | bytes 983072 | tf_op jit(solution)/shard_map/ppermute | solution.py:19
  122.2 1.5 collective-permute-done.19.refs_9_
  123.6 0.8 copy-done.9
  124.4 6.2 %last.1 = f32[16,32,128]{2,1,0:T(8,128)} custom-call(s32[5]{0:T(128)} %stack.50.where, bf16[6,32,1280]{2,1,0:T(8,128)(2,1)} %bitcast.33, bf16[6,32,1280]{2,1,0:T(8,128)(2,1)} %copy-done.1, bf16[6,32,1280]{2,1,0:T(8,128)(2,1)} %copy-done.7, bf16[6,32,1280]{2,1,0:T(8,128)(2,1)} %copy-done.8, bf16[2,6,32,1280]{3,2,1,0:T(8,128)(2,1)} %copy-done.4, ...), custom_call_target="tpu_custom_call" | custom-call | flops 1006632960 | bytes 8000000 | tf_op jit(solution)/shard_map/last/pallas_call | solution.py:191
  130.7 17.8 %all_to_all.11 = f32[16,32,128]{2,1,0:T(8,128)S(1)} all-to-all(f32[16,32,128]{2,1,0:T(8,128)} %last.1), channel_id=1, replica_groups=mesh['x'=4,'zl'=2,'y'=4,'zh'=2,'core'=2] {'x','zh','core'}, dimensions={0} | all-to-all | bytes 524288 | tf_op jit(solution)/shard_map/all_to_all | solution.py:254
  148.4 0.1 slice_bitcast_fusion.1
  148.5 0.6 copy.8
  (52 shorter events, 0.2 us)
Async XLA Ops:
  6.5 23.2 %copy-start.10 = (bf16[1280,160]{0,1:T(8,128)(2,1)S(1)}, bf16[1280,160]{0,1:T(8,128)(2,1)}, u32[]{:S(2)}) copy-start(bf16[1280,160]{0,1:T(8,128)(2,1)} %param.6) | copy-start | bytes 1228804
  6.5 40.6 %all-gather.2.cloned.1.call-start = ((), (), s32[]{:S(2)}) async-start(), calls=%async_computation.2 | async-start | bytes 2457600 | tf_op jit(solution)/shard_map/all_gather | solution.py:222
  9.4 7.5 %collective-permute-start.2 = (bf16[8,192]{1,0:T(8,128)(2,1)S(1)}, bf16[8,192]{1,0:T(8,128)(2,1)S(1)}, u32[]{:S(2)}, u32[]{:S(2)}) collective-permute-start(bf16[8,192]{1,0:T(8,128)(2,1)S(1)} %reshape.21), channel_id=1, source_target_pairs={{0,4},{4,8},{8,12},{12,0},{1,5},{5,9},{9,13},{13,1},{2,6},{6,10},{... | collective-permute-start | bytes 9224 | tf_op jit(solution)/shard_map/ppermute | solution.py:19
  11.6 5.3 %collective-permute-start.1 = (bf16[8,192]{1,0:T(8,128)(2,1)S(1)}, bf16[8,192]{1,0:T(8,128)(2,1)S(1)}, u32[]{:S(2)}, u32[]{:S(2)}) collective-permute-start(bf16[8,192]{1,0:T(8,128)(2,1)S(1)} %reshape.21), channel_id=1, source_target_pairs={{0,8},{4,12},{8,0},{12,4},{1,9},{5,13},{9,1},{13,5},{2,10},{6,14},... | collective-permute-start | bytes 9224 | tf_op jit(solution)/shard_map/ppermute | solution.py:19
  14.3 2.8 %collective-permute-start = (bf16[8,192]{1,0:T(8,128)(2,1)S(1)}, bf16[8,192]{1,0:T(8,128)(2,1)S(1)}, u32[]{:S(2)}, u32[]{:S(2)}) collective-permute-start(bf16[8,192]{1,0:T(8,128)(2,1)S(1)} %reshape.21), channel_id=1, source_target_pairs={{0,12},{4,0},{8,4},{12,8},{1,13},{5,1},{9,5},{13,9},{2,14},{6,2},{... | collective-permute-start | bytes 9224 | tf_op jit(solution)/shard_map/ppermute | solution.py:19
  15.3 14.4 %collective-permute-start.3 = (bf16[160,1280]{1,0:T(8,128)(2,1)}, bf16[160,1280]{1,0:T(8,128)(2,1)S(1)}, u32[]{:S(2)}, u32[]{:S(2)}) collective-permute-start(bf16[160,1280]{1,0:T(8,128)(2,1)} %bitcast.38), channel_id=1, source_target_pairs={{0,16},{16,0},{1,17},{17,1},{2,18},{18,2},{3,19},{19,3},{4,20},{20... | collective-permute-start | bytes 1228808 | tf_op jit(solution)/shard_map/ppermute | solution.py:27
  17.0 12.8 %collective-permute-start.4 = (bf16[160,1280]{1,0:T(8,128)(2,1)}, bf16[160,1280]{1,0:T(8,128)(2,1)S(1)}, u32[]{:S(2)}, u32[]{:S(2)}) collective-permute-start(bf16[160,1280]{1,0:T(8,128)(2,1)} %bitcast.39), channel_id=1, source_target_pairs={{0,8},{4,12},{8,0},{12,4},{1,9},{5,13},{9,1},{13,5},{2,10},{6,14},... | collective-permute-start | bytes 1228808 | tf_op jit(solution)/shard_map/ppermute | solution.py:19
  29.8 10.6 %copy-start.11 = (bf16[160,1280]{1,0:T(8,128)(2,1)}, bf16[160,1280]{1,0:T(8,128)(2,1)S(1)}, u32[]{:S(2)}) copy-start(bf16[160,1280]{1,0:T(8,128)(2,1)S(1)} %collective-permute-done.3.refs_1_) | copy-start | bytes 1228804
  29.8 10.6 %copy-start.16 = (bf16[160,1280]{1,0:T(8,128)(2,1)}, bf16[160,1280]{1,0:T(8,128)(2,1)S(1)}, u32[]{:S(2)}) copy-start(bf16[160,1280]{1,0:T(8,128)(2,1)S(1)} %collective-permute-done.4.refs_2_) | copy-start | bytes 1228804
  29.9 17.2 %collective-permute-start.7 = (bf16[2,160,1280]{2,1,0:T(8,128)(2,1)S(1)}, bf16[2,160,1280]{2,1,0:T(8,128)(2,1)S(1)}, u32[]{:S(2)}, u32[]{:S(2)}) collective-permute-start(bf16[2,160,1280]{2,1,0:T(8,128)(2,1)S(1)} %pad_maximum_fusion.1), channel_id=1, source_target_pairs={{0,4},{4,8},{8,12},{12,0},{1,5},{5,9},{9,13},{13,1},{2,6},{6,10},{... | collective-permute-start | bytes 2457608 | tf_op jit(solution)/shard_map/ppermute | solution.py:19
  31.1 16.0 %collective-permute-start.6 = (bf16[2,160,1280]{2,1,0:T(8,128)(2,1)S(1)}, bf16[2,160,1280]{2,1,0:T(8,128)(2,1)}, u32[]{:S(2)}, u32[]{:S(2)}) collective-permute-start(bf16[2,160,1280]{2,1,0:T(8,128)(2,1)S(1)} %pad_maximum_fusion.1), channel_id=1, source_target_pairs={{0,12},{4,0},{8,4},{12,8},{1,13},{5,1},{9,5},{13,9},{2,14},{6,2},{... | collective-permute-start | bytes 2457608 | tf_op jit(solution)/shard_map/ppermute | solution.py:19
  32.6 7.8 %collective-permute-start.5 = (bf16[160,1280]{1,0:T(8,128)(2,1)S(1)}, bf16[160,1280]{1,0:T(8,128)(2,1)S(1)}, u32[]{:S(2)}, u32[]{:S(2)}) collective-permute-start(bf16[160,1280]{1,0:T(8,128)(2,1)S(1)} %collective-permute-done.4.refs_2_), channel_id=1, source_target_pairs={{0,16},{16,0},{1,17},{17,1},{2,18},{18,2},{3,19},{19,3},{4,20},{20... | collective-permute-start | bytes 1228808 | tf_op jit(solution)/shard_map/ppermute | solution.py:27
  40.4 0.8 copy-start.17
  41.2 14.4 %collective-permute-start.8 = (bf16[3,64,1280]{2,1,0:T(8,128)(2,1)}, bf16[3,64,1280]{2,1,0:T(8,128)(2,1)S(1)}, u32[]{:S(2)}, u32[]{:S(2)}) collective-permute-start(bf16[3,64,1280]{2,1,0:T(8,128)(2,1)} %get-tuple-element.80), channel_id=1, source_target_pairs={{0,32},{32,64},{64,96},{96,0},{1,33},{33,65},{65,97},{97,1},{2,34}... | collective-permute-start | bytes 1474568 | tf_op jit(solution)/shard_map/ppermute | solution.py:23
  41.4 14.2 %collective-permute-start.9 = (bf16[3,64,1280]{2,1,0:T(8,128)(2,1)}, bf16[3,64,1280]{2,1,0:T(8,128)(2,1)S(1)}, u32[]{:S(2)}, u32[]{:S(2)}) collective-permute-start(bf16[3,64,1280]{2,1,0:T(8,128)(2,1)} %get-tuple-element.82), channel_id=1, source_target_pairs={{0,96},{32,0},{64,32},{96,64},{1,97},{33,1},{65,33},{97,65},{2,98}... | collective-permute-start | bytes 1474568 | tf_op jit(solution)/shard_map/ppermute | solution.py:23
  47.1 0.9 copy-start.13
  55.6 10.4 %copy-start.5 = (bf16[3,64,1280]{2,1,0:T(8,128)(2,1)}, bf16[3,64,1280]{2,1,0:T(8,128)(2,1)S(1)}, u32[]{:S(2)}) copy-start(bf16[3,64,1280]{2,1,0:T(8,128)(2,1)S(1)} %collective-permute-done.8.refs_8_) | copy-start | bytes 1474564
  55.6 10.4 %copy-start.6 = (bf16[3,64,1280]{2,1,0:T(8,128)(2,1)}, bf16[3,64,1280]{2,1,0:T(8,128)(2,1)S(1)}, u32[]{:S(2)}) copy-start(bf16[3,64,1280]{2,1,0:T(8,128)(2,1)S(1)} %collective-permute-done.9.refs_10_) | copy-start | bytes 1474564
  55.6 25.9 %copy-start.12 = (bf16[6,64,1280]{2,1,0:T(8,128)(2,1)S(1)}, bf16[6,64,1280]{2,1,0:T(8,128)(2,1)}, u32[]{:S(2)}) copy-start(bf16[6,64,1280]{2,1,0:T(8,128)(2,1)} %get-tuple-element.98) | copy-start | bytes 2949124
  55.6 8.6 %collective-permute-start.10 = (f32[2,192,1280]{2,1,0:T(8,128)}, f32[2,192,1280]{2,1,0:T(8,128)S(1)}, u32[]{:S(2)}, u32[]{:S(2)}) collective-permute-start(f32[2,192,1280]{2,1,0:T(8,128)} %get-tuple-element.85), channel_id=1, source_target_pairs={{0,1},{1,0},{2,3},{3,2},{4,5},{5,4},{6,7},{7,6},{8,9},{9,8},{10,11... | collective-permute-start | bytes 5898248 | tf_op jit(solution)/shard_map/ppermute | solution.py:27
  66.0 44.1 %copy-start.15 = (bf16[3,64,1280]{2,1,0:T(8,128)(2,1)S(1)}, bf16[3,64,1280]{2,1,0:T(8,128)(2,1)}, u32[]{:S(2)}) copy-start(bf16[3,64,1280]{2,1,0:T(8,128)(2,1)} %get-tuple-element.106) | copy-start | bytes 1474564
  66.0 44.1 %copy-start.14 = (bf16[3,64,1280]{2,1,0:T(8,128)(2,1)S(1)}, bf16[3,64,1280]{2,1,0:T(8,128)(2,1)}, u32[]{:S(2)}) copy-start(bf16[3,64,1280]{2,1,0:T(8,128)(2,1)} %get-tuple-element.108) | copy-start | bytes 1474564
  66.0 12.2 %collective-permute-start.12 = (bf16[192,1280]{1,0:T(8,128)(2,1)S(1)}, bf16[192,1280]{1,0:T(8,128)(2,1)S(1)}, u32[]{:S(2)}, u32[]{:S(2)}) collective-permute-start(bf16[192,1280]{1,0:T(8,128)(2,1)S(1)} %get-tuple-element.109), channel_id=1, source_target_pairs={{0,32},{1,96},{2,0},{3,64},{32,33},{33,97},{34,1},{35,65},{64,34},... | collective-permute-start | bytes 1474568 | tf_op jit(solution)/shard_map/ppermute | solution.py:243
  67.1 12.3 %collective-permute-start.11 = (bf16[192,1280]{1,0:T(8,128)(2,1)S(1)}, bf16[192,1280]{1,0:T(8,128)(2,1)S(1)}, u32[]{:S(2)}, u32[]{:S(2)}) collective-permute-start(bf16[192,1280]{1,0:T(8,128)(2,1)S(1)} %get-tuple-element.110), channel_id=1, source_target_pairs={{0,0},{1,64},{2,32},{3,96},{32,1},{33,65},{34,33},{35,97},{64,2},{... | collective-permute-start | bytes 1474568 | tf_op jit(solution)/shard_map/ppermute | solution.py:243
  79.6 44.8 %copy-start = (bf16[192,1280]{1,0:T(8,128)(2,1)}, bf16[192,1280]{1,0:T(8,128)(2,1)S(1)}, u32[]{:S(2)}) copy-start(bf16[192,1280]{1,0:T(8,128)(2,1)S(1)} %add_convert_fusion) | copy-start | bytes 1474564
  79.6 11.5 %collective-permute-start.14 = (bf16[6,32,1280]{2,1,0:T(8,128)(2,1)S(1)}, bf16[6,32,1280]{2,1,0:T(8,128)(2,1)S(1)}, u32[]{:S(2)}, u32[]{:S(2)}) collective-permute-start(bf16[6,32,1280]{2,1,0:T(8,128)(2,1)S(1)} %bitcast.30), channel_id=1, source_target_pairs={{0,8},{4,12},{8,0},{12,4},{1,9},{5,13},{9,1},{13,5},{2,10},{6,14},... | collective-permute-start | bytes 1474568 | tf_op jit(solution)/shard_map/ppermute | solution.py:19
  80.2 17.8 %collective-permute-start.13 = (bf16[6,32,1280]{2,1,0:T(8,128)(2,1)S(1)}, bf16[6,32,1280]{2,1,0:T(8,128)(2,1)S(1)}, u32[]{:S(2)}, u32[]{:S(2)}) collective-permute-start(bf16[6,32,1280]{2,1,0:T(8,128)(2,1)S(1)} %bitcast.31), channel_id=1, source_target_pairs={{0,16},{16,0},{1,17},{17,1},{2,18},{18,2},{3,19},{19,3},{4,20},{20... | collective-permute-start | bytes 1474568 | tf_op jit(solution)/shard_map/ppermute | solution.py:27
  81.5 28.5 %collective-permute-start.18 = (bf16[6,64,1280]{2,1,0:T(8,128)(2,1)S(1)}, bf16[6,64,1280]{2,1,0:T(8,128)(2,1)S(1)}, u32[]{:S(2)}, u32[]{:S(2)}) collective-permute-start(bf16[6,64,1280]{2,1,0:T(8,128)(2,1)S(1)} %copy-done.12), channel_id=1, source_target_pairs={{0,64},{32,96},{64,0},{96,32},{1,65},{33,97},{65,1},{97,33},{2,66}... | collective-permute-start | bytes 2949128 | tf_op jit(solution)/shard_map/ppermute | solution.py:23
  91.1 31.1 %copy-start.7 = (bf16[6,32,1280]{2,1,0:T(8,128)(2,1)}, bf16[6,32,1280]{2,1,0:T(8,128)(2,1)S(1)}, u32[]{:S(2)}) copy-start(bf16[6,32,1280]{2,1,0:T(8,128)(2,1)S(1)} %collective-permute-done.14.refs_2_) | copy-start | bytes 1474564
  97.9 26.5 %copy-start.1 = (bf16[6,32,1280]{2,1,0:T(8,128)(2,1)}, bf16[6,32,1280]{2,1,0:T(8,128)(2,1)S(1)}, u32[]{:S(2)}) copy-start(bf16[6,32,1280]{2,1,0:T(8,128)(2,1)S(1)} %collective-permute-done.13.refs_1_) | copy-start | bytes 1474564
  98.0 24.1 %collective-permute-start.17 = (bf16[2,6,32,1280]{3,2,1,0:T(8,128)(2,1)S(1)}, bf16[2,6,32,1280]{3,2,1,0:T(8,128)(2,1)S(1)}, u32[]{:S(2)}, u32[]{:S(2)}) collective-permute-start(bf16[2,6,32,1280]{3,2,1,0:T(8,128)(2,1)S(1)} %pad_maximum_fusion), channel_id=1, source_target_pairs={{0,4},{4,8},{8,12},{12,0},{1,5},{5,9},{9,13},{13,1},{2,6},{6,10},{... | collective-permute-start | bytes 2949128 | tf_op jit(solution)/shard_map/ppermute | solution.py:19
  98.1 24.0 %collective-permute-start.16 = (bf16[2,6,32,1280]{3,2,1,0:T(8,128)(2,1)S(1)}, bf16[2,6,32,1280]{3,2,1,0:T(8,128)(2,1)S(1)}, u32[]{:S(2)}, u32[]{:S(2)}) collective-permute-start(bf16[2,6,32,1280]{3,2,1,0:T(8,128)(2,1)S(1)} %pad_maximum_fusion), channel_id=1, source_target_pairs={{0,12},{4,0},{8,4},{12,8},{1,13},{5,1},{9,5},{13,9},{2,14},{6,2},{... | collective-permute-start | bytes 2949128 | tf_op jit(solution)/shard_map/ppermute | solution.py:19
  100.8 12.0 %collective-permute-start.15 = (bf16[6,32,1280]{2,1,0:T(8,128)(2,1)S(1)}, bf16[6,32,1280]{2,1,0:T(8,128)(2,1)S(1)}, u32[]{:S(2)}, u32[]{:S(2)}) collective-permute-start(bf16[6,32,1280]{2,1,0:T(8,128)(2,1)S(1)} %collective-permute-done.14.refs_2_), channel_id=1, source_target_pairs={{0,16},{16,0},{1,17},{17,1},{2,18},{18,2},{3,19},{19,3},{4,20},{20... | collective-permute-start | bytes 1474568 | tf_op jit(solution)/shard_map/ppermute | solution.py:27
  110.1 14.4 %copy-start.2 = (bf16[6,64,1280]{2,1,0:T(8,128)(2,1)}, bf16[6,64,1280]{2,1,0:T(8,128)(2,1)S(1)}, u32[]{:S(2)}) copy-start(bf16[6,64,1280]{2,1,0:T(8,128)(2,1)S(1)} %collective-permute-done.18.refs_7_) | copy-start | bytes 2949124
  110.1 13.6 %collective-permute-start.19 = (bf16[3,64,1280]{2,1,0:T(8,128)(2,1)S(1)}, bf16[3,64,1280]{2,1,0:T(8,128)(2,1)S(1)}, u32[]{:S(2)}, u32[]{:S(2)}) collective-permute-start(bf16[3,64,1280]{2,1,0:T(8,128)(2,1)S(1)} %copy-done.15), channel_id=1, source_target_pairs={{0,32},{32,64},{64,96},{96,0},{1,33},{33,65},{65,97},{97,1},{2,34}... | collective-permute-start | bytes 1474568 | tf_op jit(solution)/shard_map/ppermute | solution.py:23
  110.1 14.3 %collective-permute-start.20 = (bf16[3,64,1280]{2,1,0:T(8,128)(2,1)S(1)}, bf16[3,64,1280]{2,1,0:T(8,128)(2,1)}, u32[]{:S(2)}, u32[]{:S(2)}) collective-permute-start(bf16[3,64,1280]{2,1,0:T(8,128)(2,1)S(1)} %copy-done.14), channel_id=1, source_target_pairs={{0,96},{32,0},{64,32},{96,64},{1,97},{33,1},{65,33},{97,65},{2,98}... | collective-permute-start | bytes 1474568 | tf_op jit(solution)/shard_map/ppermute | solution.py:23
  112.7 10.9 %copy-start.8 = (bf16[6,32,1280]{2,1,0:T(8,128)(2,1)}, bf16[6,32,1280]{2,1,0:T(8,128)(2,1)S(1)}, u32[]{:S(2)}) copy-start(bf16[6,32,1280]{2,1,0:T(8,128)(2,1)S(1)} %collective-permute-done.15.refs_3_) | copy-start | bytes 1474564
  122.1 2.3 %copy-start.3 = (bf16[2,6,32,1280]{3,2,1,0:T(8,128)(2,1)}, bf16[2,6,32,1280]{3,2,1,0:T(8,128)(2,1)S(1)}, u32[]{:S(2)}) copy-start(bf16[2,6,32,1280]{3,2,1,0:T(8,128)(2,1)S(1)} %collective-permute-done.17.refs_5_) | copy-start | bytes 2949124
  122.2 2.3 %copy-start.4 = (bf16[2,6,32,1280]{3,2,1,0:T(8,128)(2,1)}, bf16[2,6,32,1280]{3,2,1,0:T(8,128)(2,1)S(1)}, u32[]{:S(2)}) copy-start(bf16[2,6,32,1280]{3,2,1,0:T(8,128)(2,1)S(1)} %collective-permute-done.16.refs_4_) | copy-start | bytes 2949124
  123.6 0.8 copy-start.9
Sparse Core Ops, SparseCore 0:
  9.0 34.3 all-gather.1
